TPU v7x, 32 devices: a whole 2x2x4 slice. The times are simulated.
32 devices in a mesh: shard: 8 (over z, y), rep: 4 (over x, core).
Axes of the slice: x: 2, y: 2, z: 4, core: 2. Of those that a mesh axis runs over, the one named last changes fastest.
Arguments:
- embeddings: bfloat16 [16384, 1024], P('shard'), may hold values from -200 to 200
- labels: int32 [16384], P('shard'), may hold values from 0 to 15, never falling along the last dimension, each value on 1 to 8193 neighbouring positions
Outputs:
- best_similarity: float32 [16384], P('shard')
Inputs may be any that keep to these rules, and one draw needn't show every extreme that they name: labels never fall along the rows; each cluster holds at most 8193 consecutive rows, and one cluster holds exactly that many.
All inputs are finite; a program needn't handle non-finite values.
Results may differ from a plain program's by a relative error of at most 0.00063.
Values may be sent and summed in bfloat16 or wider, within the bound.
No kernel may reach another device: no remote copies, remote signals or barrier semaphores. Data moves between devices by JAX's collectives and lax.ppermute only.
A program may use at most 64 MiB of HBM per device.

v0:
```python
import functools
import math

import jax
import jax.numpy as jnp
from jax import lax
from jax.experimental import pallas as pl
from jax.experimental.pallas import tpu as pltpu
from jax.sharding import PartitionSpec as P

F32 = jnp.float32
BF16 = jnp.bfloat16
TILE = 256
WIDE = 512
INFO = 16
VMEM_LIMIT = 32 * 1024 * 1024
PREPARE_LIMIT = 60 * 1024 * 1024
VMEM = pl.BlockSpec(memory_space=pltpu.VMEM)
SMEM = pl.BlockSpec(memory_space=pltpu.SMEM)


def normalize(values):
    as_float = values.astype(F32)
    inverse = lax.rsqrt(jnp.mean(as_float * as_float, axis=1, keepdims=True) + 1e-06)
    return (as_float * inverse / math.sqrt(values.shape[1])).astype(BF16)


def score(keys, queries):
    return lax.dot_general(keys, queries, (((1,), (1,)), ((), ())), preferred_element_type=F32)


def fold(values):
    rows, cols = values.shape
    return jnp.max(values.reshape(rows // 8, 8, cols), axis=0)


def position():
    rep, odd = lax.axis_index("rep"), lax.axis_index("shard") % 2
    return rep, odd, rep ^ (1 + odd)


def prepare_kernel(emb_ref, labels_ref, mine_out, across_out, raw, sems):
    rep, odd, _ = position()
    quarter = mine_out.shape[0] - INFO
    part = quarter // 2
    copies = []
    for n in range(4):
        piece = rep if n < 2 else rep ^ (2 - odd)
        at = pl.multiple_of(piece * quarter + (n % 2) * part, part)
        copies.append(pltpu.make_async_copy(emb_ref.at[pl.ds(at, part), :], raw.at[n], sems.at[n]))
        copies[-1].start()
    labels = labels_ref[...]
    first, last = jnp.min(labels), jnp.max(labels)
    head = jnp.sum((labels == first).astype(jnp.int32))
    tail = jnp.sum((labels == last).astype(jnp.int32))
    row = lax.broadcasted_iota(jnp.int32, (INFO, mine_out.shape[1]), 0)
    info = jnp.zeros(row.shape, jnp.int32)
    for n, value in enumerate([first, head // 16, head % 16, last, tail // 16, tail % 16]):
        info = jnp.where(row == n, value, info)
    info = info.astype(F32).astype(BF16)
    for n, copy in enumerate(copies):
        copy.wait()
        out = mine_out if n < 2 else across_out
        for m in range(part // 128):
            rows = pl.ds((n % 2) * part + m * 128, 128)
            out[rows, :] = normalize(raw[n, pl.ds(m * 128, 128), :])
    mine_out[pl.ds(quarter, INFO), :] = info
    across_out[pl.ds(quarter, INFO), :] = info


def read_reach(ref, at):
    block = ref[pl.ds(ref.shape[0] - INFO, INFO), pl.ds(0, 128)].astype(F32)
    packed = block[at : at + 1] + 256.0 * (16.0 * block[at + 1 : at + 2] + block[at + 2 : at + 3])
    packed = jnp.max(packed).astype(jnp.int32)
    return packed % 256, packed // 256


def group(keys, queries_ref, query_rows, out_ref, out_at, count):
    step = min(WIDE, query_rows)

    def over_queries(j, _):
        at = pl.multiple_of(j * step, step)
        queries = queries_ref[pl.ds(at, step), :]
        best = None
        for ref, row, rows, first in keys:
            scores = score(ref[pl.ds(row, rows), :], queries)
            index = lax.broadcasted_iota(jnp.int32, scores.shape, 0)
            top = fold(jnp.where(index >= first, scores, -1.0))
            best = top if best is None else jnp.maximum(best, top)
        best = jnp.max(best, axis=0, keepdims=True)
        col = lax.broadcasted_iota(jnp.int32, best.shape, 1) + at
        cols = pl.ds(pl.multiple_of(out_at + at, TILE), step)
        out_ref[:, cols] = jnp.maximum(out_ref[:, cols], jnp.where(col < count, best, -1.0))
        return 0

    lax.fori_loop(0, (count + step - 1) // step, over_queries, 0)


def own_kernel(emb_ref, labels_ref, row_labels_ref, own_out, best_out, reach_out):
    rows = emb_ref.shape[0]
    rep = lax.axis_index("rep")
    labels = labels_ref[...]
    first = jnp.min(labels)
    reach_out[0] = first
    reach_out[1] = jnp.sum((labels == first).astype(jnp.int32))
    for n in range(rows // 128):
        own_out[pl.ds(n * 128, 128), :] = normalize(emb_ref[pl.ds(n * 128, 128), :])
    best_out[...] = jnp.full(best_out.shape, -1.0, F32)
    for n in range(2):
        tile = rep if n == 0 else rows // TILE - 1 - rep
        at = pl.multiple_of(tile * TILE, TILE)
        keys = own_out[pl.ds(at, TILE), :]
        row_labels = row_labels_ref[pl.ds(at, TILE), :]

        def over_queries(j, _):
            cols = pl.ds(pl.multiple_of(j * WIDE, WIDE), WIDE)
            scores = score(keys, own_out[cols, :])
            row = lax.broadcasted_iota(jnp.int32, scores.shape, 0) + at
            col = lax.broadcasted_iota(jnp.int32, scores.shape, 1) + j * WIDE
            keep = (row_labels == labels_ref[:, cols]) & (row < col)
            best = jnp.max(fold(jnp.where(keep, scores, -1.0)), axis=0, keepdims=True)
            best_out[:, cols] = jnp.maximum(best_out[:, cols], best)
            return 0

        lax.fori_loop(at // WIDE, rows // WIDE, over_queries, 0)


def reached(query, key, offset, limit):
    count = jnp.clip(query[1] - offset, 0, limit)
    return jnp.where(query[0] == key[0], count, 0)


def lower_keys(rep, tail, quarter, pieces):
    return [
        (ref, 0, quarter, jnp.clip(4 * quarter - tail - (rep ^ flip) * quarter, 0, quarter))
        for ref, flip in pieces
    ]


def near_kernel(own_reach, own_ref, best_ref, low_0, low_1, across, high,
                best_out, across_out, high_out, reach_out):
    rows = own_ref.shape[0]
    quarter = across.shape[0] - INFO
    rep, odd, part = position()
    mine = (own_reach[0], own_reach[1])
    low, beside_head = read_reach(low_0, 3), read_reach(across, 0)
    beside_tail, up = read_reach(across, 3), read_reach(high, 0)
    for n, value in enumerate(low + beside_head + up):
        reach_out[n] = value
    best_out[...] = best_ref[...]
    across_out[...] = jnp.full(across_out.shape, -1.0, F32)
    high_out[...] = jnp.full(high_out.shape, -1.0, F32)

    lows = lower_keys(rep, low[1], quarter, [(low_0, 0), (low_1, 1)])
    besides = [
        (across, 0, quarter, jnp.clip(rows - beside_tail[1] - part * quarter, 0, quarter))
    ]
    group(lows[:1], own_ref, rows, best_out, 0, reached(mine, low, 0, rows))
    count = jnp.where(odd == 1, reached(mine, beside_tail, 0, rows), 0)
    group(besides, own_ref, rows, best_out, 0, count)
    group(lows, across, quarter, across_out, 0, reached(beside_head, low, part * quarter, quarter))
    group(besides, high, quarter, high_out, 0, reached(up, beside_tail, rep * quarter, quarter))
    group(lows, high, quarter, high_out, 0, reached(up, low, rep * quarter, quarter))


def far_kernel(reach_ref, across_ref, high_ref, low_0, low_1, low_2, across, high, up_a, up_b,
               across_out, high_out, up_out, side_out):
    quarter = across.shape[0] - INFO
    half = quarter // 2
    rep, _, part = position()
    low, beside, up = [(reach_ref[2 * n], reach_ref[2 * n + 1]) for n in range(3)]
    side = read_reach(up_b, 0)
    side_out[0], side_out[1] = side
    across_out[...] = across_ref[...]
    high_out[...] = high_ref[...]
    up_out[...] = jnp.full(up_out.shape, -1.0, F32)
    lows = lower_keys(rep, low[1], quarter, [(low_2, 2), (low_0, 0), (low_1, 1)])
    group(lows[:1], across, quarter, across_out, 0, reached(beside, low, part * quarter, quarter))
    group(lows[:1], high, quarter, high_out, 0, reached(up, low, rep * quarter, quarter))
    group(lows, up_a, half, up_out, 0, reached(side, low, (rep ^ 2) * quarter, half))
    group(lows, up_b, half, up_out, half, reached(side, low, rep * quarter + half, half))


def last_kernel(reach_ref, side_ref, high_ref, up_ref, low_3, high, up_a, up_b, high_out, up_out):
    half = up_a.shape[0]
    quarter = 2 * half
    rep = lax.axis_index("rep")
    low, up = (reach_ref[0], reach_ref[1]), (reach_ref[4], reach_ref[5])
    side = (side_ref[0], side_ref[1])
    high_out[...], up_out[...] = high_ref[...], up_ref[...]
    lows = lower_keys(rep, low[1], quarter, [(low_3, 3)])
    group(lows, high, quarter, high_out, 0, reached(up, low, rep * quarter, quarter))
    group(lows, up_a, half, up_out, 0, reached(side, low, (rep ^ 2) * quarter, half))
    group(lows, up_b, half, up_out, half, reached(side, low, rep * quarter + half, half))


def merge_kernel(best_ref, partner_ref, above_ref, beside_ref, out_ref):
    quarter = above_ref.shape[1]
    half = quarter // 2
    rep, odd, _ = position()
    inside = lax.axis_index("shard") >= 2
    out_ref[...] = best_ref[...]

    def raised(at, values):
        cols = pl.ds(pl.multiple_of(at, half), values.shape[1])
        out_ref[:, cols] = jnp.maximum(out_ref[:, cols], values)

    raised((rep ^ (2 - odd)) * quarter, partner_ref[...])
    raised(rep * quarter, jnp.where(inside, above_ref[...], -1.0))
    beside = jnp.where(inside & (odd == 0), beside_ref[...], -1.0)
    raised((rep ^ 2) * quarter, beside[:, :half])
    raised(rep * quarter + half, beside[:, half:])


def local(embeddings, labels):
    rows, width = embeddings.shape
    shards, reps = lax.axis_size("shard"), lax.axis_size("rep")
    quarter = rows // reps
    half = quarter // 2

    def along_shard(block, distance, keep=lambda i: True):
        route = [
            (i, i + distance) for i in range(shards) if i + distance in range(shards) and keep(i)
        ]
        return lax.ppermute(block, "shard", route)

    def partner(block):
        return lax.ppermute(block, "shard", [(i, i ^ 1) for i in range(shards)])

    def other_rep(block, flip):
        return lax.ppermute(block, "rep", [(i, i ^ flip) for i in range(reps)])

    def call(kernel, name, shapes, specs, *arrays):
        return pl.pallas_call(
            kernel,
            out_shape=[jax.ShapeDtypeStruct(shape, dtype) for shape, dtype in shapes],
            in_specs=specs[: len(arrays)],
            out_specs=specs[len(arrays) :],
            compiler_params=pltpu.CompilerParams(vmem_limit_bytes=VMEM_LIMIT),
            cost_estimate=pl.CostEstimate(flops=1024, bytes_accessed=1024, transcendentals=0),
            name=name,
        )(*arrays)

    mine, across = pl.pallas_call(
        prepare_kernel,
        out_shape=[jax.ShapeDtypeStruct((quarter + INFO, width), BF16)] * 2,
        in_specs=[pl.BlockSpec(memory_space=pl.ANY), VMEM],
        out_specs=[VMEM] * 2,
        scratch_shapes=[pltpu.VMEM((4, half, width), BF16), pltpu.SemaphoreType.DMA((4,))],
        compiler_params=pltpu.CompilerParams(vmem_limit_bytes=PREPARE_LIMIT),
        name="prepare",
    )(embeddings, labels.reshape(rows // 128, 128))

    odd_only, even_only = (lambda i: i % 2 == 1), (lambda i: i % 2 == 0)
    fence = lax.optimization_barrier

    low_0 = along_shard(mine, 2)
    high = along_shard(mine, -2)
    across = partner(across)

    own, best, own_reach = call(
        own_kernel, "own", [((rows, width), BF16), ((1, rows), F32), ((2,), jnp.int32)],
        [VMEM] * 5 + [SMEM], embeddings, labels[None, :], labels[:, None],
    )

    low_0, own, best = fence((low_0, own, best))
    low_2 = other_rep(low_0, 2)
    low_1 = other_rep(low_0, 1)
    across, high, low_1 = fence((across, high, low_1))
    up_b = along_shard(high[half:], 1, even_only)
    up_a = along_shard(across[:half], -2, odd_only)
    results = [((1, quarter), F32)] * 2
    best, of_across, of_high, reach = call(
        near_kernel, "near", [((1, rows), F32)] + results + [((6,), jnp.int32)],
        [SMEM] + [VMEM] * 9 + [SMEM], own_reach, own, best, low_0, low_1, across, high,
    )
    low_2, up_a, up_b, of_across = fence((low_2, up_a, up_b, of_across))
    low_3 = other_rep(low_2, 1)
    of_across, of_high, of_up, side = call(
        far_kernel, "far", results + [((1, quarter), F32), ((2,), jnp.int32)],
        [SMEM] + [VMEM] * 12 + [SMEM],
        reach, of_across, of_high, low_0, low_1, low_2, across, high, up_a, up_b,
    )
    of_high, of_up = call(
        last_kernel, "last", results, [SMEM] * 2 + [VMEM] * 8,
        reach, side, of_high, of_up, low_3, high, up_a, up_b,
    )

    above = along_shard(of_high, 2)
    beside = along_shard(of_up, 1, odd_only)
    from_partner = partner(of_across)
    (best,) = call(
        merge_kernel, "merge", [((1, rows), F32)], [VMEM] * 5, best, from_partner, above, beside
    )
    return lax.pmax(best[0], "rep")


def solution(mesh):
    placed = (P("shard", None), P("shard"))
    return jax.shard_map(local, mesh=mesh, in_specs=placed, out_specs=P("shard"), check_vma=False)
```

profile of v0, /device:TPU:8, one launch (start us, length us, event | category | flops | bytes accessed | tf_op | source)
XLA Modules:
  0.0 80.0 jit_solution(9571408011682981167)
XLA Ops:
  0.0 4.2 %prepare.1 = (bf16[528,1024]{1,0:T(8,128)(2,1)}, bf16[528,1024]{1,0:T(8,128)(2,1)}) custom-call(bf16[2048,1024]{1,0:T(8,128)(2,1)} %emb_ref.3, s32[16,128]{1,0:T(8,128)} %bitcast.4), custom_call_target="tpu_custom_call" | custom-call | tf_op jit(solution)/shard_map/prepare/pallas_call | solution.py:244
  4.2 3.5 %collective-permute-start = (bf16[528,1024]{1,0:T(8,128)(2,1)}, bf16[528,1024]{1,0:T(8,128)(2,1)S(1)}, u32[]{:S(2)}, u32[]{:S(2)}) collective-permute-start(bf16[528,1024]{1,0:T(8,128)(2,1)} %get-tuple-element.31), channel_id=1, source_target_pairs={{0,8},{4,12},{8,16},{12,20},{16,24},{20,28},{1,9},{5,13},{9,17},{1... | collective-permute-start | bytes 3244040 | tf_op jit(solution)/shard_map/ppermute | solution.py:225
  7.7 2.4 %collective-permute-start.2 = (bf16[528,1024]{1,0:T(8,128)(2,1)}, bf16[528,1024]{1,0:T(8,128)(2,1)S(1)}, u32[]{:S(2)}, u32[]{:S(2)}) collective-permute-start(bf16[528,1024]{1,0:T(8,128)(2,1)} %get-tuple-element.31), channel_id=1, source_target_pairs={{8,0},{12,4},{16,8},{20,12},{24,16},{28,20},{9,1},{13,5},{17,9},{2... | collective-permute-start | bytes 3244040 | tf_op jit(solution)/shard_map/ppermute | solution.py:225
  10.1 1.6 %collective-permute-start.1 = (bf16[528,1024]{1,0:T(8,128)(2,1)}, bf16[528,1024]{1,0:T(8,128)(2,1)S(1)}, u32[]{:S(2)}, u32[]{:S(2)}) collective-permute-start(bf16[528,1024]{1,0:T(8,128)(2,1)} %get-tuple-element.37), channel_id=1, source_target_pairs={{0,4},{4,0},{8,12},{12,8},{16,20},{20,16},{24,28},{28,24},{1,5},{5... | collective-permute-start | bytes 3244040 | tf_op jit(solution)/shard_map/ppermute | solution.py:228
  11.7 1.4 %copy.3.row_labels_ref = s32[2048,1]{1,0:T(8,128)} copy(s32[2048,1]{0,1:T(1,128)S(1)} %bitcast.5) | data formatting | bytes 16384 | tf_op jit(solution)/shard_map/broadcast_in_dim | solution.py:263
  13.1 2.2 %copy-done = bf16[2048,1024]{1,0:T(8,128)(2,1)S(1)} copy-done((bf16[2048,1024]{1,0:T(8,128)(2,1)S(1)}, bf16[2048,1024]{1,0:T(8,128)(2,1)}, u32[]{:S(2)}) %copy-start) | copy-done | bytes 4194328
  15.3 1.2 %copy-done.1 = s32[2048,1]{1,0:T(8,128)S(1)} copy-done((s32[2048,1]{1,0:T(8,128)S(1)}, s32[2048,1]{1,0:T(8,128)}, u32[]{:S(2)}) %copy-start.1) | copy-done | bytes 8216
  16.5 4.8 %own.1 = (bf16[2048,1024]{1,0:T(8,128)(2,1)S(1)}, f32[1,2048]{1,0:T(1,128)S(1)}, s32[2]{0:T(128)S(1)}) custom-call(bf16[2048,1024]{1,0:T(8,128)(2,1)S(1)} %copy-done, s32[1,2048]{1,0:T(1,128)S(1)} %bitcast.6, s32[2048,1]{1,0:T(8,128)S(1)} %copy-done.1), custom_call_target="tpu_custom_call" | custom-call | flops 1024 | bytes 1024 | tf_op jit(solution)/shard_map/own/pallas_call | solution.py:234
  21.4 10.6 %collective-permute-done.low_0 = bf16[528,1024]{1,0:T(8,128)(2,1)S(1)} collective-permute-done((bf16[528,1024]{1,0:T(8,128)(2,1)}, bf16[528,1024]{1,0:T(8,128)(2,1)S(1)}, u32[]{:S(2)}, u32[]{:S(2)}) %collective-permute-start) | collective-permute-done | bytes 1081376 | tf_op jit(solution)/shard_map/ppermute | solution.py:225
  31.9 1.5 %collective-permute-start.4 = (bf16[528,1024]{1,0:T(8,128)(2,1)S(1)}, bf16[528,1024]{1,0:T(8,128)(2,1)S(1)}, u32[]{:S(2)}, u32[]{:S(2)}) collective-permute-start(bf16[528,1024]{1,0:T(8,128)(2,1)S(1)} %collective-permute-done.low_0), channel_id=1, source_target_pairs={{0,2},{1,3},{2,0},{3,1},{4,6},{5,7},{6,4},{7,5},{8,10},{9,11},{10,... | collective-permute-start | bytes 3244040 | tf_op jit(solution)/shard_map/ppermute | solution.py:231
  33.4 2.0 %collective-permute-done.1.across = bf16[528,1024]{1,0:T(8,128)(2,1)S(1)} collective-permute-done((bf16[528,1024]{1,0:T(8,128)(2,1)}, bf16[528,1024]{1,0:T(8,128)(2,1)S(1)}, u32[]{:S(2)}, u32[]{:S(2)}) %collective-permute-start.1) | collective-permute-done | bytes 1081376 | tf_op jit(solution)/shard_map/ppermute | solution.py:228
  35.5 0.0 collective-permute-done.2.high
  35.5 3.5 %collective-permute-start.6 = (bf16[272,1024]{1,0:T(8,128)(2,1)S(1)}, bf16[272,1024]{1,0:T(8,128)(2,1)S(1)}, u32[]{:S(2)}, u32[]{:S(2)}) collective-permute-start(bf16[272,1024]{1,0:T(8,128)(2,1)S(1)} %slice.7), channel_id=1, source_target_pairs={{0,4},{8,12},{16,20},{24,28},{1,5},{9,13},{17,21},{25,29},{2,6},{1... | collective-permute-start | bytes 1671176 | tf_op jit(solution)/shard_map/ppermute | solution.py:225
  39.0 0.7 collective-permute-start.5
  39.7 2.1 %near.1 = (f32[1,2048]{1,0:T(1,128)S(1)}, f32[1,512]{1,0:T(1,128)S(1)}, f32[1,512]{1,0:T(1,128)S(1)}, s32[6]{0:T(128)S(1)}) custom-call(s32[2]{0:T(128)S(1)} %get-tuple-element.30.own_reach, bf16[2048,1024]{1,0:T(8,128)(2,1)S(1)} %get-tuple-element.34.own_ref, f32[1,2048]{1,0:T(1,128)S(1)} %get-tuple-element.35.best_ref, ...), custom_call_target="tpu_custom_call" | custom-call | flops 1024 | bytes 1024 | tf_op jit(solution)/shard_map/near/pallas_call | solution.py:234
  41.8 16.4 %collective-permute-done.4.low_2 = bf16[528,1024]{1,0:T(8,128)(2,1)S(1)} collective-permute-done((bf16[528,1024]{1,0:T(8,128)(2,1)S(1)}, bf16[528,1024]{1,0:T(8,128)(2,1)S(1)}, u32[]{:S(2)}, u32[]{:S(2)}) %collective-permute-start.4) | collective-permute-done | bytes 1081376 | tf_op jit(solution)/shard_map/ppermute | solution.py:231
  58.2 1.3 %far.1 = (f32[1,512]{1,0:T(1,128)S(1)}, f32[1,512]{1,0:T(1,128)S(1)}, f32[1,512]{1,0:T(1,128)S(1)}, s32[2]{0:T(128)S(1)}) custom-call(s32[6]{0:T(128)S(1)} %get-tuple-element.42.reach_ref, f32[1,512]{1,0:T(1,128)S(1)} %get-tuple-element.44.across_ref, f32[1,512]{1,0:T(1,128)S(1)} %get-tuple-element.45.high_ref, ...), custom_call_target="tpu_custom_call" | custom-call | flops 1024 | bytes 1024 | tf_op jit(solution)/shard_map/far/pallas_call | solution.py:234
  59.5 5.1 %collective-permute-start.7 = (f32[1,512]{1,0:T(1,128)S(1)}, f32[1,512]{1,0:T(1,128)S(1)}, u32[]{:S(2)}, u32[]{:S(2)}) collective-permute-start(f32[1,512]{1,0:T(1,128)S(1)} %get-tuple-element.49), channel_id=1, source_target_pairs={{0,4},{4,0},{8,12},{12,8},{16,20},{20,16},{24,28},{28,24},{1,5},{5... | collective-permute-start | bytes 6152 | tf_op jit(solution)/shard_map/ppermute | solution.py:228
  64.7 0.6 last.1
  65.3 1.9 %collective-permute-start.9 = (f32[1,512]{1,0:T(1,128)S(1)}, f32[1,512]{1,0:T(1,128)S(1)}, u32[]{:S(2)}, u32[]{:S(2)}) collective-permute-start(f32[1,512]{1,0:T(1,128)S(1)} %get-tuple-element.53), channel_id=1, source_target_pairs={{0,8},{4,12},{8,16},{12,20},{16,24},{20,28},{1,9},{5,13},{9,17},{1... | collective-permute-start | bytes 6152 | tf_op jit(solution)/shard_map/ppermute | solution.py:225
  67.2 1.3 %collective-permute-start.10 = (f32[1,512]{1,0:T(1,128)S(1)}, f32[1,512]{1,0:T(1,128)S(1)}, u32[]{:S(2)}, u32[]{:S(2)}) collective-permute-start(f32[1,512]{1,0:T(1,128)S(1)} %get-tuple-element.54), channel_id=1, source_target_pairs={{4,8},{12,16},{20,24},{5,9},{13,17},{21,25},{6,10},{14,18},{22,26}... | collective-permute-start | bytes 6152 | tf_op jit(solution)/shard_map/ppermute | solution.py:225
  68.5 2.2 %collective-permute-done.9.above_ref = f32[1,512]{1,0:T(1,128)S(1)} collective-permute-done((f32[1,512]{1,0:T(1,128)S(1)}, f32[1,512]{1,0:T(1,128)S(1)}, u32[]{:S(2)}, u32[]{:S(2)}) %collective-permute-start.9) | collective-permute-done | bytes 2080 | tf_op jit(solution)/shard_map/ppermute | solution.py:225
  70.8 2.8 %collective-permute-done.10.beside_ref = f32[1,512]{1,0:T(1,128)S(1)} collective-permute-done((f32[1,512]{1,0:T(1,128)S(1)}, f32[1,512]{1,0:T(1,128)S(1)}, u32[]{:S(2)}, u32[]{:S(2)}) %collective-permute-start.10) | collective-permute-done | bytes 2080 | tf_op jit(solution)/shard_map/ppermute | solution.py:225
  73.6 6.3 %pmax.7 = f32[2048]{0:T(1024)} all-reduce(f32[2048]{0:T(1024)S(1)} %bitcast.7), channel_id=1, replica_groups=mesh['shard'=8,'rep'=4] {'rep'}, use_global_device_ids=true, to_apply=%region_0.0 | all-reduce | flops 2048 | bytes 16384 | tf_op jit(solution)/shard_map/pmax | solution.py:295
  (14 shorter events, 0.1 us)
Async XLA Ops:
  0.0 11.7 %copy-start.2 = (s32[2048]{0:T(1024)S(1)}, s32[2048]{0:T(1024)}, u32[]{:S(2)}) copy-start(s32[2048]{0:T(1024)} %param.3) | copy-start | bytes 24580
  4.2 27.7 %collective-permute-start = (bf16[528,1024]{1,0:T(8,128)(2,1)}, bf16[528,1024]{1,0:T(8,128)(2,1)S(1)}, u32[]{:S(2)}, u32[]{:S(2)}) collective-permute-start(bf16[528,1024]{1,0:T(8,128)(2,1)} %get-tuple-element.31), channel_id=1, source_target_pairs={{0,8},{4,12},{8,16},{12,20},{16,24},{20,28},{1,9},{5,13},{9,17},{1... | collective-permute-start | bytes 3244040 | tf_op jit(solution)/shard_map/ppermute | solution.py:225
  7.7 27.7 %collective-permute-start.2 = (bf16[528,1024]{1,0:T(8,128)(2,1)}, bf16[528,1024]{1,0:T(8,128)(2,1)S(1)}, u32[]{:S(2)}, u32[]{:S(2)}) collective-permute-start(bf16[528,1024]{1,0:T(8,128)(2,1)} %get-tuple-element.31), channel_id=1, source_target_pairs={{8,0},{12,4},{16,8},{20,12},{24,16},{28,20},{9,1},{13,5},{17,9},{2... | collective-permute-start | bytes 3244040 | tf_op jit(solution)/shard_map/ppermute | solution.py:225
  10.1 25.3 %collective-permute-start.1 = (bf16[528,1024]{1,0:T(8,128)(2,1)}, bf16[528,1024]{1,0:T(8,128)(2,1)S(1)}, u32[]{:S(2)}, u32[]{:S(2)}) collective-permute-start(bf16[528,1024]{1,0:T(8,128)(2,1)} %get-tuple-element.37), channel_id=1, source_target_pairs={{0,4},{4,0},{8,12},{12,8},{16,20},{20,16},{24,28},{28,24},{1,5},{5... | collective-permute-start | bytes 3244040 | tf_op jit(solution)/shard_map/ppermute | solution.py:228
  13.1 2.2 %copy-start = (bf16[2048,1024]{1,0:T(8,128)(2,1)S(1)}, bf16[2048,1024]{1,0:T(8,128)(2,1)}, u32[]{:S(2)}) copy-start(bf16[2048,1024]{1,0:T(8,128)(2,1)} %emb_ref.3) | copy-start | bytes 12582916
  15.3 1.2 %copy-start.1 = (s32[2048,1]{1,0:T(8,128)S(1)}, s32[2048,1]{1,0:T(8,128)}, u32[]{:S(2)}) copy-start(s32[2048,1]{1,0:T(8,128)} %copy.3.row_labels_ref) | copy-start | bytes 24580
  31.9 3.5 %collective-permute-start.3 = (bf16[528,1024]{1,0:T(8,128)(2,1)S(1)}, bf16[528,1024]{1,0:T(8,128)(2,1)S(1)}, u32[]{:S(2)}, u32[]{:S(2)}) collective-permute-start(bf16[528,1024]{1,0:T(8,128)(2,1)S(1)} %collective-permute-done.low_0), channel_id=1, source_target_pairs={{0,1},{1,0},{2,3},{3,2},{4,5},{5,4},{6,7},{7,6},{8,9},{9,8},{10,11... | collective-permute-start | bytes 3244040 | tf_op jit(solution)/shard_map/ppermute | solution.py:231
  31.9 26.3 %collective-permute-start.4 = (bf16[528,1024]{1,0:T(8,128)(2,1)S(1)}, bf16[528,1024]{1,0:T(8,128)(2,1)S(1)}, u32[]{:S(2)}, u32[]{:S(2)}) collective-permute-start(bf16[528,1024]{1,0:T(8,128)(2,1)S(1)} %collective-permute-done.low_0), channel_id=1, source_target_pairs={{0,2},{1,3},{2,0},{3,1},{4,6},{5,7},{6,4},{7,5},{8,10},{9,11},{10,... | collective-permute-start | bytes 3244040 | tf_op jit(solution)/shard_map/ppermute | solution.py:231
  35.5 22.7 %collective-permute-start.6 = (bf16[272,1024]{1,0:T(8,128)(2,1)S(1)}, bf16[272,1024]{1,0:T(8,128)(2,1)S(1)}, u32[]{:S(2)}, u32[]{:S(2)}) collective-permute-start(bf16[272,1024]{1,0:T(8,128)(2,1)S(1)} %slice.7), channel_id=1, source_target_pairs={{0,4},{8,12},{16,20},{24,28},{1,5},{9,13},{17,21},{25,29},{2,6},{1... | collective-permute-start | bytes 1671176 | tf_op jit(solution)/shard_map/ppermute | solution.py:225
  39.0 19.2 %collective-permute-start.5 = (bf16[256,1024]{1,0:T(8,128)(2,1)S(1)}, bf16[256,1024]{1,0:T(8,128)(2,1)S(1)}, u32[]{:S(2)}, u32[]{:S(2)}) collective-permute-start(bf16[256,1024]{1,0:T(8,128)(2,1)S(1)} %slice.6), channel_id=1, source_target_pairs={{12,4},{20,12},{28,20},{13,5},{21,13},{29,21},{14,6},{22,14},{30,2... | collective-permute-start | bytes 1572872 | tf_op jit(solution)/shard_map/ppermute | solution.py:225
  58.2 6.5 %collective-permute-start.8 = (bf16[528,1024]{1,0:T(8,128)(2,1)S(1)}, bf16[528,1024]{1,0:T(8,128)(2,1)S(1)}, u32[]{:S(2)}, u32[]{:S(2)}) collective-permute-start(bf16[528,1024]{1,0:T(8,128)(2,1)S(1)} %collective-permute-done.4.low_2), channel_id=1, source_target_pairs={{0,1},{1,0},{2,3},{3,2},{4,5},{5,4},{6,7},{7,6},{8,9},{9,8},{10,11... | collective-permute-start | bytes 3244040 | tf_op jit(solution)/shard_map/ppermute | solution.py:231
  59.5 9.0 %collective-permute-start.7 = (f32[1,512]{1,0:T(1,128)S(1)}, f32[1,512]{1,0:T(1,128)S(1)}, u32[]{:S(2)}, u32[]{:S(2)}) collective-permute-start(f32[1,512]{1,0:T(1,128)S(1)} %get-tuple-element.49), channel_id=1, source_target_pairs={{0,4},{4,0},{8,12},{12,8},{16,20},{20,16},{24,28},{28,24},{1,5},{5... | collective-permute-start | bytes 6152 | tf_op jit(solution)/shard_map/ppermute | solution.py:228
  65.3 5.5 %collective-permute-start.9 = (f32[1,512]{1,0:T(1,128)S(1)}, f32[1,512]{1,0:T(1,128)S(1)}, u32[]{:S(2)}, u32[]{:S(2)}) collective-permute-start(f32[1,512]{1,0:T(1,128)S(1)} %get-tuple-element.53), channel_id=1, source_target_pairs={{0,8},{4,12},{8,16},{12,20},{16,24},{20,28},{1,9},{5,13},{9,17},{1... | collective-permute-start | bytes 6152 | tf_op jit(solution)/shard_map/ppermute | solution.py:225
  67.2 6.4 %collective-permute-start.10 = (f32[1,512]{1,0:T(1,128)S(1)}, f32[1,512]{1,0:T(1,128)S(1)}, u32[]{:S(2)}, u32[]{:S(2)}) collective-permute-start(f32[1,512]{1,0:T(1,128)S(1)} %get-tuple-element.54), channel_id=1, source_target_pairs={{4,8},{12,16},{20,24},{5,9},{13,17},{21,25},{6,10},{14,18},{22,26}... | collective-permute-start | bytes 6152 | tf_op jit(solution)/shard_map/ppermute | solution.py:225
where the time goes:
time: 79.9 us; the launch traced here: 80 us
  waiting for transfers between devices  34 us (43%)
  starting transfers between devices  21.5 us (27%)
  Pallas kernels  13.1 us (16%)
  blocking collectives  6.34 us (8%)
  local copies, waits for them, and re-layouts  4.84 us (6%)
    ppermute x3, waiting for transfers between devices, other_rep(): return lax.ppermute(block, 'rep', [(i, i ^ flip) for i in range(reps)])  16.4 us
    ppermute x6, waiting for transfers between devices, along_shard(): return lax.ppermute(block, 'shard', route)  15.6 us
    ppermute x6, starting transfers between devices, along_shard(): return lax.ppermute(block, 'shard', route)  13.3 us
    pallas_call x5, Pallas kernels, call(): pl.pallas_call(kernel, out_shape=[jax.ShapeDtypeStruct(shape, dtype) for...  8.89 us
    ppermute x2, starting transfers between devices, partner(): return lax.ppermute(block, 'shard', [(i, i ^ 1) for i in range(shards)])  6.73 us
    pmax x1, blocking collectives, local(): return lax.pmax(best[0], 'rep')  6.34 us
    pallas_call x1, Pallas kernels, local(): pl.pallas_call(prepare_kernel, out_shape=[jax.ShapeDtypeStruct((quarter +...  4.21 us
    unnamed x6, local copies, waits for them, and re-layouts  3.42 us
  transfers between devices with their start and end apart: 11, of which 5 were waited for; matrix products, arithmetic and copies ran while one was open for 2% of the time, Pallas kernels for 11%

commit v1 on v0

--- a/solution.py
+++ b/solution.py
@@ -14,6 +14,7 @@
 WIDE = 512
 INFO = 16
 VMEM_LIMIT = 32 * 1024 * 1024
+OWN_LIMIT = 46 * 1024 * 1024
 PREPARE_LIMIT = 60 * 1024 * 1024
 VMEM = pl.BlockSpec(memory_space=pltpu.VMEM)
 SMEM = pl.BlockSpec(memory_space=pltpu.SMEM)
@@ -21,8 +22,9 @@
 
 def normalize(values):
     as_float = values.astype(F32)
-    inverse = lax.rsqrt(jnp.mean(as_float * as_float, axis=1, keepdims=True) + 1e-06)
-    return (as_float * inverse / math.sqrt(values.shape[1])).astype(BF16)
+    width = values.shape[1]
+    inverse = lax.rsqrt(jnp.sum(as_float * as_float, axis=1, keepdims=True) * (1 / width) + 1e-06)
+    return (as_float * (inverse * (1 / math.sqrt(width)))).astype(BF16)
 
 
 def score(keys, queries):
@@ -39,7 +41,7 @@
     return rep, odd, rep ^ (1 + odd)
 
 
-def prepare_kernel(emb_ref, labels_ref, mine_out, across_out, raw, sems):
+def prepare_kernel(emb_ref, labels_ref, lo_out, hi_out, mine_out, across_out, raw, sems):
     rep, odd, _ = position()
     quarter = mine_out.shape[0] - INFO
     part = quarter // 2
@@ -62,8 +64,12 @@
         copy.wait()
         out = mine_out if n < 2 else across_out
         for m in range(part // 128):
-            rows = pl.ds((n % 2) * part + m * 128, 128)
-            out[rows, :] = normalize(raw[n, pl.ds(m * 128, 128), :])
+            rows = pl.ds(m * 128, 128)
+            values = normalize(raw[n, rows, :])
+            out[pl.ds((n % 2) * part + m * 128, 128), :] = values
+            if n < 2:
+                (lo_out, hi_out)[n][rows, :] = values
+    hi_out[pl.ds(part, INFO), :] = info
     mine_out[pl.ds(quarter, INFO), :] = info
     across_out[pl.ds(quarter, INFO), :] = info
 
@@ -96,28 +102,45 @@
     lax.fori_loop(0, (count + step - 1) // step, over_queries, 0)
 
 
-def own_kernel(emb_ref, labels_ref, row_labels_ref, own_out, best_out, reach_out):
+def own_kernel(emb_ref, labels_ref, own_out, best_out, reach_out, start, raw, sems):
     rows = emb_ref.shape[0]
     rep = lax.axis_index("rep")
-    labels = labels_ref[...]
+    parts = raw.shape[0]
+    size = rows // parts
+    copies = [
+        pltpu.make_async_copy(emb_ref.at[pl.ds(n * size, size), :], raw.at[n], sems.at[n])
+        for n in range(parts)
+    ]
+    for copy in copies:
+        copy.start()
+    labels = jnp.broadcast_to(labels_ref[...], start.shape)
     first = jnp.min(labels)
     reach_out[0] = first
-    reach_out[1] = jnp.sum((labels == first).astype(jnp.int32))
-    for n in range(rows // 128):
-        own_out[pl.ds(n * 128, 128), :] = normalize(emb_ref[pl.ds(n * 128, 128), :])
+    reach_out[1] = jnp.sum((labels == first).astype(jnp.int32)) // start.shape[0]
+    lane = lax.broadcasted_iota(jnp.int32, labels.shape, 1)
+    begin = jnp.where((lane == 0) | (labels != pltpu.roll(labels, 1, 1)), lane, 0)
+    shift = 1
+    while shift < rows:
+        begin = jnp.maximum(begin, jnp.where(lane >= shift, pltpu.roll(begin, shift, 1), 0))
+        shift *= 2
+    start[...] = begin
     best_out[...] = jnp.full(best_out.shape, -1.0, F32)
+    for n, copy in enumerate(copies):
+        copy.wait()
+        for m in range(size // 128):
+            values = normalize(raw[n, pl.ds(m * 128, 128), :])
+            own_out[pl.ds(n * size + m * 128, 128), :] = values
     for n in range(2):
         tile = rep if n == 0 else rows // TILE - 1 - rep
         at = pl.multiple_of(tile * TILE, TILE)
         keys = own_out[pl.ds(at, TILE), :]
-        row_labels = row_labels_ref[pl.ds(at, TILE), :]
 
         def over_queries(j, _):
             cols = pl.ds(pl.multiple_of(j * WIDE, WIDE), WIDE)
             scores = score(keys, own_out[cols, :])
             row = lax.broadcasted_iota(jnp.int32, scores.shape, 0) + at
             col = lax.broadcasted_iota(jnp.int32, scores.shape, 1) + j * WIDE
-            keep = (row_labels == labels_ref[:, cols]) & (row < col)
+            keep = (row >= start[0:1, cols]) & (row < col)
             best = jnp.max(fold(jnp.where(keep, scores, -1.0)), axis=0, keepdims=True)
             best_out[:, cols] = jnp.maximum(best_out[:, cols], best)
             return 0
@@ -130,20 +153,21 @@
     return jnp.where(query[0] == key[0], count, 0)
 
 
-def lower_keys(rep, tail, quarter, pieces):
+def lower_keys(rep, tail, rows, pieces):
+    half = rows // 8
     return [
-        (ref, 0, quarter, jnp.clip(4 * quarter - tail - (rep ^ flip) * quarter, 0, quarter))
-        for ref, flip in pieces
+        (ref, 0, half, jnp.clip(rows - tail - (rep ^ flip) * 2 * half - part * half, 0, half))
+        for ref, flip, part in pieces
     ]
 
 
-def near_kernel(own_reach, own_ref, best_ref, low_0, low_1, across, high,
+def near_kernel(own_reach, own_ref, best_ref, low_0a, low_0b, low_1a, low_2a, across, high,
                 best_out, across_out, high_out, reach_out):
     rows = own_ref.shape[0]
     quarter = across.shape[0] - INFO
     rep, odd, part = position()
     mine = (own_reach[0], own_reach[1])
-    low, beside_head = read_reach(low_0, 3), read_reach(across, 0)
+    low, beside_head = read_reach(low_0b, 3), read_reach(across, 0)
     beside_tail, up = read_reach(across, 3), read_reach(high, 0)
     for n, value in enumerate(low + beside_head + up):
         reach_out[n] = value
@@ -151,11 +175,13 @@
     across_out[...] = jnp.full(across_out.shape, -1.0, F32)
     high_out[...] = jnp.full(high_out.shape, -1.0, F32)
 
-    lows = lower_keys(rep, low[1], quarter, [(low_0, 0), (low_1, 1)])
+    lows = lower_keys(
+        rep, low[1], rows, [(low_0a, 0, 0), (low_0b, 0, 1), (low_1a, 1, 0), (low_2a, 2, 0)]
+    )
     besides = [
         (across, 0, quarter, jnp.clip(rows - beside_tail[1] - part * quarter, 0, quarter))
     ]
-    group(lows[:1], own_ref, rows, best_out, 0, reached(mine, low, 0, rows))
+    group(lows[:2], own_ref, rows, best_out, 0, reached(mine, low, 0, rows))
     count = jnp.where(odd == 1, reached(mine, beside_tail, 0, rows), 0)
     group(besides, own_ref, rows, best_out, 0, count)
     group(lows, across, quarter, across_out, 0, reached(beside_head, low, part * quarter, quarter))
@@ -163,8 +189,8 @@
     group(lows, high, quarter, high_out, 0, reached(up, low, rep * quarter, quarter))
 
 
-def far_kernel(reach_ref, across_ref, high_ref, low_0, low_1, low_2, across, high, up_a, up_b,
-               across_out, high_out, up_out, side_out):
+def far_kernel(reach_ref, across_ref, high_ref, low_0a, low_0b, low_1a, low_1b, low_2a,
+               low_2b, low_3a, across, high, up_a, up_b, across_out, high_out, up_out, side_out):
     quarter = across.shape[0] - INFO
     half = quarter // 2
     rep, _, part = position()
@@ -174,21 +200,26 @@
     across_out[...] = across_ref[...]
     high_out[...] = high_ref[...]
     up_out[...] = jnp.full(up_out.shape, -1.0, F32)
-    lows = lower_keys(rep, low[1], quarter, [(low_2, 2), (low_0, 0), (low_1, 1)])
-    group(lows[:1], across, quarter, across_out, 0, reached(beside, low, part * quarter, quarter))
-    group(lows[:1], high, quarter, high_out, 0, reached(up, low, rep * quarter, quarter))
+
+    lows = lower_keys(
+        rep, low[1], 4 * quarter,
+        [(low_1b, 1, 1), (low_2b, 2, 1), (low_3a, 3, 0), (low_0a, 0, 0), (low_0b, 0, 1), (low_1a, 1, 0), (low_2a, 2, 0)],
+    )
+    group(lows[:2], across, quarter, across_out, 0, reached(beside, low, part * quarter, quarter))
+    group(lows[:3], high, quarter, high_out, 0, reached(up, low, rep * quarter, quarter))
     group(lows, up_a, half, up_out, 0, reached(side, low, (rep ^ 2) * quarter, half))
     group(lows, up_b, half, up_out, half, reached(side, low, rep * quarter + half, half))
 
 
-def last_kernel(reach_ref, side_ref, high_ref, up_ref, low_3, high, up_a, up_b, high_out, up_out):
+def last_kernel(reach_ref, side_ref, high_ref, up_ref, low_3b, high, up_a, up_b,
+                high_out, up_out):
     half = up_a.shape[0]
     quarter = 2 * half
     rep = lax.axis_index("rep")
     low, up = (reach_ref[0], reach_ref[1]), (reach_ref[4], reach_ref[5])
     side = (side_ref[0], side_ref[1])
     high_out[...], up_out[...] = high_ref[...], up_ref[...]
-    lows = lower_keys(rep, low[1], quarter, [(low_3, 3)])
+    lows = lower_keys(rep, low[1], 4 * quarter, [(low_3b, 3, 1)])
     group(lows, high, quarter, high_out, 0, reached(up, low, rep * quarter, quarter))
     group(lows, up_a, half, up_out, 0, reached(side, low, (rep ^ 2) * quarter, half))
     group(lows, up_b, half, up_out, half, reached(side, low, rep * quarter + half, half))
@@ -241,11 +272,12 @@
             name=name,
         )(*arrays)
 
-    mine, across = pl.pallas_call(
+    sizes = [half, half + INFO, quarter + INFO, quarter + INFO]
+    lo, hi, mine, across = pl.pallas_call(
         prepare_kernel,
-        out_shape=[jax.ShapeDtypeStruct((quarter + INFO, width), BF16)] * 2,
-        in_specs=[pl.BlockSpec(memory_space=pl.ANY), VMEM],
-        out_specs=[VMEM] * 2,
+        out_shape=[jax.ShapeDtypeStruct((size, width), BF16) for size in sizes],
+        in_specs=[pl.BlockSpec(memory_space=pltpu.HBM), VMEM],
+        out_specs=[VMEM] * 4,
         scratch_shapes=[pltpu.VMEM((4, half, width), BF16), pltpu.SemaphoreType.DMA((4,))],
         compiler_params=pltpu.CompilerParams(vmem_limit_bytes=PREPARE_LIMIT),
         name="prepare",
@@ -254,36 +286,60 @@
     odd_only, even_only = (lambda i: i % 2 == 1), (lambda i: i % 2 == 0)
     fence = lax.optimization_barrier
 
-    low_0 = along_shard(mine, 2)
+    low_0a = along_shard(lo, 2)
     high = along_shard(mine, -2)
     across = partner(across)
-
-    own, best, own_reach = call(
-        own_kernel, "own", [((rows, width), BF16), ((1, rows), F32), ((2,), jnp.int32)],
-        [VMEM] * 5 + [SMEM], embeddings, labels[None, :], labels[:, None],
-    )
-
-    low_0, own, best = fence((low_0, own, best))
-    low_2 = other_rep(low_0, 2)
-    low_1 = other_rep(low_0, 1)
-    across, high, low_1 = fence((across, high, low_1))
+    low_0b = along_shard(hi, 2)
+
+    low_0a, own_labels = fence((low_0a, labels))
+    low_2a = other_rep(low_0a, 2)
+    low_1a = other_rep(low_0a, 1)
+    own, best, own_reach = pl.pallas_call(
+        own_kernel,
+        out_shape=[
+            jax.ShapeDtypeStruct((rows, width), BF16),
+            jax.ShapeDtypeStruct((1, rows), F32),
+            jax.ShapeDtypeStruct((2,), jnp.int32),
+        ],
+        in_specs=[pl.BlockSpec(memory_space=pltpu.HBM), VMEM],
+        out_specs=[VMEM, VMEM, SMEM],
+        scratch_shapes=[
+            pltpu.VMEM((8, rows), jnp.int32),
+            pltpu.VMEM((4, quarter, width), BF16),
+            pltpu.SemaphoreType.DMA((4,)),
+        ],
+        compiler_params=pltpu.CompilerParams(vmem_limit_bytes=OWN_LIMIT),
+        cost_estimate=pl.CostEstimate(flops=1024, bytes_accessed=1024, transcendentals=0),
+        name="own",
+    )(embeddings, own_labels[None, :])
+
+    across, high, low_0b, low_1a, low_2a, own, best = fence(
+        (across, high, low_0b, low_1a, low_2a, own, best)
+    )
+    low_2b = other_rep(low_0b, 2)
     up_b = along_shard(high[half:], 1, even_only)
     up_a = along_shard(across[:half], -2, odd_only)
+    low_1b = other_rep(low_0b, 1)
+    low_3a = other_rep(low_2a, 1)
     results = [((1, quarter), F32)] * 2
     best, of_across, of_high, reach = call(
         near_kernel, "near", [((1, rows), F32)] + results + [((6,), jnp.int32)],
-        [SMEM] + [VMEM] * 9 + [SMEM], own_reach, own, best, low_0, low_1, across, high,
-    )
-    low_2, up_a, up_b, of_across = fence((low_2, up_a, up_b, of_across))
-    low_3 = other_rep(low_2, 1)
+        [SMEM] + [VMEM] * 11 + [SMEM],
+        own_reach, own, best, low_0a, low_0b, low_1a, low_2a, across, high,
+    )
+    low_2b, up_a, up_b, low_1b, low_3a, of_across = fence(
+        (low_2b, up_a, up_b, low_1b, low_3a, of_across)
+    )
+    low_3b = other_rep(low_2b, 1)
     of_across, of_high, of_up, side = call(
         far_kernel, "far", results + [((1, quarter), F32), ((2,), jnp.int32)],
-        [SMEM] + [VMEM] * 12 + [SMEM],
-        reach, of_across, of_high, low_0, low_1, low_2, across, high, up_a, up_b,
+        [SMEM] + [VMEM] * 16 + [SMEM],
+        reach, of_across, of_high, low_0a, low_0b, low_1a, low_1b, low_2a, low_2b,
+        low_3a, across, high, up_a, up_b,
     )
     of_high, of_up = call(
         last_kernel, "last", results, [SMEM] * 2 + [VMEM] * 8,
-        reach, side, of_high, of_up, low_3, high, up_a, up_b,
+        reach, side, of_high, of_up, low_3b, high, up_a, up_b,
     )
 
     above = along_shard(of_high, 2)

time: 79.9 us -> 77.1 us (0.965); the launches traced: 80 us -> 75.8 us
  waiting for transfers between devices: 34 us -> 28.4 us
  starting transfers between devices: 21.5 us -> 26.6 us
  local copies, waits for them, and re-layouts: 4.84 us -> 0.08 us
  Pallas kernels: 13.1 us -> 14.2 us
    ppermute x3 -> x6, waiting for transfers between devices: 16.4 us -> 5.25 us  [other_rep(): return lax.ppermute(block, 'rep', [(i, i ^ flip) for i in range(reps)])]
    ppermute x6 -> x7, waiting for transfers between devices: 15.6 us -> 23.2 us  [along_shard(): return lax.ppermute(block, 'shard', route)]
    pallas_call x1 -> x2, Pallas kernels: 4.21 us -> 10.1 us  [the longest x1 6.02 us: local(): pl.pallas_call(own_kernel, out_shape=[jax.ShapeDtypeStruct((rows, width),...]
    pallas_call x5 -> x4, Pallas kernels: 8.89 us -> 4.03 us  [call(): pl.pallas_call(kernel, out_shape=[jax.ShapeDtypeStruct(shape, dtype) for...]
    unnamed x6 -> x2, local copies, waits for them, and re-layouts: 3.42 us -> 0.01 us
    ppermute x6 -> x7, starting transfers between devices: 13.3 us -> 15.9 us  [along_shard(): return lax.ppermute(block, 'shard', route)]
    ppermute x2, waiting for transfers between devices: 2.04 us -> 0.01 us  [partner(): return lax.ppermute(block, 'shard', [(i, i ^ 1) for i in range(shards)])]
    ppermute x3 -> x6, starting transfers between devices: 1.5 us -> 3.22 us  [other_rep(): return lax.ppermute(block, 'rep', [(i, i ^ flip) for i in range(reps)])]
  transfers between devices with their start and end apart: 11 -> 15, of which waited for: 5 -> 7; matrix products, arithmetic and copies ran while one was open for 2% -> 0% of each run, Pallas kernels for 11% -> 13%
where the time goes in v1:
time: 77.1 us; the launch traced here: 75.8 us
  waiting for transfers between devices  28.4 us (37%)
  starting transfers between devices  26.6 us (35%)
  Pallas kernels  14.2 us (18%)
  blocking collectives  6.34 us (8%)
    ppermute x7, waiting for transfers between devices, along_shard(): return lax.ppermute(block, 'shard', route)  23.2 us
    ppermute x7, starting transfers between devices, along_shard(): return lax.ppermute(block, 'shard', route)  15.9 us
    ppermute x2, starting transfers between devices, partner(): return lax.ppermute(block, 'shard', [(i, i ^ 1) for i in range(shards)])  7.55 us
    pmax x1, blocking collectives, local(): return lax.pmax(best[0], 'rep')  6.34 us
    pallas_call x1, Pallas kernels, local(): pl.pallas_call(own_kernel, out_shape=[jax.ShapeDtypeStruct((rows, width),...  6.02 us
    ppermute x6, waiting for transfers between devices, other_rep(): return lax.ppermute(block, 'rep', [(i, i ^ flip) for i in range(reps)])  5.25 us
    pallas_call x1, Pallas kernels, local(): pl.pallas_call(prepare_kernel, out_shape=[jax.ShapeDtypeStruct((size, wid...  4.13 us
    pallas_call x4, Pallas kernels, call(): pl.pallas_call(kernel, out_shape=[jax.ShapeDtypeStruct(shape, dtype) for...  4.03 us
  transfers between devices with their start and end apart: 15, of which 7 were waited for; matrix products, arithmetic and copies ran while one was open for 0% of the time, Pallas kernels for 13%

profile of v1, /device:TPU:8, one launch (start us, length us, event | category | flops | bytes accessed | tf_op | source)
XLA Modules:
  0.0 75.8 jit_solution(2516638372792430079)
XLA Ops:
  0.0 4.1 %prepare.1 = (bf16[256,1024]{1,0:T(8,128)(2,1)}, bf16[272,1024]{1,0:T(8,128)(2,1)}, bf16[528,1024]{1,0:T(8,128)(2,1)}, bf16[528,1024]{1,0:T(8,128)(2,1)}) custom-call(bf16[2048,1024]{1,0:T(8,128)(2,1)} %emb_ref.3, s32[16,128]{1,0:T(8,128)} %bitcast.3), custom_call_target="tpu_custom_call" | custom-call | tf_op jit(solution)/shard_map/prepare/pallas_call | solution.py:276
  4.1 1.6 %collective-permute-start.1 = (bf16[528,1024]{1,0:T(8,128)(2,1)}, bf16[528,1024]{1,0:T(8,128)(2,1)S(1)}, u32[]{:S(2)}, u32[]{:S(2)}) collective-permute-start(bf16[528,1024]{1,0:T(8,128)(2,1)} %get-tuple-element.40), channel_id=1, source_target_pairs={{0,4},{4,0},{8,12},{12,8},{16,20},{20,16},{24,28},{28,24},{1,5},{5... | collective-permute-start | bytes 3244040 | tf_op jit(solution)/shard_map/ppermute | solution.py:259
  5.7 2.3 %collective-permute-start.2 = (bf16[528,1024]{1,0:T(8,128)(2,1)}, bf16[528,1024]{1,0:T(8,128)(2,1)S(1)}, u32[]{:S(2)}, u32[]{:S(2)}) collective-permute-start(bf16[528,1024]{1,0:T(8,128)(2,1)} %get-tuple-element.41), channel_id=1, source_target_pairs={{8,0},{12,4},{16,8},{20,12},{24,16},{28,20},{9,1},{13,5},{17,9},{2... | collective-permute-start | bytes 3244040 | tf_op jit(solution)/shard_map/ppermute | solution.py:256
  8.1 3.5 %collective-permute-start = (bf16[256,1024]{1,0:T(8,128)(2,1)}, bf16[256,1024]{1,0:T(8,128)(2,1)S(1)}, u32[]{:S(2)}, u32[]{:S(2)}) collective-permute-start(bf16[256,1024]{1,0:T(8,128)(2,1)} %get-tuple-element.37), channel_id=1, source_target_pairs={{0,8},{4,12},{8,16},{12,20},{16,24},{20,28},{1,9},{5,13},{9,17},{1... | collective-permute-start | bytes 1572872 | tf_op jit(solution)/shard_map/ppermute | solution.py:256
  11.6 3.5 %collective-permute-start.3 = (bf16[272,1024]{1,0:T(8,128)(2,1)}, bf16[272,1024]{1,0:T(8,128)(2,1)S(1)}, u32[]{:S(2)}, u32[]{:S(2)}) collective-permute-start(bf16[272,1024]{1,0:T(8,128)(2,1)} %get-tuple-element.42), channel_id=1, source_target_pairs={{0,8},{4,12},{8,16},{12,20},{16,24},{20,28},{1,9},{5,13},{9,17},{1... | collective-permute-start | bytes 1671176 | tf_op jit(solution)/shard_map/ppermute | solution.py:256
  15.1 9.9 %collective-permute-done.low_0a = bf16[256,1024]{1,0:T(8,128)(2,1)S(1)} collective-permute-done((bf16[256,1024]{1,0:T(8,128)(2,1)}, bf16[256,1024]{1,0:T(8,128)(2,1)S(1)}, u32[]{:S(2)}, u32[]{:S(2)}) %collective-permute-start) | collective-permute-done | bytes 524320 | tf_op jit(solution)/shard_map/ppermute | solution.py:256
  25.1 1.5 %collective-permute-start.5 = (bf16[256,1024]{1,0:T(8,128)(2,1)S(1)}, bf16[256,1024]{1,0:T(8,128)(2,1)S(1)}, u32[]{:S(2)}, u32[]{:S(2)}) collective-permute-start(bf16[256,1024]{1,0:T(8,128)(2,1)S(1)} %collective-permute-done.low_0a), channel_id=1, source_target_pairs={{0,2},{1,3},{2,0},{3,1},{4,6},{5,7},{6,4},{7,5},{8,10},{9,11},{10,... | collective-permute-start | bytes 1572872 | tf_op jit(solution)/shard_map/ppermute | solution.py:262
  26.5 6.0 %own.1 = (bf16[2048,1024]{1,0:T(8,128)(2,1)S(1)}, f32[1,2048]{1,0:T(1,128)S(1)}, s32[2]{0:T(128)S(1)}) custom-call(bf16[2048,1024]{1,0:T(8,128)(2,1)} %emb_ref.3, s32[1,2048]{1,0:T(1,128)S(1)} %bitcast.4), custom_call_target="tpu_custom_call" | custom-call | flops 1024 | bytes 1024 | tf_op jit(solution)/shard_map/own/pallas_call | solution.py:297
  32.6 2.7 %collective-permute-done.3.low_0b = bf16[272,1024]{1,0:T(8,128)(2,1)S(1)} collective-permute-done((bf16[272,1024]{1,0:T(8,128)(2,1)}, bf16[272,1024]{1,0:T(8,128)(2,1)S(1)}, u32[]{:S(2)}, u32[]{:S(2)}) %collective-permute-start.3) | collective-permute-done | bytes 557088 | tf_op jit(solution)/shard_map/ppermute | solution.py:256
  35.2 0.2 collective-permute-done.5.low_2a
  35.5 2.6 %collective-permute-start.8 = (bf16[272,1024]{1,0:T(8,128)(2,1)S(1)}, bf16[272,1024]{1,0:T(8,128)(2,1)S(1)}, u32[]{:S(2)}, u32[]{:S(2)}) collective-permute-start(bf16[272,1024]{1,0:T(8,128)(2,1)S(1)} %slice.7), channel_id=1, source_target_pairs={{0,4},{8,12},{16,20},{24,28},{1,5},{9,13},{17,21},{25,29},{2,6},{1... | collective-permute-start | bytes 1671176 | tf_op jit(solution)/shard_map/ppermute | solution.py:256
  38.2 1.4 %collective-permute-start.6 = (bf16[272,1024]{1,0:T(8,128)(2,1)S(1)}, bf16[272,1024]{1,0:T(8,128)(2,1)S(1)}, u32[]{:S(2)}, u32[]{:S(2)}) collective-permute-start(bf16[272,1024]{1,0:T(8,128)(2,1)S(1)} %collective-permute-done.3.low_0b), channel_id=1, source_target_pairs={{0,2},{1,3},{2,0},{3,1},{4,6},{5,7},{6,4},{7,5},{8,10},{9,11},{10,... | collective-permute-start | bytes 1671176 | tf_op jit(solution)/shard_map/ppermute | solution.py:262
  39.7 0.7 collective-permute-start.7
  40.6 2.1 %near.1 = (f32[1,2048]{1,0:T(1,128)S(1)}, f32[1,512]{1,0:T(1,128)S(1)}, f32[1,512]{1,0:T(1,128)S(1)}, s32[6]{0:T(128)S(1)}) custom-call(s32[2]{0:T(128)S(1)} %get-tuple-element.39.own_reach, bf16[2048,1024]{1,0:T(8,128)(2,1)S(1)} %get-tuple-element.46.own_ref, f32[1,2048]{1,0:T(1,128)S(1)} %get-tuple-element.47.best_ref, ...), custom_call_target="tpu_custom_call" | custom-call | flops 1024 | bytes 1024 | tf_op jit(solution)/shard_map/near/pallas_call | solution.py:265
  42.7 5.5 %collective-permute-done.8.up_b = bf16[272,1024]{1,0:T(8,128)(2,1)S(1)} collective-permute-done((bf16[272,1024]{1,0:T(8,128)(2,1)S(1)}, bf16[272,1024]{1,0:T(8,128)(2,1)S(1)}, u32[]{:S(2)}, u32[]{:S(2)}) %collective-permute-start.8) | collective-permute-done | bytes 557088 | tf_op jit(solution)/shard_map/ppermute | solution.py:256
  48.2 5.0 %collective-permute-done.6.low_2b = bf16[272,1024]{1,0:T(8,128)(2,1)S(1)} collective-permute-done((bf16[272,1024]{1,0:T(8,128)(2,1)S(1)}, bf16[272,1024]{1,0:T(8,128)(2,1)S(1)}, u32[]{:S(2)}, u32[]{:S(2)}) %collective-permute-start.6) | collective-permute-done | bytes 557088 | tf_op jit(solution)/shard_map/ppermute | solution.py:262
  53.2 1.3 %far.1 = (f32[1,512]{1,0:T(1,128)S(1)}, f32[1,512]{1,0:T(1,128)S(1)}, f32[1,512]{1,0:T(1,128)S(1)}, s32[2]{0:T(128)S(1)}) custom-call(s32[6]{0:T(128)S(1)} %get-tuple-element.54.reach_ref, f32[1,512]{1,0:T(1,128)S(1)} %get-tuple-element.56.across_ref, f32[1,512]{1,0:T(1,128)S(1)} %get-tuple-element.57.high_ref, ...), custom_call_target="tpu_custom_call" | custom-call | flops 1024 | bytes 1024 | tf_op jit(solution)/shard_map/far/pallas_call | solution.py:265
  54.6 6.0 %collective-permute-start.11 = (f32[1,512]{1,0:T(1,128)S(1)}, f32[1,512]{1,0:T(1,128)S(1)}, u32[]{:S(2)}, u32[]{:S(2)}) collective-permute-start(f32[1,512]{1,0:T(1,128)S(1)} %get-tuple-element.63), channel_id=1, source_target_pairs={{0,4},{4,0},{8,12},{12,8},{16,20},{20,16},{24,28},{28,24},{1,5},{5... | collective-permute-start | bytes 6152 | tf_op jit(solution)/shard_map/ppermute | solution.py:259
  60.5 0.6 last.1
  61.1 1.9 %collective-permute-start.13 = (f32[1,512]{1,0:T(1,128)S(1)}, f32[1,512]{1,0:T(1,128)S(1)}, u32[]{:S(2)}, u32[]{:S(2)}) collective-permute-start(f32[1,512]{1,0:T(1,128)S(1)} %get-tuple-element.67), channel_id=1, source_target_pairs={{0,8},{4,12},{8,16},{12,20},{16,24},{20,28},{1,9},{5,13},{9,17},{1... | collective-permute-start | bytes 6152 | tf_op jit(solution)/shard_map/ppermute | solution.py:256
  63.1 1.3 %collective-permute-start.14 = (f32[1,512]{1,0:T(1,128)S(1)}, f32[1,512]{1,0:T(1,128)S(1)}, u32[]{:S(2)}, u32[]{:S(2)}) collective-permute-start(f32[1,512]{1,0:T(1,128)S(1)} %get-tuple-element.68), channel_id=1, source_target_pairs={{4,8},{12,16},{20,24},{5,9},{13,17},{21,25},{6,10},{14,18},{22,26}... | collective-permute-start | bytes 6152 | tf_op jit(solution)/shard_map/ppermute | solution.py:256
  64.4 2.2 %collective-permute-done.13.above_ref = f32[1,512]{1,0:T(1,128)S(1)} collective-permute-done((f32[1,512]{1,0:T(1,128)S(1)}, f32[1,512]{1,0:T(1,128)S(1)}, u32[]{:S(2)}, u32[]{:S(2)}) %collective-permute-start.13) | collective-permute-done | bytes 2080 | tf_op jit(solution)/shard_map/ppermute | solution.py:256
  66.6 2.8 %collective-permute-done.14.beside_ref = f32[1,512]{1,0:T(1,128)S(1)} collective-permute-done((f32[1,512]{1,0:T(1,128)S(1)}, f32[1,512]{1,0:T(1,128)S(1)}, u32[]{:S(2)}, u32[]{:S(2)}) %collective-permute-start.14) | collective-permute-done | bytes 2080 | tf_op jit(solution)/shard_map/ppermute | solution.py:256
  69.5 6.3 %pmax.7 = f32[2048]{0:T(1024)} all-reduce(f32[2048]{0:T(1024)S(1)} %bitcast.5), channel_id=1, replica_groups=mesh['shard'=8,'rep'=4] {'rep'}, use_global_device_ids=true, to_apply=%region_0.0 | all-reduce | flops 2048 | bytes 16384 | tf_op jit(solution)/shard_map/pmax | solution.py:351
  (17 shorter events, 0.4 us)
Async XLA Ops:
  0.0 26.5 %copy-start = (s32[2048]{0:T(1024)S(1)}, s32[2048]{0:T(1024)}, u32[]{:S(2)}) copy-start(s32[2048]{0:T(1024)} %param.3) | copy-start | bytes 24580
  4.1 31.3 %collective-permute-start.1 = (bf16[528,1024]{1,0:T(8,128)(2,1)}, bf16[528,1024]{1,0:T(8,128)(2,1)S(1)}, u32[]{:S(2)}, u32[]{:S(2)}) collective-permute-start(bf16[528,1024]{1,0:T(8,128)(2,1)} %get-tuple-element.40), channel_id=1, source_target_pairs={{0,4},{4,0},{8,12},{12,8},{16,20},{20,16},{24,28},{28,24},{1,5},{5... | collective-permute-start | bytes 3244040 | tf_op jit(solution)/shard_map/ppermute | solution.py:259
  5.7 29.7 %collective-permute-start.2 = (bf16[528,1024]{1,0:T(8,128)(2,1)}, bf16[528,1024]{1,0:T(8,128)(2,1)S(1)}, u32[]{:S(2)}, u32[]{:S(2)}) collective-permute-start(bf16[528,1024]{1,0:T(8,128)(2,1)} %get-tuple-element.41), channel_id=1, source_target_pairs={{8,0},{12,4},{16,8},{20,12},{24,16},{28,20},{9,1},{13,5},{17,9},{2... | collective-permute-start | bytes 3244040 | tf_op jit(solution)/shard_map/ppermute | solution.py:256
  8.1 17.0 %collective-permute-start = (bf16[256,1024]{1,0:T(8,128)(2,1)}, bf16[256,1024]{1,0:T(8,128)(2,1)S(1)}, u32[]{:S(2)}, u32[]{:S(2)}) collective-permute-start(bf16[256,1024]{1,0:T(8,128)(2,1)} %get-tuple-element.37), channel_id=1, source_target_pairs={{0,8},{4,12},{8,16},{12,20},{16,24},{20,28},{1,9},{5,13},{9,17},{1... | collective-permute-start | bytes 1572872 | tf_op jit(solution)/shard_map/ppermute | solution.py:256
  11.6 23.7 %collective-permute-start.3 = (bf16[272,1024]{1,0:T(8,128)(2,1)}, bf16[272,1024]{1,0:T(8,128)(2,1)S(1)}, u32[]{:S(2)}, u32[]{:S(2)}) collective-permute-start(bf16[272,1024]{1,0:T(8,128)(2,1)} %get-tuple-element.42), channel_id=1, source_target_pairs={{0,8},{4,12},{8,16},{12,20},{16,24},{20,28},{1,9},{5,13},{9,17},{1... | collective-permute-start | bytes 1671176 | tf_op jit(solution)/shard_map/ppermute | solution.py:256
  25.1 10.4 %collective-permute-start.5 = (bf16[256,1024]{1,0:T(8,128)(2,1)S(1)}, bf16[256,1024]{1,0:T(8,128)(2,1)S(1)}, u32[]{:S(2)}, u32[]{:S(2)}) collective-permute-start(bf16[256,1024]{1,0:T(8,128)(2,1)S(1)} %collective-permute-done.low_0a), channel_id=1, source_target_pairs={{0,2},{1,3},{2,0},{3,1},{4,6},{5,7},{6,4},{7,5},{8,10},{9,11},{10,... | collective-permute-start | bytes 1572872 | tf_op jit(solution)/shard_map/ppermute | solution.py:262
  26.5 8.9 %collective-permute-start.4 = (bf16[256,1024]{1,0:T(8,128)(2,1)S(1)}, bf16[256,1024]{1,0:T(8,128)(2,1)S(1)}, u32[]{:S(2)}, u32[]{:S(2)}) collective-permute-start(bf16[256,1024]{1,0:T(8,128)(2,1)S(1)} %collective-permute-done.low_0a), channel_id=1, source_target_pairs={{0,1},{1,0},{2,3},{3,2},{4,5},{5,4},{6,7},{7,6},{8,9},{9,8},{10,11... | collective-permute-start | bytes 1572872 | tf_op jit(solution)/shard_map/ppermute | solution.py:262
  35.5 12.7 %collective-permute-start.8 = (bf16[272,1024]{1,0:T(8,128)(2,1)S(1)}, bf16[272,1024]{1,0:T(8,128)(2,1)S(1)}, u32[]{:S(2)}, u32[]{:S(2)}) collective-permute-start(bf16[272,1024]{1,0:T(8,128)(2,1)S(1)} %slice.7), channel_id=1, source_target_pairs={{0,4},{8,12},{16,20},{24,28},{1,5},{9,13},{17,21},{25,29},{2,6},{1... | collective-permute-start | bytes 1671176 | tf_op jit(solution)/shard_map/ppermute | solution.py:256
  38.1 10.1 %collective-permute-start.9 = (bf16[272,1024]{1,0:T(8,128)(2,1)S(1)}, bf16[272,1024]{1,0:T(8,128)(2,1)S(1)}, u32[]{:S(2)}, u32[]{:S(2)}) collective-permute-start(bf16[272,1024]{1,0:T(8,128)(2,1)S(1)} %collective-permute-done.3.low_0b), channel_id=1, source_target_pairs={{0,1},{1,0},{2,3},{3,2},{4,5},{5,4},{6,7},{7,6},{8,9},{9,8},{10,11... | collective-permute-start | bytes 1671176 | tf_op jit(solution)/shard_map/ppermute | solution.py:262
  38.2 15.0 %collective-permute-start.6 = (bf16[272,1024]{1,0:T(8,128)(2,1)S(1)}, bf16[272,1024]{1,0:T(8,128)(2,1)S(1)}, u32[]{:S(2)}, u32[]{:S(2)}) collective-permute-start(bf16[272,1024]{1,0:T(8,128)(2,1)S(1)} %collective-permute-done.3.low_0b), channel_id=1, source_target_pairs={{0,2},{1,3},{2,0},{3,1},{4,6},{5,7},{6,4},{7,5},{8,10},{9,11},{10,... | collective-permute-start | bytes 1671176 | tf_op jit(solution)/shard_map/ppermute | solution.py:262
  39.7 3.1 %collective-permute-start.7 = (bf16[256,1024]{1,0:T(8,128)(2,1)S(1)}, bf16[256,1024]{1,0:T(8,128)(2,1)S(1)}, u32[]{:S(2)}, u32[]{:S(2)}) collective-permute-start(bf16[256,1024]{1,0:T(8,128)(2,1)S(1)} %slice.6), channel_id=1, source_target_pairs={{12,4},{20,12},{28,20},{13,5},{21,13},{29,21},{14,6},{22,14},{30,2... | collective-permute-start | bytes 1572872 | tf_op jit(solution)/shard_map/ppermute | solution.py:256
  40.4 2.4 %collective-permute-start.10 = (bf16[256,1024]{1,0:T(8,128)(2,1)S(1)}, bf16[256,1024]{1,0:T(8,128)(2,1)S(1)}, u32[]{:S(2)}, u32[]{:S(2)}) collective-permute-start(bf16[256,1024]{1,0:T(8,128)(2,1)S(1)} %collective-permute-done.5.low_2a), channel_id=1, source_target_pairs={{0,1},{1,0},{2,3},{3,2},{4,5},{5,4},{6,7},{7,6},{8,9},{9,8},{10,11... | collective-permute-start | bytes 1572872 | tf_op jit(solution)/shard_map/ppermute | solution.py:262
  53.2 7.3 %collective-permute-start.12 = (bf16[272,1024]{1,0:T(8,128)(2,1)S(1)}, bf16[272,1024]{1,0:T(8,128)(2,1)S(1)}, u32[]{:S(2)}, u32[]{:S(2)}) collective-permute-start(bf16[272,1024]{1,0:T(8,128)(2,1)S(1)} %collective-permute-done.6.low_2b), channel_id=1, source_target_pairs={{0,1},{1,0},{2,3},{3,2},{4,5},{5,4},{6,7},{7,6},{8,9},{9,8},{10,11... | collective-permute-start | bytes 1671176 | tf_op jit(solution)/shard_map/ppermute | solution.py:262
  54.6 9.8 %collective-permute-start.11 = (f32[1,512]{1,0:T(1,128)S(1)}, f32[1,512]{1,0:T(1,128)S(1)}, u32[]{:S(2)}, u32[]{:S(2)}) collective-permute-start(f32[1,512]{1,0:T(1,128)S(1)} %get-tuple-element.63), channel_id=1, source_target_pairs={{0,4},{4,0},{8,12},{12,8},{16,20},{20,16},{24,28},{28,24},{1,5},{5... | collective-permute-start | bytes 6152 | tf_op jit(solution)/shard_map/ppermute | solution.py:259
  61.1 5.5 %collective-permute-start.13 = (f32[1,512]{1,0:T(1,128)S(1)}, f32[1,512]{1,0:T(1,128)S(1)}, u32[]{:S(2)}, u32[]{:S(2)}) collective-permute-start(f32[1,512]{1,0:T(1,128)S(1)} %get-tuple-element.67), channel_id=1, source_target_pairs={{0,8},{4,12},{8,16},{12,20},{16,24},{20,28},{1,9},{5,13},{9,17},{1... | collective-permute-start | bytes 6152 | tf_op jit(solution)/shard_map/ppermute | solution.py:256
  63.1 6.4 %collective-permute-start.14 = (f32[1,512]{1,0:T(1,128)S(1)}, f32[1,512]{1,0:T(1,128)S(1)}, u32[]{:S(2)}, u32[]{:S(2)}) collective-permute-start(f32[1,512]{1,0:T(1,128)S(1)} %get-tuple-element.68), channel_id=1, source_target_pairs={{4,8},{12,16},{20,24},{5,9},{13,17},{21,25},{6,10},{14,18},{22,26}... | collective-permute-start | bytes 6152 | tf_op jit(solution)/shard_map/ppermute | solution.py:256

commit v2 on v1

--- a/solution.py
+++ b/solution.py
@@ -15,7 +15,7 @@
 INFO = 16
 VMEM_LIMIT = 32 * 1024 * 1024
 OWN_LIMIT = 46 * 1024 * 1024
-PREPARE_LIMIT = 60 * 1024 * 1024
+PREPARE_LIMIT = 50 * 1024 * 1024
 VMEM = pl.BlockSpec(memory_space=pltpu.VMEM)
 SMEM = pl.BlockSpec(memory_space=pltpu.SMEM)
 
@@ -41,7 +41,7 @@
     return rep, odd, rep ^ (1 + odd)
 
 
-def prepare_kernel(emb_ref, labels_ref, lo_out, hi_out, mine_out, across_out, raw, sems):
+def prepare_kernel(emb_ref, labels_hbm, lo_out, hi_out, mine_out, across_out, raw, labels_ref, sems):
     rep, odd, _ = position()
     quarter = mine_out.shape[0] - INFO
     part = quarter // 2
@@ -51,6 +51,9 @@
         at = pl.multiple_of(piece * quarter + (n % 2) * part, part)
         copies.append(pltpu.make_async_copy(emb_ref.at[pl.ds(at, part), :], raw.at[n], sems.at[n]))
         copies[-1].start()
+    fetch = pltpu.make_async_copy(labels_hbm, labels_ref, sems.at[4])
+    fetch.start()
+    fetch.wait()
     labels = labels_ref[...]
     first, last = jnp.min(labels), jnp.max(labels)
     head = jnp.sum((labels == first).astype(jnp.int32))
@@ -276,9 +279,13 @@
     lo, hi, mine, across = pl.pallas_call(
         prepare_kernel,
         out_shape=[jax.ShapeDtypeStruct((size, width), BF16) for size in sizes],
-        in_specs=[pl.BlockSpec(memory_space=pltpu.HBM), VMEM],
+        in_specs=[pl.BlockSpec(memory_space=pltpu.HBM)] * 2,
         out_specs=[VMEM] * 4,
-        scratch_shapes=[pltpu.VMEM((4, half, width), BF16), pltpu.SemaphoreType.DMA((4,))],
+        scratch_shapes=[
+            pltpu.VMEM((4, half, width), BF16),
+            pltpu.VMEM((rows // 128, 128), jnp.int32),
+            pltpu.SemaphoreType.DMA((5,)),
+        ],
         compiler_params=pltpu.CompilerParams(vmem_limit_bytes=PREPARE_LIMIT),
         name="prepare",
     )(embeddings, labels.reshape(rows // 128, 128))
@@ -313,12 +320,11 @@
         name="own",
     )(embeddings, own_labels[None, :])
 
-    across, high, low_0b, low_1a, low_2a, own, best = fence(
-        (across, high, low_0b, low_1a, low_2a, own, best)
-    )
+    across, high, own, best = fence((across, high, own, best))
+    up_a = along_shard(across[:half], -2, odd_only)
+    up_b = along_shard(high[half:], 1, even_only)
+    low_0b, low_1a, low_2a, across, high = fence((low_0b, low_1a, low_2a, across, high))
     low_2b = other_rep(low_0b, 2)
-    up_b = along_shard(high[half:], 1, even_only)
-    up_a = along_shard(across[:half], -2, odd_only)
     low_1b = other_rep(low_0b, 1)
     low_3a = other_rep(low_2a, 1)
     results = [((1, quarter), F32)] * 2

time: 77.1 us -> 74.4 us (0.965); the launches traced: 75.8 us -> 75.6 us
  Pallas kernels: 14.2 us -> 11.9 us
  starting transfers between devices: 26.6 us -> 28.2 us
    ppermute x7, starting transfers between devices: 15.9 us -> 20.8 us  [along_shard(): return lax.ppermute(block, 'shard', route)]
    ppermute x2, starting transfers between devices: 7.55 us -> 4.18 us  [partner(): return lax.ppermute(block, 'shard', [(i, i ^ 1) for i in range(shards)])]
    pallas_call x1, Pallas kernels: 4.13 us -> 1.87 us  [local(): pl.pallas_call(prepare_kernel, out_shape=[jax.ShapeDtypeStruct((size, wid...]
where the time goes in v2:
time: 74.4 us; the launch traced here: 75.6 us
  starting transfers between devices  28.2 us (38%)
  waiting for transfers between devices  28.1 us (38%)
  Pallas kernels  11.9 us (16%)
  blocking collectives  6.44 us (9%)
  local copies, waits for them, and re-layouts  0.77 us (1%)
    ppermute x7, waiting for transfers between devices, along_shard(): return lax.ppermute(block, 'shard', route)  22.9 us
    ppermute x7, starting transfers between devices, along_shard(): return lax.ppermute(block, 'shard', route)  20.8 us
    pmax x1, blocking collectives, local(): return lax.pmax(best[0], 'rep')  6.44 us
    pallas_call x1, Pallas kernels, local(): pl.pallas_call(own_kernel, out_shape=[jax.ShapeDtypeStruct((rows, width),...  6.02 us
    ppermute x6, waiting for transfers between devices, other_rep(): return lax.ppermute(block, 'rep', [(i, i ^ flip) for i in range(reps)])  5.26 us
    ppermute x2, starting transfers between devices, partner(): return lax.ppermute(block, 'shard', [(i, i ^ 1) for i in range(shards)])  4.18 us
    pallas_call x4, Pallas kernels, call(): pl.pallas_call(kernel, out_shape=[jax.ShapeDtypeStruct(shape, dtype) for...  4.03 us
    ppermute x6, starting transfers between devices, other_rep(): return lax.ppermute(block, 'rep', [(i, i ^ flip) for i in range(reps)])  3.22 us
  transfers between devices with their start and end apart: 15, of which 7 were waited for; matrix products, arithmetic and copies ran while one was open for 0% of the time, Pallas kernels for 13%

profile of v2, /device:TPU:8, one launch (start us, length us, event | category | flops | bytes accessed | tf_op | source)
XLA Modules:
  0.0 75.6 jit_solution(11173445609253760546)
XLA Ops:
  0.0 0.7 copy-done
  0.7 1.9 %prepare.1 = (bf16[256,1024]{1,0:T(8,128)(2,1)S(1)}, bf16[272,1024]{1,0:T(8,128)(2,1)S(1)}, bf16[528,1024]{1,0:T(8,128)(2,1)S(1)}, bf16[528,1024]{1,0:T(8,128)(2,1)S(1)}) custom-call(bf16[2048,1024]{1,0:T(8,128)(2,1)} %emb_ref.3, s32[16,128]{1,0:T(8,128)S(1)} %bitcast.3), custom_call_target="tpu_custom_call" | custom-call | tf_op jit(solution)/shard_map/prepare/pallas_call | solution.py:279
  2.6 1.6 %collective-permute-start.1 = (bf16[528,1024]{1,0:T(8,128)(2,1)S(1)}, bf16[528,1024]{1,0:T(8,128)(2,1)S(1)}, u32[]{:S(2)}, u32[]{:S(2)}) collective-permute-start(bf16[528,1024]{1,0:T(8,128)(2,1)S(1)} %get-tuple-element.42), channel_id=1, source_target_pairs={{0,4},{4,0},{8,12},{12,8},{16,20},{20,16},{24,28},{28,24},{1,5},{5... | collective-permute-start | bytes 3244040 | tf_op jit(solution)/shard_map/ppermute | solution.py:262
  4.2 2.3 %collective-permute-start.2 = (bf16[528,1024]{1,0:T(8,128)(2,1)S(1)}, bf16[528,1024]{1,0:T(8,128)(2,1)S(1)}, u32[]{:S(2)}, u32[]{:S(2)}) collective-permute-start(bf16[528,1024]{1,0:T(8,128)(2,1)S(1)} %get-tuple-element.43), channel_id=1, source_target_pairs={{8,0},{12,4},{16,8},{20,12},{24,16},{28,20},{9,1},{13,5},{17,9},{2... | collective-permute-start | bytes 3244040 | tf_op jit(solution)/shard_map/ppermute | solution.py:259
  6.5 3.5 %collective-permute-start = (bf16[256,1024]{1,0:T(8,128)(2,1)S(1)}, bf16[256,1024]{1,0:T(8,128)(2,1)S(1)}, u32[]{:S(2)}, u32[]{:S(2)}) collective-permute-start(bf16[256,1024]{1,0:T(8,128)(2,1)S(1)} %get-tuple-element.39), channel_id=1, source_target_pairs={{0,8},{4,12},{8,16},{12,20},{16,24},{20,28},{1,9},{5,13},{9,17},{1... | collective-permute-start | bytes 1572872 | tf_op jit(solution)/shard_map/ppermute | solution.py:259
  10.0 3.5 %collective-permute-start.3 = (bf16[272,1024]{1,0:T(8,128)(2,1)S(1)}, bf16[272,1024]{1,0:T(8,128)(2,1)S(1)}, u32[]{:S(2)}, u32[]{:S(2)}) collective-permute-start(bf16[272,1024]{1,0:T(8,128)(2,1)S(1)} %get-tuple-element.49), channel_id=1, source_target_pairs={{0,8},{4,12},{8,16},{12,20},{16,24},{20,28},{1,9},{5,13},{9,17},{1... | collective-permute-start | bytes 1671176 | tf_op jit(solution)/shard_map/ppermute | solution.py:259
  13.6 9.7 %collective-permute-done.low_0a = bf16[256,1024]{1,0:T(8,128)(2,1)S(1)} collective-permute-done((bf16[256,1024]{1,0:T(8,128)(2,1)S(1)}, bf16[256,1024]{1,0:T(8,128)(2,1)S(1)}, u32[]{:S(2)}, u32[]{:S(2)}) %collective-permute-start) | collective-permute-done | bytes 524320 | tf_op jit(solution)/shard_map/ppermute | solution.py:259
  23.3 1.5 %collective-permute-start.5 = (bf16[256,1024]{1,0:T(8,128)(2,1)S(1)}, bf16[256,1024]{1,0:T(8,128)(2,1)S(1)}, u32[]{:S(2)}, u32[]{:S(2)}) collective-permute-start(bf16[256,1024]{1,0:T(8,128)(2,1)S(1)} %collective-permute-done.low_0a), channel_id=1, source_target_pairs={{0,2},{1,3},{2,0},{3,1},{4,6},{5,7},{6,4},{7,5},{8,10},{9,11},{10,... | collective-permute-start | bytes 1572872 | tf_op jit(solution)/shard_map/ppermute | solution.py:265
  24.8 6.0 %own.1 = (bf16[2048,1024]{1,0:T(8,128)(2,1)S(1)}, f32[1,2048]{1,0:T(1,128)S(1)}, s32[2]{0:T(128)S(1)}) custom-call(bf16[2048,1024]{1,0:T(8,128)(2,1)} %emb_ref.3, s32[1,2048]{1,0:T(1,128)S(1)} %bitcast.4), custom_call_target="tpu_custom_call" | custom-call | flops 1024 | bytes 1024 | tf_op jit(solution)/shard_map/own/pallas_call | solution.py:304
  30.8 0.6 collective-permute-done.2.high
  31.4 2.0 %collective-permute-done.3.low_0b = bf16[272,1024]{1,0:T(8,128)(2,1)S(1)} collective-permute-done((bf16[272,1024]{1,0:T(8,128)(2,1)S(1)}, bf16[272,1024]{1,0:T(8,128)(2,1)S(1)}, u32[]{:S(2)}, u32[]{:S(2)}) %collective-permute-start.3) | collective-permute-done | bytes 557088 | tf_op jit(solution)/shard_map/ppermute | solution.py:259
  33.7 2.6 %collective-permute-start.8 = (bf16[272,1024]{1,0:T(8,128)(2,1)S(1)}, bf16[272,1024]{1,0:T(8,128)(2,1)S(1)}, u32[]{:S(2)}, u32[]{:S(2)}) collective-permute-start(bf16[272,1024]{1,0:T(8,128)(2,1)S(1)} %slice.7), channel_id=1, source_target_pairs={{0,4},{8,12},{16,20},{24,28},{1,5},{9,13},{17,21},{25,29},{2,6},{1... | collective-permute-start | bytes 1671176 | tf_op jit(solution)/shard_map/ppermute | solution.py:259
  36.4 1.4 %collective-permute-start.6 = (bf16[272,1024]{1,0:T(8,128)(2,1)S(1)}, bf16[272,1024]{1,0:T(8,128)(2,1)S(1)}, u32[]{:S(2)}, u32[]{:S(2)}) collective-permute-start(bf16[272,1024]{1,0:T(8,128)(2,1)S(1)} %collective-permute-done.3.low_0b), channel_id=1, source_target_pairs={{0,2},{1,3},{2,0},{3,1},{4,6},{5,7},{6,4},{7,5},{8,10},{9,11},{10,... | collective-permute-start | bytes 1671176 | tf_op jit(solution)/shard_map/ppermute | solution.py:265
  37.8 0.7 collective-permute-start.7
  38.7 2.1 %near.1 = (f32[1,2048]{1,0:T(1,128)S(1)}, f32[1,512]{1,0:T(1,128)S(1)}, f32[1,512]{1,0:T(1,128)S(1)}, s32[6]{0:T(128)S(1)}) custom-call(s32[2]{0:T(128)S(1)} %get-tuple-element.41.own_reach, bf16[2048,1024]{1,0:T(8,128)(2,1)S(1)} %get-tuple-element.46.own_ref, f32[1,2048]{1,0:T(1,128)S(1)} %get-tuple-element.47.best_ref, ...), custom_call_target="tpu_custom_call" | custom-call | flops 1024 | bytes 1024 | tf_op jit(solution)/shard_map/near/pallas_call | solution.py:268
  40.9 5.5 %collective-permute-done.8.up_b = bf16[272,1024]{1,0:T(8,128)(2,1)S(1)} collective-permute-done((bf16[272,1024]{1,0:T(8,128)(2,1)S(1)}, bf16[272,1024]{1,0:T(8,128)(2,1)S(1)}, u32[]{:S(2)}, u32[]{:S(2)}) %collective-permute-start.8) | collective-permute-done | bytes 557088 | tf_op jit(solution)/shard_map/ppermute | solution.py:259
  46.4 5.0 %collective-permute-done.6.low_2b = bf16[272,1024]{1,0:T(8,128)(2,1)S(1)} collective-permute-done((bf16[272,1024]{1,0:T(8,128)(2,1)S(1)}, bf16[272,1024]{1,0:T(8,128)(2,1)S(1)}, u32[]{:S(2)}, u32[]{:S(2)}) %collective-permute-start.6) | collective-permute-done | bytes 557088 | tf_op jit(solution)/shard_map/ppermute | solution.py:265
  51.4 1.3 %far.1 = (f32[1,512]{1,0:T(1,128)S(1)}, f32[1,512]{1,0:T(1,128)S(1)}, f32[1,512]{1,0:T(1,128)S(1)}, s32[2]{0:T(128)S(1)}) custom-call(s32[6]{0:T(128)S(1)} %get-tuple-element.58.reach_ref, f32[1,512]{1,0:T(1,128)S(1)} %get-tuple-element.60.across_ref, f32[1,512]{1,0:T(1,128)S(1)} %get-tuple-element.61.high_ref, ...), custom_call_target="tpu_custom_call" | custom-call | flops 1024 | bytes 1024 | tf_op jit(solution)/shard_map/far/pallas_call | solution.py:268
  52.7 2.6 %collective-permute-start.11 = (f32[1,512]{1,0:T(1,128)S(1)}, f32[1,512]{1,0:T(1,128)S(1)}, u32[]{:S(2)}, u32[]{:S(2)}) collective-permute-start(f32[1,512]{1,0:T(1,128)S(1)} %get-tuple-element.67), channel_id=1, source_target_pairs={{0,4},{4,0},{8,12},{12,8},{16,20},{20,16},{24,28},{28,24},{1,5},{5... | collective-permute-start | bytes 6152 | tf_op jit(solution)/shard_map/ppermute | solution.py:262
  55.3 0.6 last.1
  55.9 6.9 %collective-permute-start.13 = (f32[1,512]{1,0:T(1,128)S(1)}, f32[1,512]{1,0:T(1,128)S(1)}, u32[]{:S(2)}, u32[]{:S(2)}) collective-permute-start(f32[1,512]{1,0:T(1,128)S(1)} %get-tuple-element.71), channel_id=1, source_target_pairs={{0,8},{4,12},{8,16},{12,20},{16,24},{20,28},{1,9},{5,13},{9,17},{1... | collective-permute-start | bytes 6152 | tf_op jit(solution)/shard_map/ppermute | solution.py:259
  62.8 1.3 %collective-permute-start.14 = (f32[1,512]{1,0:T(1,128)S(1)}, f32[1,512]{1,0:T(1,128)S(1)}, u32[]{:S(2)}, u32[]{:S(2)}) collective-permute-start(f32[1,512]{1,0:T(1,128)S(1)} %get-tuple-element.72), channel_id=1, source_target_pairs={{4,8},{12,16},{20,24},{5,9},{13,17},{21,25},{6,10},{14,18},{22,26}... | collective-permute-start | bytes 6152 | tf_op jit(solution)/shard_map/ppermute | solution.py:259
  64.1 5.1 %collective-permute-done.14.beside_ref = f32[1,512]{1,0:T(1,128)S(1)} collective-permute-done((f32[1,512]{1,0:T(1,128)S(1)}, f32[1,512]{1,0:T(1,128)S(1)}, u32[]{:S(2)}, u32[]{:S(2)}) %collective-permute-start.14) | collective-permute-done | bytes 2080 | tf_op jit(solution)/shard_map/ppermute | solution.py:259
  69.2 6.4 %pmax.7 = f32[2048]{0:T(1024)} all-reduce(f32[2048]{0:T(1024)S(1)} %bitcast.5), channel_id=1, replica_groups=mesh['shard'=8,'rep'=4] {'rep'}, use_global_device_ids=true, to_apply=%region_0.0 | all-reduce | flops 2048 | bytes 16384 | tf_op jit(solution)/shard_map/pmax | solution.py:357
  (19 shorter events, 0.7 us)
Async XLA Ops:
  0.0 0.7 copy-start
  0.7 24.1 %copy-start.1 = (s32[2048]{0:T(1024)S(1)}, s32[2048]{0:T(1024)}, u32[]{:S(2)}) copy-start(s32[2048]{0:T(1024)} %param.3) | copy-start | bytes 24580
  2.6 28.2 %collective-permute-start.1 = (bf16[528,1024]{1,0:T(8,128)(2,1)S(1)}, bf16[528,1024]{1,0:T(8,128)(2,1)S(1)}, u32[]{:S(2)}, u32[]{:S(2)}) collective-permute-start(bf16[528,1024]{1,0:T(8,128)(2,1)S(1)} %get-tuple-element.42), channel_id=1, source_target_pairs={{0,4},{4,0},{8,12},{12,8},{16,20},{20,16},{24,28},{28,24},{1,5},{5... | collective-permute-start | bytes 3244040 | tf_op jit(solution)/shard_map/ppermute | solution.py:262
  4.2 27.2 %collective-permute-start.2 = (bf16[528,1024]{1,0:T(8,128)(2,1)S(1)}, bf16[528,1024]{1,0:T(8,128)(2,1)S(1)}, u32[]{:S(2)}, u32[]{:S(2)}) collective-permute-start(bf16[528,1024]{1,0:T(8,128)(2,1)S(1)} %get-tuple-element.43), channel_id=1, source_target_pairs={{8,0},{12,4},{16,8},{20,12},{24,16},{28,20},{9,1},{13,5},{17,9},{2... | collective-permute-start | bytes 3244040 | tf_op jit(solution)/shard_map/ppermute | solution.py:259
  6.5 16.8 %collective-permute-start = (bf16[256,1024]{1,0:T(8,128)(2,1)S(1)}, bf16[256,1024]{1,0:T(8,128)(2,1)S(1)}, u32[]{:S(2)}, u32[]{:S(2)}) collective-permute-start(bf16[256,1024]{1,0:T(8,128)(2,1)S(1)} %get-tuple-element.39), channel_id=1, source_target_pairs={{0,8},{4,12},{8,16},{12,20},{16,24},{20,28},{1,9},{5,13},{9,17},{1... | collective-permute-start | bytes 1572872 | tf_op jit(solution)/shard_map/ppermute | solution.py:259
  10.0 23.4 %collective-permute-start.3 = (bf16[272,1024]{1,0:T(8,128)(2,1)S(1)}, bf16[272,1024]{1,0:T(8,128)(2,1)S(1)}, u32[]{:S(2)}, u32[]{:S(2)}) collective-permute-start(bf16[272,1024]{1,0:T(8,128)(2,1)S(1)} %get-tuple-element.49), channel_id=1, source_target_pairs={{0,8},{4,12},{8,16},{12,20},{16,24},{20,28},{1,9},{5,13},{9,17},{1... | collective-permute-start | bytes 1671176 | tf_op jit(solution)/shard_map/ppermute | solution.py:259
  23.3 10.4 %collective-permute-start.5 = (bf16[256,1024]{1,0:T(8,128)(2,1)S(1)}, bf16[256,1024]{1,0:T(8,128)(2,1)S(1)}, u32[]{:S(2)}, u32[]{:S(2)}) collective-permute-start(bf16[256,1024]{1,0:T(8,128)(2,1)S(1)} %collective-permute-done.low_0a), channel_id=1, source_target_pairs={{0,2},{1,3},{2,0},{3,1},{4,6},{5,7},{6,4},{7,5},{8,10},{9,11},{10,... | collective-permute-start | bytes 1572872 | tf_op jit(solution)/shard_map/ppermute | solution.py:265
  24.8 8.9 %collective-permute-start.4 = (bf16[256,1024]{1,0:T(8,128)(2,1)S(1)}, bf16[256,1024]{1,0:T(8,128)(2,1)S(1)}, u32[]{:S(2)}, u32[]{:S(2)}) collective-permute-start(bf16[256,1024]{1,0:T(8,128)(2,1)S(1)} %collective-permute-done.low_0a), channel_id=1, source_target_pairs={{0,1},{1,0},{2,3},{3,2},{4,5},{5,4},{6,7},{7,6},{8,9},{9,8},{10,11... | collective-permute-start | bytes 1572872 | tf_op jit(solution)/shard_map/ppermute | solution.py:265
  33.7 12.7 %collective-permute-start.8 = (bf16[272,1024]{1,0:T(8,128)(2,1)S(1)}, bf16[272,1024]{1,0:T(8,128)(2,1)S(1)}, u32[]{:S(2)}, u32[]{:S(2)}) collective-permute-start(bf16[272,1024]{1,0:T(8,128)(2,1)S(1)} %slice.7), channel_id=1, source_target_pairs={{0,4},{8,12},{16,20},{24,28},{1,5},{9,13},{17,21},{25,29},{2,6},{1... | collective-permute-start | bytes 1671176 | tf_op jit(solution)/shard_map/ppermute | solution.py:259
  36.3 10.1 %collective-permute-start.9 = (bf16[272,1024]{1,0:T(8,128)(2,1)S(1)}, bf16[272,1024]{1,0:T(8,128)(2,1)S(1)}, u32[]{:S(2)}, u32[]{:S(2)}) collective-permute-start(bf16[272,1024]{1,0:T(8,128)(2,1)S(1)} %collective-permute-done.3.low_0b), channel_id=1, source_target_pairs={{0,1},{1,0},{2,3},{3,2},{4,5},{5,4},{6,7},{7,6},{8,9},{9,8},{10,11... | collective-permute-start | bytes 1671176 | tf_op jit(solution)/shard_map/ppermute | solution.py:265
  36.4 15.0 %collective-permute-start.6 = (bf16[272,1024]{1,0:T(8,128)(2,1)S(1)}, bf16[272,1024]{1,0:T(8,128)(2,1)S(1)}, u32[]{:S(2)}, u32[]{:S(2)}) collective-permute-start(bf16[272,1024]{1,0:T(8,128)(2,1)S(1)} %collective-permute-done.3.low_0b), channel_id=1, source_target_pairs={{0,2},{1,3},{2,0},{3,1},{4,6},{5,7},{6,4},{7,5},{8,10},{9,11},{10,... | collective-permute-start | bytes 1671176 | tf_op jit(solution)/shard_map/ppermute | solution.py:265
  37.8 3.1 %collective-permute-start.7 = (bf16[256,1024]{1,0:T(8,128)(2,1)S(1)}, bf16[256,1024]{1,0:T(8,128)(2,1)S(1)}, u32[]{:S(2)}, u32[]{:S(2)}) collective-permute-start(bf16[256,1024]{1,0:T(8,128)(2,1)S(1)} %slice.6), channel_id=1, source_target_pairs={{12,4},{20,12},{28,20},{13,5},{21,13},{29,21},{14,6},{22,14},{30,2... | collective-permute-start | bytes 1572872 | tf_op jit(solution)/shard_map/ppermute | solution.py:259
  38.5 2.4 %collective-permute-start.10 = (bf16[256,1024]{1,0:T(8,128)(2,1)S(1)}, bf16[256,1024]{1,0:T(8,128)(2,1)S(1)}, u32[]{:S(2)}, u32[]{:S(2)}) collective-permute-start(bf16[256,1024]{1,0:T(8,128)(2,1)S(1)} %collective-permute-done.5.low_2a), channel_id=1, source_target_pairs={{0,1},{1,0},{2,3},{3,2},{4,5},{5,4},{6,7},{7,6},{8,9},{9,8},{10,11... | collective-permute-start | bytes 1572872 | tf_op jit(solution)/shard_map/ppermute | solution.py:265
  51.4 3.9 %collective-permute-start.12 = (bf16[272,1024]{1,0:T(8,128)(2,1)S(1)}, bf16[272,1024]{1,0:T(8,128)(2,1)S(1)}, u32[]{:S(2)}, u32[]{:S(2)}) collective-permute-start(bf16[272,1024]{1,0:T(8,128)(2,1)S(1)} %collective-permute-done.6.low_2b), channel_id=1, source_target_pairs={{0,1},{1,0},{2,3},{3,2},{4,5},{5,4},{6,7},{7,6},{8,9},{9,8},{10,11... | collective-permute-start | bytes 1671176 | tf_op jit(solution)/shard_map/ppermute | solution.py:265
  52.7 11.4 %collective-permute-start.11 = (f32[1,512]{1,0:T(1,128)S(1)}, f32[1,512]{1,0:T(1,128)S(1)}, u32[]{:S(2)}, u32[]{:S(2)}) collective-permute-start(f32[1,512]{1,0:T(1,128)S(1)} %get-tuple-element.67), channel_id=1, source_target_pairs={{0,4},{4,0},{8,12},{12,8},{16,20},{20,16},{24,28},{28,24},{1,5},{5... | collective-permute-start | bytes 6152 | tf_op jit(solution)/shard_map/ppermute | solution.py:262
  55.9 8.2 %collective-permute-start.13 = (f32[1,512]{1,0:T(1,128)S(1)}, f32[1,512]{1,0:T(1,128)S(1)}, u32[]{:S(2)}, u32[]{:S(2)}) collective-permute-start(f32[1,512]{1,0:T(1,128)S(1)} %get-tuple-element.71), channel_id=1, source_target_pairs={{0,8},{4,12},{8,16},{12,20},{16,24},{20,28},{1,9},{5,13},{9,17},{1... | collective-permute-start | bytes 6152 | tf_op jit(solution)/shard_map/ppermute | solution.py:259
  62.8 6.4 %collective-permute-start.14 = (f32[1,512]{1,0:T(1,128)S(1)}, f32[1,512]{1,0:T(1,128)S(1)}, u32[]{:S(2)}, u32[]{:S(2)}) collective-permute-start(f32[1,512]{1,0:T(1,128)S(1)} %get-tuple-element.72), channel_id=1, source_target_pairs={{4,8},{12,16},{20,24},{5,9},{13,17},{21,25},{6,10},{14,18},{22,26}... | collective-permute-start | bytes 6152 | tf_op jit(solution)/shard_map/ppermute | solution.py:259

commit v3 on v2

--- a/solution.py
+++ b/solution.py
@@ -85,18 +85,20 @@
 
 
 def group(keys, queries_ref, query_rows, out_ref, out_at, count):
-    step = min(WIDE, query_rows)
+    step = min(2 * WIDE, query_rows)
 
     def over_queries(j, _):
         at = pl.multiple_of(j * step, step)
         queries = queries_ref[pl.ds(at, step), :]
         best = None
         for ref, row, rows, first in keys:
-            scores = score(ref[pl.ds(row, rows), :], queries)
-            index = lax.broadcasted_iota(jnp.int32, scores.shape, 0)
-            top = fold(jnp.where(index >= first, scores, -1.0))
-            best = top if best is None else jnp.maximum(best, top)
-        best = jnp.max(best, axis=0, keepdims=True)
+            scores = score(queries, ref[pl.ds(row, rows), :])
+            for n in range(0, rows, 128):
+                part = scores[:, n : n + 128]
+                lane = lax.broadcasted_iota(jnp.int32, part.shape, 1) + n
+                part = jnp.where(lane >= first, part, -1.0)
+                best = part if best is None else jnp.maximum(best, part)
+        best = jnp.max(jnp.transpose(best), axis=0, keepdims=True)
         col = lax.broadcasted_iota(jnp.int32, best.shape, 1) + at
         cols = pl.ds(pl.multiple_of(out_at + at, TILE), step)
         out_ref[:, cols] = jnp.maximum(out_ref[:, cols], jnp.where(col < count, best, -1.0))

time: 74.4 us -> 75.6 us (1.016); the launches traced: 75.6 us -> 74.2 us
  Pallas kernels: 11.9 us -> 20.1 us
  waiting for transfers between devices: 28.1 us -> 22.6 us
  starting transfers between devices: 28.2 us -> 23.9 us
    pallas_call x4, Pallas kernels: 4.03 us -> 12.2 us  [call(): pl.pallas_call(kernel, out_shape=[jax.ShapeDtypeStruct(shape, dtype) for...]
    ppermute x7, waiting for transfers between devices: 22.9 us -> 17.4 us  [along_shard(): return lax.ppermute(block, 'shard', route)]
    ppermute x7, starting transfers between devices: 20.8 us -> 15.9 us  [along_shard(): return lax.ppermute(block, 'shard', route)]
  transfers between devices with their start and end apart: 15 -> 15, of which waited for: 7 -> 7; matrix products, arithmetic and copies ran while one was open for 0% -> 0% of each run, Pallas kernels for 13% -> 25%
where the time goes in v3:
time: 75.6 us; the launch traced here: 74.2 us
  starting transfers between devices  23.9 us (32%)
  waiting for transfers between devices  22.6 us (30%)
  Pallas kernels  20.1 us (27%)
  blocking collectives  6.64 us (9%)
  local copies, waits for them, and re-layouts  0.77 us (1%)
    ppermute x7, waiting for transfers between devices, along_shard(): return lax.ppermute(block, 'shard', route)  17.4 us
    ppermute x7, starting transfers between devices, along_shard(): return lax.ppermute(block, 'shard', route)  15.9 us
    pallas_call x4, Pallas kernels, call(): pl.pallas_call(kernel, out_shape=[jax.ShapeDtypeStruct(shape, dtype) for...  12.2 us
    pmax x1, blocking collectives, local(): return lax.pmax(best[0], 'rep')  6.64 us
    pallas_call x1, Pallas kernels, local(): pl.pallas_call(own_kernel, out_shape=[jax.ShapeDtypeStruct((rows, width),...  6.02 us
    ppermute x6, waiting for transfers between devices, other_rep(): return lax.ppermute(block, 'rep', [(i, i ^ flip) for i in range(reps)])  5.2 us
    ppermute x2, starting transfers between devices, partner(): return lax.ppermute(block, 'shard', [(i, i ^ 1) for i in range(shards)])  4.81 us
    ppermute x6, starting transfers between devices, other_rep(): return lax.ppermute(block, 'rep', [(i, i ^ flip) for i in range(reps)])  3.22 us
  transfers between devices with their start and end apart: 15, of which 7 were waited for; matrix products, arithmetic and copies ran while one was open for 0% of the time, Pallas kernels for 25%

profile of v3, /device:TPU:8, one launch (start us, length us, event | category | flops | bytes accessed | tf_op | source)
XLA Modules:
  0.0 74.2 jit_solution(6229801899794190311)
XLA Ops:
  0.0 0.7 copy-done
  0.7 1.9 %prepare.1 = (bf16[256,1024]{1,0:T(8,128)(2,1)S(1)}, bf16[272,1024]{1,0:T(8,128)(2,1)S(1)}, bf16[528,1024]{1,0:T(8,128)(2,1)S(1)}, bf16[528,1024]{1,0:T(8,128)(2,1)S(1)}) custom-call(bf16[2048,1024]{1,0:T(8,128)(2,1)} %emb_ref.3, s32[16,128]{1,0:T(8,128)S(1)} %bitcast.3), custom_call_target="tpu_custom_call" | custom-call | tf_op jit(solution)/shard_map/prepare/pallas_call | solution.py:281
  2.6 1.6 %collective-permute-start.1 = (bf16[528,1024]{1,0:T(8,128)(2,1)S(1)}, bf16[528,1024]{1,0:T(8,128)(2,1)S(1)}, u32[]{:S(2)}, u32[]{:S(2)}) collective-permute-start(bf16[528,1024]{1,0:T(8,128)(2,1)S(1)} %get-tuple-element.42), channel_id=1, source_target_pairs={{0,4},{4,0},{8,12},{12,8},{16,20},{20,16},{24,28},{28,24},{1,5},{5... | collective-permute-start | bytes 3244040 | tf_op jit(solution)/shard_map/ppermute | solution.py:264
  4.2 2.3 %collective-permute-start.2 = (bf16[528,1024]{1,0:T(8,128)(2,1)S(1)}, bf16[528,1024]{1,0:T(8,128)(2,1)S(1)}, u32[]{:S(2)}, u32[]{:S(2)}) collective-permute-start(bf16[528,1024]{1,0:T(8,128)(2,1)S(1)} %get-tuple-element.43), channel_id=1, source_target_pairs={{8,0},{12,4},{16,8},{20,12},{24,16},{28,20},{9,1},{13,5},{17,9},{2... | collective-permute-start | bytes 3244040 | tf_op jit(solution)/shard_map/ppermute | solution.py:261
  6.5 3.5 %collective-permute-start = (bf16[256,1024]{1,0:T(8,128)(2,1)S(1)}, bf16[256,1024]{1,0:T(8,128)(2,1)S(1)}, u32[]{:S(2)}, u32[]{:S(2)}) collective-permute-start(bf16[256,1024]{1,0:T(8,128)(2,1)S(1)} %get-tuple-element.39), channel_id=1, source_target_pairs={{0,8},{4,12},{8,16},{12,20},{16,24},{20,28},{1,9},{5,13},{9,17},{1... | collective-permute-start | bytes 1572872 | tf_op jit(solution)/shard_map/ppermute | solution.py:261
  10.0 3.5 %collective-permute-start.3 = (bf16[272,1024]{1,0:T(8,128)(2,1)S(1)}, bf16[272,1024]{1,0:T(8,128)(2,1)S(1)}, u32[]{:S(2)}, u32[]{:S(2)}) collective-permute-start(bf16[272,1024]{1,0:T(8,128)(2,1)S(1)} %get-tuple-element.49), channel_id=1, source_target_pairs={{0,8},{4,12},{8,16},{12,20},{16,24},{20,28},{1,9},{5,13},{9,17},{1... | collective-permute-start | bytes 1671176 | tf_op jit(solution)/shard_map/ppermute | solution.py:261
  13.6 9.7 %collective-permute-done.low_0a = bf16[256,1024]{1,0:T(8,128)(2,1)S(1)} collective-permute-done((bf16[256,1024]{1,0:T(8,128)(2,1)S(1)}, bf16[256,1024]{1,0:T(8,128)(2,1)S(1)}, u32[]{:S(2)}, u32[]{:S(2)}) %collective-permute-start) | collective-permute-done | bytes 524320 | tf_op jit(solution)/shard_map/ppermute | solution.py:261
  23.3 1.5 %collective-permute-start.5 = (bf16[256,1024]{1,0:T(8,128)(2,1)S(1)}, bf16[256,1024]{1,0:T(8,128)(2,1)S(1)}, u32[]{:S(2)}, u32[]{:S(2)}) collective-permute-start(bf16[256,1024]{1,0:T(8,128)(2,1)S(1)} %collective-permute-done.low_0a), channel_id=1, source_target_pairs={{0,2},{1,3},{2,0},{3,1},{4,6},{5,7},{6,4},{7,5},{8,10},{9,11},{10,... | collective-permute-start | bytes 1572872 | tf_op jit(solution)/shard_map/ppermute | solution.py:267
  24.8 6.0 %own.1 = (bf16[2048,1024]{1,0:T(8,128)(2,1)S(1)}, f32[1,2048]{1,0:T(1,128)S(1)}, s32[2]{0:T(128)S(1)}) custom-call(bf16[2048,1024]{1,0:T(8,128)(2,1)} %emb_ref.3, s32[1,2048]{1,0:T(1,128)S(1)} %bitcast.4), custom_call_target="tpu_custom_call" | custom-call | flops 1024 | bytes 1024 | tf_op jit(solution)/shard_map/own/pallas_call | solution.py:306
  30.8 0.6 collective-permute-done.2.high
  31.4 2.0 %collective-permute-done.3.low_0b = bf16[272,1024]{1,0:T(8,128)(2,1)S(1)} collective-permute-done((bf16[272,1024]{1,0:T(8,128)(2,1)S(1)}, bf16[272,1024]{1,0:T(8,128)(2,1)S(1)}, u32[]{:S(2)}, u32[]{:S(2)}) %collective-permute-start.3) | collective-permute-done | bytes 557088 | tf_op jit(solution)/shard_map/ppermute | solution.py:261
  33.7 2.6 %collective-permute-start.8 = (bf16[272,1024]{1,0:T(8,128)(2,1)S(1)}, bf16[272,1024]{1,0:T(8,128)(2,1)S(1)}, u32[]{:S(2)}, u32[]{:S(2)}) collective-permute-start(bf16[272,1024]{1,0:T(8,128)(2,1)S(1)} %slice.7), channel_id=1, source_target_pairs={{0,4},{8,12},{16,20},{24,28},{1,5},{9,13},{17,21},{25,29},{2,6},{1... | collective-permute-start | bytes 1671176 | tf_op jit(solution)/shard_map/ppermute | solution.py:261
  36.4 1.4 %collective-permute-start.6 = (bf16[272,1024]{1,0:T(8,128)(2,1)S(1)}, bf16[272,1024]{1,0:T(8,128)(2,1)S(1)}, u32[]{:S(2)}, u32[]{:S(2)}) collective-permute-start(bf16[272,1024]{1,0:T(8,128)(2,1)S(1)} %collective-permute-done.3.low_0b), channel_id=1, source_target_pairs={{0,2},{1,3},{2,0},{3,1},{4,6},{5,7},{6,4},{7,5},{8,10},{9,11},{10,... | collective-permute-start | bytes 1671176 | tf_op jit(solution)/shard_map/ppermute | solution.py:267
  37.8 0.7 collective-permute-start.7
  38.7 7.6 %near.1 = (f32[1,2048]{1,0:T(1,128)S(1)}, f32[1,512]{1,0:T(1,128)S(1)}, f32[1,512]{1,0:T(1,128)S(1)}, s32[6]{0:T(128)S(1)}) custom-call(s32[2]{0:T(128)S(1)} %get-tuple-element.41.own_reach, bf16[2048,1024]{1,0:T(8,128)(2,1)S(1)} %get-tuple-element.46.own_ref, f32[1,2048]{1,0:T(1,128)S(1)} %get-tuple-element.47.best_ref, ...), custom_call_target="tpu_custom_call" | custom-call | flops 1024 | bytes 1024 | tf_op jit(solution)/shard_map/near/pallas_call | solution.py:270
  46.4 5.0 %collective-permute-done.6.low_2b = bf16[272,1024]{1,0:T(8,128)(2,1)S(1)} collective-permute-done((bf16[272,1024]{1,0:T(8,128)(2,1)S(1)}, bf16[272,1024]{1,0:T(8,128)(2,1)S(1)}, u32[]{:S(2)}, u32[]{:S(2)}) %collective-permute-start.6) | collective-permute-done | bytes 557088 | tf_op jit(solution)/shard_map/ppermute | solution.py:267
  51.4 3.4 %far.1 = (f32[1,512]{1,0:T(1,128)S(1)}, f32[1,512]{1,0:T(1,128)S(1)}, f32[1,512]{1,0:T(1,128)S(1)}, s32[2]{0:T(128)S(1)}) custom-call(s32[6]{0:T(128)S(1)} %get-tuple-element.58.reach_ref, f32[1,512]{1,0:T(1,128)S(1)} %get-tuple-element.60.across_ref, f32[1,512]{1,0:T(1,128)S(1)} %get-tuple-element.61.high_ref, ...), custom_call_target="tpu_custom_call" | custom-call | flops 1024 | bytes 1024 | tf_op jit(solution)/shard_map/far/pallas_call | solution.py:270
  54.8 3.2 %collective-permute-start.11 = (f32[1,512]{1,0:T(1,128)S(1)}, f32[1,512]{1,0:T(1,128)S(1)}, u32[]{:S(2)}, u32[]{:S(2)}) collective-permute-start(f32[1,512]{1,0:T(1,128)S(1)} %get-tuple-element.67), channel_id=1, source_target_pairs={{0,4},{4,0},{8,12},{12,8},{16,20},{20,16},{24,28},{28,24},{1,5},{5... | collective-permute-start | bytes 6152 | tf_op jit(solution)/shard_map/ppermute | solution.py:264
  58.0 1.2 %last.1 = (f32[1,512]{1,0:T(1,128)S(1)}, f32[1,512]{1,0:T(1,128)S(1)}) custom-call(s32[6]{0:T(128)S(1)} %get-tuple-element.58.reach_ref, s32[2]{0:T(128)S(1)} %get-tuple-element.68.side_ref, f32[1,512]{1,0:T(1,128)S(1)} %get-tuple-element.69.high_ref, f32[1,512]{1,0:T(1,128)S(1)} %get-tuple-element.70.up_ref, ...), custom_call_target="tpu_custom_call" | custom-call | flops 1024 | bytes 1024 | tf_op jit(solution)/shard_map/last/pallas_call | solution.py:270
  59.2 1.9 %collective-permute-start.13 = (f32[1,512]{1,0:T(1,128)S(1)}, f32[1,512]{1,0:T(1,128)S(1)}, u32[]{:S(2)}, u32[]{:S(2)}) collective-permute-start(f32[1,512]{1,0:T(1,128)S(1)} %get-tuple-element.71), channel_id=1, source_target_pairs={{0,8},{4,12},{8,16},{12,20},{16,24},{20,28},{1,9},{5,13},{9,17},{1... | collective-permute-start | bytes 6152 | tf_op jit(solution)/shard_map/ppermute | solution.py:261
  61.1 1.3 %collective-permute-start.14 = (f32[1,512]{1,0:T(1,128)S(1)}, f32[1,512]{1,0:T(1,128)S(1)}, u32[]{:S(2)}, u32[]{:S(2)}) collective-permute-start(f32[1,512]{1,0:T(1,128)S(1)} %get-tuple-element.72), channel_id=1, source_target_pairs={{4,8},{12,16},{20,24},{5,9},{13,17},{21,25},{6,10},{14,18},{22,26}... | collective-permute-start | bytes 6152 | tf_op jit(solution)/shard_map/ppermute | solution.py:261
  62.4 2.2 %collective-permute-done.13.above_ref = f32[1,512]{1,0:T(1,128)S(1)} collective-permute-done((f32[1,512]{1,0:T(1,128)S(1)}, f32[1,512]{1,0:T(1,128)S(1)}, u32[]{:S(2)}, u32[]{:S(2)}) %collective-permute-start.13) | collective-permute-done | bytes 2080 | tf_op jit(solution)/shard_map/ppermute | solution.py:261
  64.7 2.8 %collective-permute-done.14.beside_ref = f32[1,512]{1,0:T(1,128)S(1)} collective-permute-done((f32[1,512]{1,0:T(1,128)S(1)}, f32[1,512]{1,0:T(1,128)S(1)}, u32[]{:S(2)}, u32[]{:S(2)}) %collective-permute-start.14) | collective-permute-done | bytes 2080 | tf_op jit(solution)/shard_map/ppermute | solution.py:261
  67.5 6.6 %pmax.7 = f32[2048]{0:T(1024)} all-reduce(f32[2048]{0:T(1024)S(1)} %bitcast.5), channel_id=1, replica_groups=mesh['shard'=8,'rep'=4] {'rep'}, use_global_device_ids=true, to_apply=%region_0.0 | all-reduce | flops 2048 | bytes 16384 | tf_op jit(solution)/shard_map/pmax | solution.py:359
  (19 shorter events, 0.7 us)
Async XLA Ops:
  0.0 0.7 copy-start
  0.7 24.1 %copy-start.1 = (s32[2048]{0:T(1024)S(1)}, s32[2048]{0:T(1024)}, u32[]{:S(2)}) copy-start(s32[2048]{0:T(1024)} %param.3) | copy-start | bytes 24580
  2.6 28.2 %collective-permute-start.1 = (bf16[528,1024]{1,0:T(8,128)(2,1)S(1)}, bf16[528,1024]{1,0:T(8,128)(2,1)S(1)}, u32[]{:S(2)}, u32[]{:S(2)}) collective-permute-start(bf16[528,1024]{1,0:T(8,128)(2,1)S(1)} %get-tuple-element.42), channel_id=1, source_target_pairs={{0,4},{4,0},{8,12},{12,8},{16,20},{20,16},{24,28},{28,24},{1,5},{5... | collective-permute-start | bytes 3244040 | tf_op jit(solution)/shard_map/ppermute | solution.py:264
  4.2 27.2 %collective-permute-start.2 = (bf16[528,1024]{1,0:T(8,128)(2,1)S(1)}, bf16[528,1024]{1,0:T(8,128)(2,1)S(1)}, u32[]{:S(2)}, u32[]{:S(2)}) collective-permute-start(bf16[528,1024]{1,0:T(8,128)(2,1)S(1)} %get-tuple-element.43), channel_id=1, source_target_pairs={{8,0},{12,4},{16,8},{20,12},{24,16},{28,20},{9,1},{13,5},{17,9},{2... | collective-permute-start | bytes 3244040 | tf_op jit(solution)/shard_map/ppermute | solution.py:261
  6.5 16.8 %collective-permute-start = (bf16[256,1024]{1,0:T(8,128)(2,1)S(1)}, bf16[256,1024]{1,0:T(8,128)(2,1)S(1)}, u32[]{:S(2)}, u32[]{:S(2)}) collective-permute-start(bf16[256,1024]{1,0:T(8,128)(2,1)S(1)} %get-tuple-element.39), channel_id=1, source_target_pairs={{0,8},{4,12},{8,16},{12,20},{16,24},{20,28},{1,9},{5,13},{9,17},{1... | collective-permute-start | bytes 1572872 | tf_op jit(solution)/shard_map/ppermute | solution.py:261
  10.0 23.4 %collective-permute-start.3 = (bf16[272,1024]{1,0:T(8,128)(2,1)S(1)}, bf16[272,1024]{1,0:T(8,128)(2,1)S(1)}, u32[]{:S(2)}, u32[]{:S(2)}) collective-permute-start(bf16[272,1024]{1,0:T(8,128)(2,1)S(1)} %get-tuple-element.49), channel_id=1, source_target_pairs={{0,8},{4,12},{8,16},{12,20},{16,24},{20,28},{1,9},{5,13},{9,17},{1... | collective-permute-start | bytes 1671176 | tf_op jit(solution)/shard_map/ppermute | solution.py:261
  23.3 10.4 %collective-permute-start.5 = (bf16[256,1024]{1,0:T(8,128)(2,1)S(1)}, bf16[256,1024]{1,0:T(8,128)(2,1)S(1)}, u32[]{:S(2)}, u32[]{:S(2)}) collective-permute-start(bf16[256,1024]{1,0:T(8,128)(2,1)S(1)} %collective-permute-done.low_0a), channel_id=1, source_target_pairs={{0,2},{1,3},{2,0},{3,1},{4,6},{5,7},{6,4},{7,5},{8,10},{9,11},{10,... | collective-permute-start | bytes 1572872 | tf_op jit(solution)/shard_map/ppermute | solution.py:267
  24.8 8.9 %collective-permute-start.4 = (bf16[256,1024]{1,0:T(8,128)(2,1)S(1)}, bf16[256,1024]{1,0:T(8,128)(2,1)S(1)}, u32[]{:S(2)}, u32[]{:S(2)}) collective-permute-start(bf16[256,1024]{1,0:T(8,128)(2,1)S(1)} %collective-permute-done.low_0a), channel_id=1, source_target_pairs={{0,1},{1,0},{2,3},{3,2},{4,5},{5,4},{6,7},{7,6},{8,9},{9,8},{10,11... | collective-permute-start | bytes 1572872 | tf_op jit(solution)/shard_map/ppermute | solution.py:267
  33.7 12.7 %collective-permute-start.8 = (bf16[272,1024]{1,0:T(8,128)(2,1)S(1)}, bf16[272,1024]{1,0:T(8,128)(2,1)S(1)}, u32[]{:S(2)}, u32[]{:S(2)}) collective-permute-start(bf16[272,1024]{1,0:T(8,128)(2,1)S(1)} %slice.7), channel_id=1, source_target_pairs={{0,4},{8,12},{16,20},{24,28},{1,5},{9,13},{17,21},{25,29},{2,6},{1... | collective-permute-start | bytes 1671176 | tf_op jit(solution)/shard_map/ppermute | solution.py:261
  36.3 10.2 %collective-permute-start.9 = (bf16[272,1024]{1,0:T(8,128)(2,1)S(1)}, bf16[272,1024]{1,0:T(8,128)(2,1)S(1)}, u32[]{:S(2)}, u32[]{:S(2)}) collective-permute-start(bf16[272,1024]{1,0:T(8,128)(2,1)S(1)} %collective-permute-done.3.low_0b), channel_id=1, source_target_pairs={{0,1},{1,0},{2,3},{3,2},{4,5},{5,4},{6,7},{7,6},{8,9},{9,8},{10,11... | collective-permute-start | bytes 1671176 | tf_op jit(solution)/shard_map/ppermute | solution.py:267
  36.4 15.0 %collective-permute-start.6 = (bf16[272,1024]{1,0:T(8,128)(2,1)S(1)}, bf16[272,1024]{1,0:T(8,128)(2,1)S(1)}, u32[]{:S(2)}, u32[]{:S(2)}) collective-permute-start(bf16[272,1024]{1,0:T(8,128)(2,1)S(1)} %collective-permute-done.3.low_0b), channel_id=1, source_target_pairs={{0,2},{1,3},{2,0},{3,1},{4,6},{5,7},{6,4},{7,5},{8,10},{9,11},{10,... | collective-permute-start | bytes 1671176 | tf_op jit(solution)/shard_map/ppermute | solution.py:267
  37.8 8.6 %collective-permute-start.7 = (bf16[256,1024]{1,0:T(8,128)(2,1)S(1)}, bf16[256,1024]{1,0:T(8,128)(2,1)S(1)}, u32[]{:S(2)}, u32[]{:S(2)}) collective-permute-start(bf16[256,1024]{1,0:T(8,128)(2,1)S(1)} %slice.6), channel_id=1, source_target_pairs={{12,4},{20,12},{28,20},{13,5},{21,13},{29,21},{14,6},{22,14},{30,2... | collective-permute-start | bytes 1572872 | tf_op jit(solution)/shard_map/ppermute | solution.py:261
  38.5 7.9 %collective-permute-start.10 = (bf16[256,1024]{1,0:T(8,128)(2,1)S(1)}, bf16[256,1024]{1,0:T(8,128)(2,1)S(1)}, u32[]{:S(2)}, u32[]{:S(2)}) collective-permute-start(bf16[256,1024]{1,0:T(8,128)(2,1)S(1)} %collective-permute-done.5.low_2a), channel_id=1, source_target_pairs={{0,1},{1,0},{2,3},{3,2},{4,5},{5,4},{6,7},{7,6},{8,9},{9,8},{10,11... | collective-permute-start | bytes 1572872 | tf_op jit(solution)/shard_map/ppermute | solution.py:267
  51.4 6.6 %collective-permute-start.12 = (bf16[272,1024]{1,0:T(8,128)(2,1)S(1)}, bf16[272,1024]{1,0:T(8,128)(2,1)S(1)}, u32[]{:S(2)}, u32[]{:S(2)}) collective-permute-start(bf16[272,1024]{1,0:T(8,128)(2,1)S(1)} %collective-permute-done.6.low_2b), channel_id=1, source_target_pairs={{0,1},{1,0},{2,3},{3,2},{4,5},{5,4},{6,7},{7,6},{8,9},{9,8},{10,11... | collective-permute-start | bytes 1671176 | tf_op jit(solution)/shard_map/ppermute | solution.py:267
  54.8 7.6 %collective-permute-start.11 = (f32[1,512]{1,0:T(1,128)S(1)}, f32[1,512]{1,0:T(1,128)S(1)}, u32[]{:S(2)}, u32[]{:S(2)}) collective-permute-start(f32[1,512]{1,0:T(1,128)S(1)} %get-tuple-element.67), channel_id=1, source_target_pairs={{0,4},{4,0},{8,12},{12,8},{16,20},{20,16},{24,28},{28,24},{1,5},{5... | collective-permute-start | bytes 6152 | tf_op jit(solution)/shard_map/ppermute | solution.py:264
  59.2 5.5 %collective-permute-start.13 = (f32[1,512]{1,0:T(1,128)S(1)}, f32[1,512]{1,0:T(1,128)S(1)}, u32[]{:S(2)}, u32[]{:S(2)}) collective-permute-start(f32[1,512]{1,0:T(1,128)S(1)} %get-tuple-element.71), channel_id=1, source_target_pairs={{0,8},{4,12},{8,16},{12,20},{16,24},{20,28},{1,9},{5,13},{9,17},{1... | collective-permute-start | bytes 6152 | tf_op jit(solution)/shard_map/ppermute | solution.py:261
  61.1 6.4 %collective-permute-start.14 = (f32[1,512]{1,0:T(1,128)S(1)}, f32[1,512]{1,0:T(1,128)S(1)}, u32[]{:S(2)}, u32[]{:S(2)}) collective-permute-start(f32[1,512]{1,0:T(1,128)S(1)} %get-tuple-element.72), channel_id=1, source_target_pairs={{4,8},{12,16},{20,24},{5,9},{13,17},{21,25},{6,10},{14,18},{22,26}... | collective-permute-start | bytes 6152 | tf_op jit(solution)/shard_map/ppermute | solution.py:261

commit v4 on v2

--- a/solution.py
+++ b/solution.py
@@ -228,22 +228,28 @@
     group(lows, up_b, half, up_out, half, reached(side, low, rep * quarter + half, half))
 
 
-def merge_kernel(best_ref, partner_ref, above_ref, beside_ref, out_ref):
-    quarter = above_ref.shape[1]
+def merge_kernel(best_ref, across_ref, high_ref, up_ref, out_ref):
+    rows, quarter = best_ref.shape[1], high_ref.shape[1]
     half = quarter // 2
-    rep, odd, _ = position()
-    inside = lax.axis_index("shard") >= 2
-    out_ref[...] = best_ref[...]
-
-    def raised(at, values):
-        cols = pl.ds(pl.multiple_of(at, half), values.shape[1])
-        out_ref[:, cols] = jnp.maximum(out_ref[:, cols], values)
-
-    raised((rep ^ (2 - odd)) * quarter, partner_ref[...])
-    raised(rep * quarter, jnp.where(inside, above_ref[...], -1.0))
-    beside = jnp.where(inside & (odd == 0), beside_ref[...], -1.0)
-    raised((rep ^ 2) * quarter, beside[:, :half])
-    raised(rep * quarter + half, beside[:, half:])
+    shards = out_ref.shape[1] // rows
+    rep, odd, part = position()
+    shard = lax.axis_index("shard")
+    out_ref[...] = jnp.full(out_ref.shape, -1.0, F32)
+
+    def put(at, values):
+        out_ref[:, pl.ds(pl.multiple_of(at, half), values.shape[1])] = values
+
+    put(shard * rows, best_ref[...])
+    put((shard ^ 1) * rows + part * quarter, across_ref[...])
+
+    @pl.when(shard + 2 < shards)
+    def _():
+        put((shard + 2) * rows + rep * quarter, high_ref[...])
+
+    @pl.when((odd == 1) & (shard + 1 < shards))
+    def _():
+        put((shard + 1) * rows + (rep ^ 2) * quarter, up_ref[:, :half])
+        put((shard + 1) * rows + rep * quarter + half, up_ref[:, half:])
 
 
 def local(embeddings, labels):
@@ -348,13 +354,11 @@
         reach, side, of_high, of_up, low_3b, high, up_a, up_b,
     )
 
-    above = along_shard(of_high, 2)
-    beside = along_shard(of_up, 1, odd_only)
-    from_partner = partner(of_across)
     (best,) = call(
-        merge_kernel, "merge", [((1, rows), F32)], [VMEM] * 5, best, from_partner, above, beside
-    )
-    return lax.pmax(best[0], "rep")
+        merge_kernel, "merge", [((1, shards * rows), F32)], [VMEM] * 5, best, of_across, of_high, of_up
+    )
+    best = lax.pmax(best[0], ("shard", "rep"))
+    return lax.dynamic_slice_in_dim(best, lax.axis_index("shard") * rows, rows, 0)
 
 
 def solution(mesh):

time: 74.4 us -> 194 us (2.61); the launches traced: 75.6 us -> 191 us
  waiting for transfers between devices: 28.1 us -> 146 us
  between operations: 0.16 us -> 13.5 us
  starting transfers between devices: 28.2 us -> 17.5 us
  blocking collectives: 6.44 us -> 0 us
    pmax x0 -> x1, waiting for transfers between devices: none -> 122 us  [local(): best = lax.pmax(best[0], ('shard', 'rep'))]
    ppermute x7 -> x5, starting transfers between devices: 20.8 us -> 12.6 us  [along_shard(): return lax.ppermute(block, 'shard', route)]
    pmax x1 -> x0, blocking collectives: 6.44 us -> none  [local(): return lax.pmax(best[0], 'rep')]
    ppermute x7 -> x5, waiting for transfers between devices: 22.9 us -> 17.8 us  [along_shard(): return lax.ppermute(block, 'shard', route)]
    ppermute x2 -> x1, starting transfers between devices: 4.18 us -> 1.58 us  [partner(): return lax.ppermute(block, 'shard', [(i, i ^ 1) for i in range(shards)])]
  transfers between devices with their start and end apart: 15 -> 13, of which waited for: 7 -> 8; matrix products, arithmetic and copies ran while one was open for 0% -> 0% of each run, Pallas kernels for 13% -> 5%
where the time goes in v4:
time: 194 us; the launch traced here: 191 us
  waiting for transfers between devices  146 us (75%)
  starting transfers between devices  17.5 us (9%)
  between operations  13.5 us (7%)
  Pallas kernels  12.6 us (6%)
  local copies, waits for them, and re-layouts  2.07 us (1%)
    pmax x1, waiting for transfers between devices, local(): best = lax.pmax(best[0], ('shard', 'rep'))  122 us
    ppermute x5, waiting for transfers between devices, along_shard(): return lax.ppermute(block, 'shard', route)  17.8 us
    ppermute x5, starting transfers between devices, along_shard(): return lax.ppermute(block, 'shard', route)  12.6 us
    pallas_call x1, Pallas kernels, local(): pl.pallas_call(own_kernel, out_shape=[jax.ShapeDtypeStruct((rows, width),...  6.02 us
    ppermute x6, waiting for transfers between devices, other_rep(): return lax.ppermute(block, 'rep', [(i, i ^ flip) for i in range(reps)])  5.89 us
    pallas_call x4, Pallas kernels, call(): pl.pallas_call(kernel, out_shape=[jax.ShapeDtypeStruct(shape, dtype) for...  4.66 us
  transfers between devices with their start and end apart: 13, of which 8 were waited for; matrix products, arithmetic and copies ran while one was open for 0% of the time, Pallas kernels for 5%

profile of v4, /device:TPU:8, one launch (start us, length us, event | category | flops | bytes accessed | tf_op | source)
XLA Modules:
  0.0 191.1 jit_solution(13582209542963908095)
XLA Ops:
  6.5 0.7 copy-done
  7.2 1.9 prepare.1
  9.1 1.6 collective-permute-start.1
  10.7 2.3 %collective-permute-start.2 = (bf16[528,1024]{1,0:T(8,128)(2,1)S(1)}, bf16[528,1024]{1,0:T(8,128)(2,1)S(1)}, u32[]{:S(2)}, u32[]{:S(2)}) collective-permute-start(bf16[528,1024]{1,0:T(8,128)(2,1)S(1)} %get-tuple-element.43), channel_id=1, source_target_pairs={{8,0},{12,4},{16,8},{20,12},{24,16},{28,20},{9,1},{13,5},{17,9},{2... | collective-permute-start | bytes 3244040 | tf_op jit(solution)/shard_map/ppermute | solution.py:265
  13.1 3.5 %collective-permute-start = (bf16[256,1024]{1,0:T(8,128)(2,1)S(1)}, bf16[256,1024]{1,0:T(8,128)(2,1)S(1)}, u32[]{:S(2)}, u32[]{:S(2)}) collective-permute-start(bf16[256,1024]{1,0:T(8,128)(2,1)S(1)} %get-tuple-element.39), channel_id=1, source_target_pairs={{0,8},{4,12},{8,16},{12,20},{16,24},{20,28},{1,9},{5,13},{9,17},{1... | collective-permute-start | bytes 1572872 | tf_op jit(solution)/shard_map/ppermute | solution.py:265
  16.5 3.5 %collective-permute-start.3 = (bf16[272,1024]{1,0:T(8,128)(2,1)S(1)}, bf16[272,1024]{1,0:T(8,128)(2,1)S(1)}, u32[]{:S(2)}, u32[]{:S(2)}) collective-permute-start(bf16[272,1024]{1,0:T(8,128)(2,1)S(1)} %get-tuple-element.49), channel_id=1, source_target_pairs={{0,8},{4,12},{8,16},{12,20},{16,24},{20,28},{1,9},{5,13},{9,17},{1... | collective-permute-start | bytes 1671176 | tf_op jit(solution)/shard_map/ppermute | solution.py:265
  20.1 9.7 %collective-permute-done.low_0a = bf16[256,1024]{1,0:T(8,128)(2,1)S(1)} collective-permute-done((bf16[256,1024]{1,0:T(8,128)(2,1)S(1)}, bf16[256,1024]{1,0:T(8,128)(2,1)S(1)}, u32[]{:S(2)}, u32[]{:S(2)}) %collective-permute-start) | collective-permute-done | bytes 524320 | tf_op jit(solution)/shard_map/ppermute | solution.py:265
  29.8 1.5 collective-permute-start.5
  31.3 6.0 %own.1 = (bf16[2048,1024]{1,0:T(8,128)(2,1)S(1)}, f32[1,2048]{1,0:T(1,128)S(1)}, s32[2]{0:T(128)S(1)}) custom-call(bf16[2048,1024]{1,0:T(8,128)(2,1)} %emb_ref.3, s32[1,2048]{1,0:T(1,128)S(1)} %bitcast.4), custom_call_target="tpu_custom_call" | custom-call | flops 1024 | bytes 1024 | tf_op jit(solution)/shard_map/own/pallas_call | solution.py:310
  37.4 0.6 collective-permute-done.2.high
  37.9 2.0 %collective-permute-done.3.low_0b = bf16[272,1024]{1,0:T(8,128)(2,1)S(1)} collective-permute-done((bf16[272,1024]{1,0:T(8,128)(2,1)S(1)}, bf16[272,1024]{1,0:T(8,128)(2,1)S(1)}, u32[]{:S(2)}, u32[]{:S(2)}) %collective-permute-start.3) | collective-permute-done | bytes 557088 | tf_op jit(solution)/shard_map/ppermute | solution.py:265
  40.0 0.2 collective-permute-done.5.low_2a
  40.2 2.6 %collective-permute-start.8 = (bf16[272,1024]{1,0:T(8,128)(2,1)S(1)}, bf16[272,1024]{1,0:T(8,128)(2,1)S(1)}, u32[]{:S(2)}, u32[]{:S(2)}) collective-permute-start(bf16[272,1024]{1,0:T(8,128)(2,1)S(1)} %slice.7), channel_id=1, source_target_pairs={{0,4},{8,12},{16,20},{24,28},{1,5},{9,13},{17,21},{25,29},{2,6},{1... | collective-permute-start | bytes 1671176 | tf_op jit(solution)/shard_map/ppermute | solution.py:265
  42.9 1.4 collective-permute-start.6
  44.4 0.7 collective-permute-start.7
  45.3 2.1 %near.1 = (f32[1,2048]{1,0:T(1,128)S(1)}, f32[1,512]{1,0:T(1,128)S(1)}, f32[1,512]{1,0:T(1,128)S(1)}, s32[6]{0:T(128)S(1)}) custom-call(s32[2]{0:T(128)S(1)} %get-tuple-element.41.own_reach, bf16[2048,1024]{1,0:T(8,128)(2,1)S(1)} %get-tuple-element.46.own_ref, f32[1,2048]{1,0:T(1,128)S(1)} %get-tuple-element.47.best_ref, ...), custom_call_target="tpu_custom_call" | custom-call | flops 1024 | bytes 1024 | tf_op jit(solution)/shard_map/near/pallas_call | solution.py:274
  47.4 5.5 %collective-permute-done.8.up_b = bf16[272,1024]{1,0:T(8,128)(2,1)S(1)} collective-permute-done((bf16[272,1024]{1,0:T(8,128)(2,1)S(1)}, bf16[272,1024]{1,0:T(8,128)(2,1)S(1)}, u32[]{:S(2)}, u32[]{:S(2)}) %collective-permute-start.8) | collective-permute-done | bytes 557088 | tf_op jit(solution)/shard_map/ppermute | solution.py:265
  52.9 5.0 %collective-permute-done.6.low_2b = bf16[272,1024]{1,0:T(8,128)(2,1)S(1)} collective-permute-done((bf16[272,1024]{1,0:T(8,128)(2,1)S(1)}, bf16[272,1024]{1,0:T(8,128)(2,1)S(1)}, u32[]{:S(2)}, u32[]{:S(2)}) %collective-permute-start.6) | collective-permute-done | bytes 557088 | tf_op jit(solution)/shard_map/ppermute | solution.py:271
  57.9 1.3 far.1
  59.3 0.6 collective-permute-done.11.low_3b
  59.9 0.6 last.1
  60.5 0.6 merge.1
  61.2 121.8 %all-reduce.2.cloned.1.call-done = f32[16384]{0:T(1024)} async-done(((f32[16384]{0:T(1024)}), f32[16384]{0:T(1024)}) %all-reduce.2.cloned.1.call-update) | async-done | bytes 65552 | tf_op jit(solution)/shard_map/pmax | solution.py:360
  183.0 1.3 dynamic_slice.3
  (16 shorter events, 0.4 us)
Async XLA Ops:
  6.5 176.5 %all-reduce.2.cloned.1.call-start = ((), (), s32[]{:S(2)}) async-start(), calls=%async_computation | async-start | bytes 131072 | tf_op jit(solution)/shard_map/pmax | solution.py:360
  6.5 0.7 copy-start
  7.2 24.1 %copy-start.1 = (s32[2048]{0:T(1024)S(1)}, s32[2048]{0:T(1024)}, u32[]{:S(2)}) copy-start(s32[2048]{0:T(1024)} %param.3) | copy-start | bytes 24580
  9.1 28.2 %collective-permute-start.1 = (bf16[528,1024]{1,0:T(8,128)(2,1)S(1)}, bf16[528,1024]{1,0:T(8,128)(2,1)S(1)}, u32[]{:S(2)}, u32[]{:S(2)}) collective-permute-start(bf16[528,1024]{1,0:T(8,128)(2,1)S(1)} %get-tuple-element.42), channel_id=1, source_target_pairs={{0,4},{4,0},{8,12},{12,8},{16,20},{20,16},{24,28},{28,24},{1,5},{5... | collective-permute-start | bytes 3244040 | tf_op jit(solution)/shard_map/ppermute | solution.py:268
  10.7 27.2 %collective-permute-start.2 = (bf16[528,1024]{1,0:T(8,128)(2,1)S(1)}, bf16[528,1024]{1,0:T(8,128)(2,1)S(1)}, u32[]{:S(2)}, u32[]{:S(2)}) collective-permute-start(bf16[528,1024]{1,0:T(8,128)(2,1)S(1)} %get-tuple-element.43), channel_id=1, source_target_pairs={{8,0},{12,4},{16,8},{20,12},{24,16},{28,20},{9,1},{13,5},{17,9},{2... | collective-permute-start | bytes 3244040 | tf_op jit(solution)/shard_map/ppermute | solution.py:265
  13.1 16.8 %collective-permute-start = (bf16[256,1024]{1,0:T(8,128)(2,1)S(1)}, bf16[256,1024]{1,0:T(8,128)(2,1)S(1)}, u32[]{:S(2)}, u32[]{:S(2)}) collective-permute-start(bf16[256,1024]{1,0:T(8,128)(2,1)S(1)} %get-tuple-element.39), channel_id=1, source_target_pairs={{0,8},{4,12},{8,16},{12,20},{16,24},{20,28},{1,9},{5,13},{9,17},{1... | collective-permute-start | bytes 1572872 | tf_op jit(solution)/shard_map/ppermute | solution.py:265
  16.5 23.4 %collective-permute-start.3 = (bf16[272,1024]{1,0:T(8,128)(2,1)S(1)}, bf16[272,1024]{1,0:T(8,128)(2,1)S(1)}, u32[]{:S(2)}, u32[]{:S(2)}) collective-permute-start(bf16[272,1024]{1,0:T(8,128)(2,1)S(1)} %get-tuple-element.49), channel_id=1, source_target_pairs={{0,8},{4,12},{8,16},{12,20},{16,24},{20,28},{1,9},{5,13},{9,17},{1... | collective-permute-start | bytes 1671176 | tf_op jit(solution)/shard_map/ppermute | solution.py:265
  29.8 10.4 %collective-permute-start.5 = (bf16[256,1024]{1,0:T(8,128)(2,1)S(1)}, bf16[256,1024]{1,0:T(8,128)(2,1)S(1)}, u32[]{:S(2)}, u32[]{:S(2)}) collective-permute-start(bf16[256,1024]{1,0:T(8,128)(2,1)S(1)} %collective-permute-done.low_0a), channel_id=1, source_target_pairs={{0,2},{1,3},{2,0},{3,1},{4,6},{5,7},{6,4},{7,5},{8,10},{9,11},{10,... | collective-permute-start | bytes 1572872 | tf_op jit(solution)/shard_map/ppermute | solution.py:271
  31.3 8.9 %collective-permute-start.4 = (bf16[256,1024]{1,0:T(8,128)(2,1)S(1)}, bf16[256,1024]{1,0:T(8,128)(2,1)S(1)}, u32[]{:S(2)}, u32[]{:S(2)}) collective-permute-start(bf16[256,1024]{1,0:T(8,128)(2,1)S(1)} %collective-permute-done.low_0a), channel_id=1, source_target_pairs={{0,1},{1,0},{2,3},{3,2},{4,5},{5,4},{6,7},{7,6},{8,9},{9,8},{10,11... | collective-permute-start | bytes 1572872 | tf_op jit(solution)/shard_map/ppermute | solution.py:271
  40.2 12.7 %collective-permute-start.8 = (bf16[272,1024]{1,0:T(8,128)(2,1)S(1)}, bf16[272,1024]{1,0:T(8,128)(2,1)S(1)}, u32[]{:S(2)}, u32[]{:S(2)}) collective-permute-start(bf16[272,1024]{1,0:T(8,128)(2,1)S(1)} %slice.7), channel_id=1, source_target_pairs={{0,4},{8,12},{16,20},{24,28},{1,5},{9,13},{17,21},{25,29},{2,6},{1... | collective-permute-start | bytes 1671176 | tf_op jit(solution)/shard_map/ppermute | solution.py:265
  42.8 10.1 %collective-permute-start.9 = (bf16[272,1024]{1,0:T(8,128)(2,1)S(1)}, bf16[272,1024]{1,0:T(8,128)(2,1)S(1)}, u32[]{:S(2)}, u32[]{:S(2)}) collective-permute-start(bf16[272,1024]{1,0:T(8,128)(2,1)S(1)} %collective-permute-done.3.low_0b), channel_id=1, source_target_pairs={{0,1},{1,0},{2,3},{3,2},{4,5},{5,4},{6,7},{7,6},{8,9},{9,8},{10,11... | collective-permute-start | bytes 1671176 | tf_op jit(solution)/shard_map/ppermute | solution.py:271
  42.9 15.0 %collective-permute-start.6 = (bf16[272,1024]{1,0:T(8,128)(2,1)S(1)}, bf16[272,1024]{1,0:T(8,128)(2,1)S(1)}, u32[]{:S(2)}, u32[]{:S(2)}) collective-permute-start(bf16[272,1024]{1,0:T(8,128)(2,1)S(1)} %collective-permute-done.3.low_0b), channel_id=1, source_target_pairs={{0,2},{1,3},{2,0},{3,1},{4,6},{5,7},{6,4},{7,5},{8,10},{9,11},{10,... | collective-permute-start | bytes 1671176 | tf_op jit(solution)/shard_map/ppermute | solution.py:271
  44.4 3.1 %collective-permute-start.7 = (bf16[256,1024]{1,0:T(8,128)(2,1)S(1)}, bf16[256,1024]{1,0:T(8,128)(2,1)S(1)}, u32[]{:S(2)}, u32[]{:S(2)}) collective-permute-start(bf16[256,1024]{1,0:T(8,128)(2,1)S(1)} %slice.6), channel_id=1, source_target_pairs={{12,4},{20,12},{28,20},{13,5},{21,13},{29,21},{14,6},{22,14},{30,2... | collective-permute-start | bytes 1572872 | tf_op jit(solution)/shard_map/ppermute | solution.py:265
  45.1 2.4 %collective-permute-start.10 = (bf16[256,1024]{1,0:T(8,128)(2,1)S(1)}, bf16[256,1024]{1,0:T(8,128)(2,1)S(1)}, u32[]{:S(2)}, u32[]{:S(2)}) collective-permute-start(bf16[256,1024]{1,0:T(8,128)(2,1)S(1)} %collective-permute-done.5.low_2a), channel_id=1, source_target_pairs={{0,1},{1,0},{2,3},{3,2},{4,5},{5,4},{6,7},{7,6},{8,9},{9,8},{10,11... | collective-permute-start | bytes 1572872 | tf_op jit(solution)/shard_map/ppermute | solution.py:271
  57.9 2.0 %collective-permute-start.11 = (bf16[272,1024]{1,0:T(8,128)(2,1)S(1)}, bf16[272,1024]{1,0:T(8,128)(2,1)S(1)}, u32[]{:S(2)}, u32[]{:S(2)}) collective-permute-start(bf16[272,1024]{1,0:T(8,128)(2,1)S(1)} %collective-permute-done.6.low_2b), channel_id=1, source_target_pairs={{0,1},{1,0},{2,3},{3,2},{4,5},{5,4},{6,7},{7,6},{8,9},{9,8},{10,11... | collective-permute-start | bytes 1671176 | tf_op jit(solution)/shard_map/ppermute | solution.py:271
Sparse Core Ops, SparseCore 0:
  61.3 121.6 all-reduce.1

commit v5 on v2

v5 whole, which is shorter than its diff:
```python
import functools
import math

import jax
import jax.numpy as jnp
from jax import lax
from jax.experimental import pallas as pl
from jax.experimental.pallas import tpu as pltpu
from jax.sharding import PartitionSpec as P

F32 = jnp.float32
BF16 = jnp.bfloat16
TILE = 256
WIDE = 512
INFO = 16
VMEM_LIMIT = 32 * 1024 * 1024
OWN_LIMIT = 46 * 1024 * 1024
PREPARE_LIMIT = 50 * 1024 * 1024
VMEM = pl.BlockSpec(memory_space=pltpu.VMEM)
SMEM = pl.BlockSpec(memory_space=pltpu.SMEM)


def normalize(values):
    as_float = values.astype(F32)
    width = values.shape[1]
    inverse = lax.rsqrt(jnp.sum(as_float * as_float, axis=1, keepdims=True) * (1 / width) + 1e-06)
    return (as_float * (inverse * (1 / math.sqrt(width)))).astype(BF16)


def score(keys, queries):
    return lax.dot_general(keys, queries, (((1,), (1,)), ((), ())), preferred_element_type=F32)


def fold(values):
    rows, cols = values.shape
    return jnp.max(values.reshape(rows // 8, 8, cols), axis=0)


def prepare_kernel(emb_ref, labels_hbm, lo_out, hi_out, mine_out, raw, labels_ref, sems):
    rep = lax.axis_index("rep")
    quarter = mine_out.shape[0] - INFO
    part = quarter // 2
    copies = []
    for n in range(2):
        at = pl.multiple_of(rep * quarter + n * part, part)
        copies.append(pltpu.make_async_copy(emb_ref.at[pl.ds(at, part), :], raw.at[n], sems.at[n]))
        copies[-1].start()
    fetch = pltpu.make_async_copy(labels_hbm, labels_ref, sems.at[2])
    fetch.start()
    fetch.wait()
    labels = labels_ref[...]
    first, last = jnp.min(labels), jnp.max(labels)
    head = jnp.sum((labels == first).astype(jnp.int32))
    tail = jnp.sum((labels == last).astype(jnp.int32))
    row = lax.broadcasted_iota(jnp.int32, (INFO, mine_out.shape[1]), 0)
    info = jnp.zeros(row.shape, jnp.int32)
    for n, value in enumerate([first, head // 16, head % 16, last, tail // 16, tail % 16]):
        info = jnp.where(row == n, value, info)
    info = info.astype(F32).astype(BF16)
    for n, copy in enumerate(copies):
        copy.wait()
        for m in range(part // 128):
            rows = pl.ds(m * 128, 128)
            values = normalize(raw[n, rows, :])
            mine_out[pl.ds(n * part + m * 128, 128), :] = values
            (lo_out, hi_out)[n][rows, :] = values
    hi_out[pl.ds(part, INFO), :] = info
    mine_out[pl.ds(quarter, INFO), :] = info


def read_reach(ref, at):
    block = ref[pl.ds(ref.shape[0] - INFO, INFO), pl.ds(0, 128)].astype(F32)
    packed = block[at : at + 1] + 256.0 * (16.0 * block[at + 1 : at + 2] + block[at + 2 : at + 3])
    packed = jnp.max(packed).astype(jnp.int32)
    return packed % 256, packed // 256


def group(keys, queries_ref, query_rows, out_ref, out_at, count):
    step = min(WIDE, query_rows)

    def over_queries(j, _):
        at = pl.multiple_of(j * step, step)
        queries = queries_ref[pl.ds(at, step), :]
        best = None
        for ref, row, rows, first in keys:
            scores = score(ref[pl.ds(row, rows), :], queries)
            index = lax.broadcasted_iota(jnp.int32, scores.shape, 0)
            top = fold(jnp.where(index >= first, scores, -1.0))
            best = top if best is None else jnp.maximum(best, top)
        best = jnp.max(best, axis=0, keepdims=True)
        col = lax.broadcasted_iota(jnp.int32, best.shape, 1) + at
        cols = pl.ds(pl.multiple_of(out_at + at, TILE), step)
        out_ref[:, cols] = jnp.maximum(out_ref[:, cols], jnp.where(col < count, best, -1.0))
        return 0

    lax.fori_loop(0, (count + step - 1) // step, over_queries, 0)


def own_kernel(emb_ref, labels_ref, own_out, best_out, reach_out, start, raw, sems):
    rows = emb_ref.shape[0]
    rep = lax.axis_index("rep")
    parts = raw.shape[0]
    size = rows // parts
    copies = [
        pltpu.make_async_copy(emb_ref.at[pl.ds(n * size, size), :], raw.at[n], sems.at[n])
        for n in range(parts)
    ]
    for copy in copies:
        copy.start()
    labels = jnp.broadcast_to(labels_ref[...], start.shape)
    first = jnp.min(labels)
    reach_out[0] = first
    reach_out[1] = jnp.sum((labels == first).astype(jnp.int32)) // start.shape[0]
    lane = lax.broadcasted_iota(jnp.int32, labels.shape, 1)
    begin = jnp.where((lane == 0) | (labels != pltpu.roll(labels, 1, 1)), lane, 0)
    shift = 1
    while shift < rows:
        begin = jnp.maximum(begin, jnp.where(lane >= shift, pltpu.roll(begin, shift, 1), 0))
        shift *= 2
    start[...] = begin
    best_out[...] = jnp.full(best_out.shape, -1.0, F32)
    for n, copy in enumerate(copies):
        copy.wait()
        for m in range(size // 128):
            values = normalize(raw[n, pl.ds(m * 128, 128), :])
            own_out[pl.ds(n * size + m * 128, 128), :] = values
    for n in range(2):
        tile = rep if n == 0 else rows // TILE - 1 - rep
        at = pl.multiple_of(tile * TILE, TILE)
        keys = own_out[pl.ds(at, TILE), :]

        def over_queries(j, _):
            cols = pl.ds(pl.multiple_of(j * WIDE, WIDE), WIDE)
            scores = score(keys, own_out[cols, :])
            row = lax.broadcasted_iota(jnp.int32, scores.shape, 0) + at
            col = lax.broadcasted_iota(jnp.int32, scores.shape, 1) + j * WIDE
            keep = (row >= start[0:1, cols]) & (row < col)
            best = jnp.max(fold(jnp.where(keep, scores, -1.0)), axis=0, keepdims=True)
            best_out[:, cols] = jnp.maximum(best_out[:, cols], best)
            return 0

        lax.fori_loop(at // WIDE, rows // WIDE, over_queries, 0)


def reached(query, key, offset, limit):
    count = jnp.clip(query[1] - offset, 0, limit)
    return jnp.where(query[0] == key[0], count, 0)


def key_piece(ref, tail, rows, at, size):
    return (ref, 0, size, jnp.clip(rows - tail - at, 0, size))


def upper(pieces, keys, up, rep, out_ref, enabled=True):
    half = TILE
    for ref, flip, part in pieces:
        at = (rep ^ flip) * 2 * half + part * half
        for last, several in keys:
            count = jnp.where(enabled, reached(up, last, at, half), 0)
            group(several, ref, half, out_ref, at, count)


def near_kernel(own_reach, own_ref, best_ref, low, across, high_0a, high_0b, high_1a, high_2a,
                best_out, high_out, reach_out):
    rows = own_ref.shape[0]
    quarter = across.shape[0] - INFO
    rep, odd = lax.axis_index("rep"), lax.axis_index("shard") % 2
    mine = (own_reach[0], own_reach[1])
    lower, beside, up = read_reach(low, 3), read_reach(across, 3), read_reach(high_0b, 0)
    for n, value in enumerate(lower + beside + up):
        reach_out[n] = value
    best_out[...] = best_ref[...]
    high_out[...] = jnp.full(high_out.shape, -1.0, F32)
    lows = [key_piece(low, lower[1], rows, rep * quarter, quarter)]
    besides = [key_piece(across, beside[1], rows, rep * quarter, quarter)]
    group(lows, own_ref, rows, best_out, 0, reached(mine, lower, 0, rows))
    count = jnp.where(odd == 1, reached(mine, beside, 0, rows), 0)
    group(besides, own_ref, rows, best_out, 0, count)
    pieces = [(high_0a, 0, 0), (high_0b, 0, 1), (high_1a, 1, 0), (high_2a, 2, 0)]
    upper(pieces, [(beside, besides), (lower, lows)], up, rep, high_out)


def far_parts(reach_ref, side, low, across, side_a, side_b):
    half = TILE
    quarter, rows = 2 * half, 8 * half
    rep, odd = lax.axis_index("rep"), lax.axis_index("shard") % 2
    lower, beside, up = [(reach_ref[2 * n], reach_ref[2 * n + 1]) for n in range(3)]
    at = rep * quarter
    both = [
        (beside, [key_piece(across, beside[1], rows, at, quarter)]),
        (lower, [key_piece(low, lower[1], rows, at, quarter)]),
    ]
    sides = [
        key_piece(side_a, side[1], rows, at + half, half),
        key_piece(side_b, side[1], rows, at, half),
    ]
    return rep, odd == 0, up, both, [(side, sides)]


def far_kernel(reach_ref, prior_ref, low, across, high_0a, high_0b, high_1a, high_1b, high_2a,
               high_2b, high_3a, side_a, side_b, high_out, side_out):
    side = read_reach(side_a, 3)
    side_out[0], side_out[1] = side
    rep, even, up, both, sides = far_parts(reach_ref, side, low, across, side_a, side_b)
    high_out[...] = prior_ref[...]
    late = [(high_1b, 1, 1), (high_2b, 2, 1), (high_3a, 3, 0)]
    upper(late, both, up, rep, high_out)
    early = [(high_0a, 0, 0), (high_0b, 0, 1), (high_1a, 1, 0), (high_2a, 2, 0)]
    upper(early + late, sides, up, rep, high_out, even)


def last_kernel(reach_ref, side_ref, prior_ref, low, across, high_3b, side_a, side_b, high_out):
    side = (side_ref[0], side_ref[1])
    rep, even, up, both, sides = far_parts(reach_ref, side, low, across, side_a, side_b)
    high_out[...] = prior_ref[...]
    upper([(high_3b, 3, 1)], both, up, rep, high_out)
    upper([(high_3b, 3, 1)], sides, up, rep, high_out, even)


def local(embeddings, labels):
    rows, width = embeddings.shape
    shards, reps = lax.axis_size("shard"), lax.axis_size("rep")
    quarter = rows // reps
    half = quarter // 2

    def along_shard(block, distance, keep=lambda i: True):
        route = [
            (i, i + distance) for i in range(shards) if i + distance in range(shards) and keep(i)
        ]
        return lax.ppermute(block, "shard", route)

    def partner(block):
        return lax.ppermute(block, "shard", [(i, i ^ 1) for i in range(shards)])

    def other_rep(block, flip):
        return lax.ppermute(block, "rep", [(i, i ^ flip) for i in range(reps)])

    def call(kernel, name, shapes, specs, *arrays):
        return pl.pallas_call(
            kernel,
            out_shape=[jax.ShapeDtypeStruct(shape, dtype) for shape, dtype in shapes],
            in_specs=specs[: len(arrays)],
            out_specs=specs[len(arrays) :],
            compiler_params=pltpu.CompilerParams(vmem_limit_bytes=VMEM_LIMIT),
            cost_estimate=pl.CostEstimate(flops=1024, bytes_accessed=1024, transcendentals=0),
            name=name,
        )(*arrays)

    sizes = [half, half + INFO, quarter + INFO]
    lo, hi, mine = pl.pallas_call(
        prepare_kernel,
        out_shape=[jax.ShapeDtypeStruct((size, width), BF16) for size in sizes],
        in_specs=[pl.BlockSpec(memory_space=pltpu.HBM)] * 2,
        out_specs=[VMEM] * 3,
        scratch_shapes=[
            pltpu.VMEM((2, half, width), BF16),
            pltpu.VMEM((rows // 128, 128), jnp.int32),
            pltpu.SemaphoreType.DMA((3,)),
        ],
        compiler_params=pltpu.CompilerParams(vmem_limit_bytes=PREPARE_LIMIT),
        name="prepare",
    )(embeddings, labels.reshape(rows // 128, 128))

    odd_only, even_only = (lambda i: i % 2 == 1), (lambda i: i % 2 == 0)
    fence = lax.optimization_barrier

    high_0a = along_shard(lo, -2)
    low = along_shard(mine, 2)
    across = partner(mine)
    high_0b = along_shard(hi, -2)

    high_0a, own_labels = fence((high_0a, labels))
    high_2a = other_rep(high_0a, 2)
    high_1a = other_rep(high_0a, 1)
    own, best, own_reach = pl.pallas_call(
        own_kernel,
        out_shape=[
            jax.ShapeDtypeStruct((rows, width), BF16),
            jax.ShapeDtypeStruct((1, rows), F32),
            jax.ShapeDtypeStruct((2,), jnp.int32),
        ],
        in_specs=[pl.BlockSpec(memory_space=pltpu.HBM), VMEM],
        out_specs=[VMEM, VMEM, SMEM],
        scratch_shapes=[
            pltpu.VMEM((8, rows), jnp.int32),
            pltpu.VMEM((4, quarter, width), BF16),
            pltpu.SemaphoreType.DMA((4,)),
        ],
        compiler_params=pltpu.CompilerParams(vmem_limit_bytes=OWN_LIMIT),
        cost_estimate=pl.CostEstimate(flops=1024, bytes_accessed=1024, transcendentals=0),
        name="own",
    )(embeddings, own_labels[None, :])

    across, low, own, best = fence((across, low, own, best))
    side_b = along_shard(across[:half], 2, even_only)
    side_a = along_shard(low[half:], -1, odd_only)
    high_0b, high_1a, high_2a, across, low = fence((high_0b, high_1a, high_2a, across, low))
    high_2b = other_rep(high_0b, 2)
    high_1b = other_rep(high_0b, 1)
    high_3a = other_rep(high_2a, 1)
    line = ((1, rows), F32)
    best, of_high, reach = call(
        near_kernel, "near", [line, line, ((6,), jnp.int32)],
        [SMEM] + [VMEM] * 10 + [SMEM],
        own_reach, own, best, low, across, high_0a, high_0b, high_1a, high_2a,
    )
    high_2b, side_a, side_b, high_1b, high_3a, of_high = fence(
        (high_2b, side_a, side_b, high_1b, high_3a, of_high)
    )
    high_3b = other_rep(high_2b, 1)
    of_high, side = call(
        far_kernel, "far", [line, ((2,), jnp.int32)], [SMEM] + [VMEM] * 13 + [SMEM],
        reach, of_high, low, across, high_0a, high_0b, high_1a, high_1b, high_2a, high_2b,
        high_3a, side_a, side_b,
    )
    (of_high,) = call(
        last_kernel, "last", [line], [SMEM] * 2 + [VMEM] * 7,
        reach, side, of_high, low, across, high_3b, side_a, side_b,
    )

    above = along_shard(of_high, 2)[0]
    above = jnp.where(lax.axis_index("shard") >= 2, above, -1.0)
    return lax.pmax(jnp.maximum(best[0], above), "rep")


def solution(mesh):
    placed = (P("shard", None), P("shard"))
    return jax.shard_map(local, mesh=mesh, in_specs=placed, out_specs=P("shard"), check_vma=False)
```

time: 74.4 us -> 73.9 us (level); the launches traced: 75.6 us -> 72.8 us
  starting transfers between devices: 28.2 us -> 24.9 us
  Pallas kernels: 11.9 us -> 14.8 us
  waiting for transfers between devices: 28.1 us -> 25.5 us
    ppermute x6, waiting for transfers between devices: 5.26 us -> 0.25 us  [other_rep(): return lax.ppermute(block, 'rep', [(i, i ^ flip) for i in range(reps)])]
    pallas_call x4 -> x3, Pallas kernels: 4.03 us -> 7.34 us  [call(): pl.pallas_call(kernel, out_shape=[jax.ShapeDtypeStruct(shape, dtype) for...]
    ppermute x2 -> x1, starting transfers between devices: 4.18 us -> 1.58 us  [partner(): return lax.ppermute(block, 'shard', [(i, i ^ 1) for i in range(shards)])]
    ppermute x7 -> x6, waiting for transfers between devices: 22.9 us -> 25.3 us  [along_shard(): return lax.ppermute(block, 'shard', route)]
    ppermute x7 -> x6, starting transfers between devices: 20.8 us -> 20 us  [along_shard(): return lax.ppermute(block, 'shard', route)]
  transfers between devices with their start and end apart: 15 -> 13, of which waited for: 7 -> 5; matrix products, arithmetic and copies ran while one was open for 0% -> 0% of each run, Pallas kernels for 13% -> 17%
where the time goes in v5:
time: 73.9 us; the launch traced here: 72.8 us
  waiting for transfers between devices  25.5 us (35%)
  starting transfers between devices  24.9 us (34%)
  Pallas kernels  14.8 us (20%)
  blocking collectives  6.61 us (9%)
  local copies, waits for them, and re-layouts  0.77 us (1%)
    ppermute x6, waiting for transfers between devices, along_shard(): return lax.ppermute(block, 'shard', route)  25.3 us
    ppermute x6, starting transfers between devices, along_shard(): return lax.ppermute(block, 'shard', route)  20 us
    pallas_call x3, Pallas kernels, call(): pl.pallas_call(kernel, out_shape=[jax.ShapeDtypeStruct(shape, dtype) for...  7.34 us
    pmax x1, blocking collectives, local(): return lax.pmax(jnp.maximum(best[0], above), 'rep')  6.61 us
    pallas_call x1, Pallas kernels, local(): pl.pallas_call(own_kernel, out_shape=[jax.ShapeDtypeStruct((rows, width),...  6.02 us
    ppermute x6, starting transfers between devices, other_rep(): return lax.ppermute(block, 'rep', [(i, i ^ flip) for i in range(reps)])  3.26 us
    ppermute x1, starting transfers between devices, partner(): return lax.ppermute(block, 'shard', [(i, i ^ 1) for i in range(shards)])  1.58 us
  transfers between devices with their start and end apart: 13, of which 5 were waited for; matrix products, arithmetic and copies ran while one was open for 0% of the time, Pallas kernels for 17%

profile of v5, /device:TPU:8, one launch (start us, length us, event | category | flops | bytes accessed | tf_op | source)
XLA Modules:
  0.0 72.8 jit_solution(2382913540406708789)
XLA Ops:
  0.0 0.7 copy-done
  0.7 1.5 %prepare.1 = (bf16[256,1024]{1,0:T(8,128)(2,1)S(1)}, bf16[272,1024]{1,0:T(8,128)(2,1)S(1)}, bf16[528,1024]{1,0:T(8,128)(2,1)S(1)}) custom-call(bf16[2048,1024]{1,0:T(8,128)(2,1)} %emb_ref.3, s32[16,128]{1,0:T(8,128)S(1)} %bitcast.3), custom_call_target="tpu_custom_call" | custom-call | tf_op jit(solution)/shard_map/prepare/pallas_call | solution.py:250
  2.2 3.5 %collective-permute-start.2 = (bf16[528,1024]{1,0:T(8,128)(2,1)S(1)}, bf16[528,1024]{1,0:T(8,128)(2,1)S(1)}, u32[]{:S(2)}, u32[]{:S(2)}) collective-permute-start(bf16[528,1024]{1,0:T(8,128)(2,1)S(1)} %get-tuple-element.36), channel_id=1, source_target_pairs={{0,8},{4,12},{8,16},{12,20},{16,24},{20,28},{1,9},{5,13},{9,17},{1... | collective-permute-start | bytes 3244040 | tf_op jit(solution)/shard_map/ppermute | solution.py:230
  5.7 1.6 %collective-permute-start.1 = (bf16[528,1024]{1,0:T(8,128)(2,1)S(1)}, bf16[528,1024]{1,0:T(8,128)(2,1)S(1)}, u32[]{:S(2)}, u32[]{:S(2)}) collective-permute-start(bf16[528,1024]{1,0:T(8,128)(2,1)S(1)} %get-tuple-element.36), channel_id=1, source_target_pairs={{0,4},{4,0},{8,12},{12,8},{16,20},{20,16},{24,28},{28,24},{1,5},{5... | collective-permute-start | bytes 3244040 | tf_op jit(solution)/shard_map/ppermute | solution.py:233
  7.3 2.4 %collective-permute-start = (bf16[256,1024]{1,0:T(8,128)(2,1)S(1)}, bf16[256,1024]{1,0:T(8,128)(2,1)S(1)}, u32[]{:S(2)}, u32[]{:S(2)}) collective-permute-start(bf16[256,1024]{1,0:T(8,128)(2,1)S(1)} %get-tuple-element.33), channel_id=1, source_target_pairs={{8,0},{12,4},{16,8},{20,12},{24,16},{28,20},{9,1},{13,5},{17,9},{2... | collective-permute-start | bytes 1572872 | tf_op jit(solution)/shard_map/ppermute | solution.py:230
  9.7 1.9 %collective-permute-start.3 = (bf16[272,1024]{1,0:T(8,128)(2,1)S(1)}, bf16[272,1024]{1,0:T(8,128)(2,1)S(1)}, u32[]{:S(2)}, u32[]{:S(2)}) collective-permute-start(bf16[272,1024]{1,0:T(8,128)(2,1)S(1)} %get-tuple-element.41), channel_id=1, source_target_pairs={{8,0},{12,4},{16,8},{20,12},{24,16},{28,20},{9,1},{13,5},{17,9},{2... | collective-permute-start | bytes 1671176 | tf_op jit(solution)/shard_map/ppermute | solution.py:230
  11.6 12.4 %collective-permute-done.high_0a = bf16[256,1024]{1,0:T(8,128)(2,1)S(1)} collective-permute-done((bf16[256,1024]{1,0:T(8,128)(2,1)S(1)}, bf16[256,1024]{1,0:T(8,128)(2,1)S(1)}, u32[]{:S(2)}, u32[]{:S(2)}) %collective-permute-start) | collective-permute-done | bytes 524320 | tf_op jit(solution)/shard_map/ppermute | solution.py:230
  24.0 1.5 %collective-permute-start.5 = (bf16[256,1024]{1,0:T(8,128)(2,1)S(1)}, bf16[256,1024]{1,0:T(8,128)(2,1)S(1)}, u32[]{:S(2)}, u32[]{:S(2)}) collective-permute-start(bf16[256,1024]{1,0:T(8,128)(2,1)S(1)} %collective-permute-done.high_0a), channel_id=1, source_target_pairs={{0,2},{1,3},{2,0},{3,1},{4,6},{5,7},{6,4},{7,5},{8,10},{9,11},{10,... | collective-permute-start | bytes 1572872 | tf_op jit(solution)/shard_map/ppermute | solution.py:236
  25.5 6.0 %own.1 = (bf16[2048,1024]{1,0:T(8,128)(2,1)S(1)}, f32[1,2048]{1,0:T(1,128)S(1)}, s32[2]{0:T(128)S(1)}) custom-call(bf16[2048,1024]{1,0:T(8,128)(2,1)} %emb_ref.3, s32[1,2048]{1,0:T(1,128)S(1)} %bitcast.4), custom_call_target="tpu_custom_call" | custom-call | flops 1024 | bytes 1024 | tf_op jit(solution)/shard_map/own/pallas_call | solution.py:275
  31.6 2.6 %collective-permute-done.3.high_0b = bf16[272,1024]{1,0:T(8,128)(2,1)S(1)} collective-permute-done((bf16[272,1024]{1,0:T(8,128)(2,1)S(1)}, bf16[272,1024]{1,0:T(8,128)(2,1)S(1)}, u32[]{:S(2)}, u32[]{:S(2)}) %collective-permute-start.3) | collective-permute-done | bytes 557088 | tf_op jit(solution)/shard_map/ppermute | solution.py:230
  34.2 0.2 collective-permute-done.5.high_2a
  34.4 1.3 %collective-permute-start.7 = (bf16[272,1024]{1,0:T(8,128)(2,1)S(1)}, bf16[272,1024]{1,0:T(8,128)(2,1)S(1)}, u32[]{:S(2)}, u32[]{:S(2)}) collective-permute-start(bf16[272,1024]{1,0:T(8,128)(2,1)S(1)} %slice.6), channel_id=1, source_target_pairs={{4,0},{12,8},{20,16},{28,24},{5,1},{13,9},{21,17},{29,25},{6,2},{1... | collective-permute-start | bytes 1671176 | tf_op jit(solution)/shard_map/ppermute | solution.py:230
  35.7 0.1 collective-permute-start.9
  35.8 1.6 %collective-permute-start.6 = (bf16[272,1024]{1,0:T(8,128)(2,1)S(1)}, bf16[272,1024]{1,0:T(8,128)(2,1)S(1)}, u32[]{:S(2)}, u32[]{:S(2)}) collective-permute-start(bf16[272,1024]{1,0:T(8,128)(2,1)S(1)} %collective-permute-done.3.high_0b), channel_id=1, source_target_pairs={{0,2},{1,3},{2,0},{3,1},{4,6},{5,7},{6,4},{7,5},{8,10},{9,11},{10,... | collective-permute-start | bytes 1671176 | tf_op jit(solution)/shard_map/ppermute | solution.py:236
  37.4 3.5 %collective-permute-start.8 = (bf16[256,1024]{1,0:T(8,128)(2,1)S(1)}, bf16[256,1024]{1,0:T(8,128)(2,1)S(1)}, u32[]{:S(2)}, u32[]{:S(2)}) collective-permute-start(bf16[256,1024]{1,0:T(8,128)(2,1)S(1)} %slice.7), channel_id=1, source_target_pairs={{0,8},{8,16},{16,24},{1,9},{9,17},{17,25},{2,10},{10,18},{18,26},{... | collective-permute-start | bytes 1572872 | tf_op jit(solution)/shard_map/ppermute | solution.py:230
  40.9 0.1 collective-permute-start.10
  41.0 3.3 %near.1 = (f32[1,2048]{1,0:T(1,128)S(1)}, f32[1,2048]{1,0:T(1,128)S(1)}, s32[6]{0:T(128)S(1)}) custom-call(s32[2]{0:T(128)S(1)} %get-tuple-element.35.own_reach, bf16[2048,1024]{1,0:T(8,128)(2,1)S(1)} %get-tuple-element.39.own_ref, f32[1,2048]{1,0:T(1,128)S(1)} %get-tuple-element.40.best_ref, bf16[528,1024]{1,0:T(8,128)(2,1)S(1)} %collective-permute-done.2.low, ...), custom_call_target="tpu_custom_call" | custom-call | flops 1024 | bytes 1024 | tf_op jit(solution)/shard_map/near/pallas_call | solution.py:239
  44.3 9.0 %collective-permute-done.8.side_b = bf16[256,1024]{1,0:T(8,128)(2,1)S(1)} collective-permute-done((bf16[256,1024]{1,0:T(8,128)(2,1)S(1)}, bf16[256,1024]{1,0:T(8,128)(2,1)S(1)}, u32[]{:S(2)}, u32[]{:S(2)}) %collective-permute-start.8) | collective-permute-done | bytes 524320 | tf_op jit(solution)/shard_map/ppermute | solution.py:230
  53.3 0.1 collective-permute-start.11
  53.4 2.9 %far.1 = (f32[1,2048]{1,0:T(1,128)S(1)}, s32[2]{0:T(128)S(1)}) custom-call(s32[6]{0:T(128)S(1)} %get-tuple-element.51.reach_ref, f32[1,2048]{1,0:T(1,128)S(1)} %get-tuple-element.53.prior_ref, bf16[528,1024]{1,0:T(8,128)(2,1)S(1)} %collective-permute-done.2.low, bf16[528,1024]{1,0:T(8,128)(2,1)S(1)} %collective-permute-done.1.across, ...), custom_call_target="tpu_custom_call" | custom-call | flops 1024 | bytes 1024 | tf_op jit(solution)/shard_map/far/pallas_call | solution.py:239
  56.3 1.1 %last.1 = f32[1,2048]{1,0:T(1,128)S(1)} custom-call(s32[6]{0:T(128)S(1)} %get-tuple-element.51.reach_ref, s32[2]{0:T(128)S(1)} %get-tuple-element.59.side_ref, f32[1,2048]{1,0:T(1,128)S(1)} %get-tuple-element.60.prior_ref, bf16[528,1024]{1,0:T(8,128)(2,1)S(1)} %collective-permute-done.2.low, bf16[528,1024]{1,0:T(8,128)(2,1)S(1)} %collective-permute-done.1.across, ...), custom_call_target="tpu_custom_call" | custom-call | flops 1024 | bytes 1024 | tf_op jit(solution)/shard_map/last/pallas_call | solution.py:239
  57.4 7.5 %collective-permute-start.12 = (f32[1,2048]{1,0:T(1,128)S(1)}, f32[1,2048]{1,0:T(1,128)S(1)}, u32[]{:S(2)}, u32[]{:S(2)}) collective-permute-start(f32[1,2048]{1,0:T(1,128)S(1)} %last.1), channel_id=1, source_target_pairs={{0,8},{4,12},{8,16},{12,20},{16,24},{20,28},{1,9},{5,13},{9,17},{1... | collective-permute-start | bytes 24584 | tf_op jit(solution)/shard_map/ppermute | solution.py:230
  64.9 1.3 %collective-permute-done.12 = f32[1,2048]{1,0:T(1,128)S(1)} collective-permute-done((f32[1,2048]{1,0:T(1,128)S(1)}, f32[1,2048]{1,0:T(1,128)S(1)}, u32[]{:S(2)}, u32[]{:S(2)}) %collective-permute-start.12) | collective-permute-done | bytes 8224 | tf_op jit(solution)/shard_map/ppermute | solution.py:230
  66.2 6.6 %pmax.7 = f32[2048]{0:T(1024)} all-reduce(f32[2048]{0:T(1024)S(1)} %bitcast.5), channel_id=1, replica_groups=mesh['shard'=8,'rep'=4] {'rep'}, use_global_device_ids=true, to_apply=%region_0.1 | all-reduce | flops 2048 | bytes 16384 | tf_op jit(solution)/shard_map/pmax | solution.py:323
  (15 shorter events, 0.1 us)
Async XLA Ops:
  0.0 0.7 copy-start
  0.7 24.8 %copy-start.1 = (s32[2048]{0:T(1024)S(1)}, s32[2048]{0:T(1024)}, u32[]{:S(2)}) copy-start(s32[2048]{0:T(1024)} %param.3) | copy-start | bytes 24580
  2.2 29.4 %collective-permute-start.2 = (bf16[528,1024]{1,0:T(8,128)(2,1)S(1)}, bf16[528,1024]{1,0:T(8,128)(2,1)S(1)}, u32[]{:S(2)}, u32[]{:S(2)}) collective-permute-start(bf16[528,1024]{1,0:T(8,128)(2,1)S(1)} %get-tuple-element.36), channel_id=1, source_target_pairs={{0,8},{4,12},{8,16},{12,20},{16,24},{20,28},{1,9},{5,13},{9,17},{1... | collective-permute-start | bytes 3244040 | tf_op jit(solution)/shard_map/ppermute | solution.py:230
  5.7 25.9 %collective-permute-start.1 = (bf16[528,1024]{1,0:T(8,128)(2,1)S(1)}, bf16[528,1024]{1,0:T(8,128)(2,1)S(1)}, u32[]{:S(2)}, u32[]{:S(2)}) collective-permute-start(bf16[528,1024]{1,0:T(8,128)(2,1)S(1)} %get-tuple-element.36), channel_id=1, source_target_pairs={{0,4},{4,0},{8,12},{12,8},{16,20},{20,16},{24,28},{28,24},{1,5},{5... | collective-permute-start | bytes 3244040 | tf_op jit(solution)/shard_map/ppermute | solution.py:233
  7.3 16.7 %collective-permute-start = (bf16[256,1024]{1,0:T(8,128)(2,1)S(1)}, bf16[256,1024]{1,0:T(8,128)(2,1)S(1)}, u32[]{:S(2)}, u32[]{:S(2)}) collective-permute-start(bf16[256,1024]{1,0:T(8,128)(2,1)S(1)} %get-tuple-element.33), channel_id=1, source_target_pairs={{8,0},{12,4},{16,8},{20,12},{24,16},{28,20},{9,1},{13,5},{17,9},{2... | collective-permute-start | bytes 1572872 | tf_op jit(solution)/shard_map/ppermute | solution.py:230
  9.7 24.5 %collective-permute-start.3 = (bf16[272,1024]{1,0:T(8,128)(2,1)S(1)}, bf16[272,1024]{1,0:T(8,128)(2,1)S(1)}, u32[]{:S(2)}, u32[]{:S(2)}) collective-permute-start(bf16[272,1024]{1,0:T(8,128)(2,1)S(1)} %get-tuple-element.41), channel_id=1, source_target_pairs={{8,0},{12,4},{16,8},{20,12},{24,16},{28,20},{9,1},{13,5},{17,9},{2... | collective-permute-start | bytes 1671176 | tf_op jit(solution)/shard_map/ppermute | solution.py:230
  24.0 10.4 %collective-permute-start.5 = (bf16[256,1024]{1,0:T(8,128)(2,1)S(1)}, bf16[256,1024]{1,0:T(8,128)(2,1)S(1)}, u32[]{:S(2)}, u32[]{:S(2)}) collective-permute-start(bf16[256,1024]{1,0:T(8,128)(2,1)S(1)} %collective-permute-done.high_0a), channel_id=1, source_target_pairs={{0,2},{1,3},{2,0},{3,1},{4,6},{5,7},{6,4},{7,5},{8,10},{9,11},{10,... | collective-permute-start | bytes 1572872 | tf_op jit(solution)/shard_map/ppermute | solution.py:236
  25.5 8.9 %collective-permute-start.4 = (bf16[256,1024]{1,0:T(8,128)(2,1)S(1)}, bf16[256,1024]{1,0:T(8,128)(2,1)S(1)}, u32[]{:S(2)}, u32[]{:S(2)}) collective-permute-start(bf16[256,1024]{1,0:T(8,128)(2,1)S(1)} %collective-permute-done.high_0a), channel_id=1, source_target_pairs={{0,1},{1,0},{2,3},{3,2},{4,5},{5,4},{6,7},{7,6},{8,9},{9,8},{10,11... | collective-permute-start | bytes 1572872 | tf_op jit(solution)/shard_map/ppermute | solution.py:236
  34.4 18.9 %collective-permute-start.7 = (bf16[272,1024]{1,0:T(8,128)(2,1)S(1)}, bf16[272,1024]{1,0:T(8,128)(2,1)S(1)}, u32[]{:S(2)}, u32[]{:S(2)}) collective-permute-start(bf16[272,1024]{1,0:T(8,128)(2,1)S(1)} %slice.6), channel_id=1, source_target_pairs={{4,0},{12,8},{20,16},{28,24},{5,1},{13,9},{21,17},{29,25},{6,2},{1... | collective-permute-start | bytes 1671176 | tf_op jit(solution)/shard_map/ppermute | solution.py:230
  35.7 17.6 %collective-permute-start.9 = (bf16[272,1024]{1,0:T(8,128)(2,1)S(1)}, bf16[272,1024]{1,0:T(8,128)(2,1)S(1)}, u32[]{:S(2)}, u32[]{:S(2)}) collective-permute-start(bf16[272,1024]{1,0:T(8,128)(2,1)S(1)} %collective-permute-done.3.high_0b), channel_id=1, source_target_pairs={{0,1},{1,0},{2,3},{3,2},{4,5},{5,4},{6,7},{7,6},{8,9},{9,8},{10,11... | collective-permute-start | bytes 1671176 | tf_op jit(solution)/shard_map/ppermute | solution.py:236
  35.8 17.5 %collective-permute-start.6 = (bf16[272,1024]{1,0:T(8,128)(2,1)S(1)}, bf16[272,1024]{1,0:T(8,128)(2,1)S(1)}, u32[]{:S(2)}, u32[]{:S(2)}) collective-permute-start(bf16[272,1024]{1,0:T(8,128)(2,1)S(1)} %collective-permute-done.3.high_0b), channel_id=1, source_target_pairs={{0,2},{1,3},{2,0},{3,1},{4,6},{5,7},{6,4},{7,5},{8,10},{9,11},{10,... | collective-permute-start | bytes 1671176 | tf_op jit(solution)/shard_map/ppermute | solution.py:236
  37.4 15.9 %collective-permute-start.8 = (bf16[256,1024]{1,0:T(8,128)(2,1)S(1)}, bf16[256,1024]{1,0:T(8,128)(2,1)S(1)}, u32[]{:S(2)}, u32[]{:S(2)}) collective-permute-start(bf16[256,1024]{1,0:T(8,128)(2,1)S(1)} %slice.7), channel_id=1, source_target_pairs={{0,8},{8,16},{16,24},{1,9},{9,17},{17,25},{2,10},{10,18},{18,26},{... | collective-permute-start | bytes 1572872 | tf_op jit(solution)/shard_map/ppermute | solution.py:230
  40.9 12.4 %collective-permute-start.10 = (bf16[256,1024]{1,0:T(8,128)(2,1)S(1)}, bf16[256,1024]{1,0:T(8,128)(2,1)S(1)}, u32[]{:S(2)}, u32[]{:S(2)}) collective-permute-start(bf16[256,1024]{1,0:T(8,128)(2,1)S(1)} %collective-permute-done.5.high_2a), channel_id=1, source_target_pairs={{0,1},{1,0},{2,3},{3,2},{4,5},{5,4},{6,7},{7,6},{8,9},{9,8},{10,11... | collective-permute-start | bytes 1572872 | tf_op jit(solution)/shard_map/ppermute | solution.py:236
  53.3 3.0 %collective-permute-start.11 = (bf16[272,1024]{1,0:T(8,128)(2,1)S(1)}, bf16[272,1024]{1,0:T(8,128)(2,1)S(1)}, u32[]{:S(2)}, u32[]{:S(2)}) collective-permute-start(bf16[272,1024]{1,0:T(8,128)(2,1)S(1)} %collective-permute-done.6.high_2b), channel_id=1, source_target_pairs={{0,1},{1,0},{2,3},{3,2},{4,5},{5,4},{6,7},{7,6},{8,9},{9,8},{10,11... | collective-permute-start | bytes 1671176 | tf_op jit(solution)/shard_map/ppermute | solution.py:236
  57.4 8.8 %collective-permute-start.12 = (f32[1,2048]{1,0:T(1,128)S(1)}, f32[1,2048]{1,0:T(1,128)S(1)}, u32[]{:S(2)}, u32[]{:S(2)}) collective-permute-start(f32[1,2048]{1,0:T(1,128)S(1)} %last.1), channel_id=1, source_target_pairs={{0,8},{4,12},{8,16},{12,20},{16,24},{20,28},{1,9},{5,13},{9,17},{1... | collective-permute-start | bytes 24584 | tf_op jit(solution)/shard_map/ppermute | solution.py:230

commit v6 on v5

--- a/solution.py
+++ b/solution.py
@@ -180,21 +180,33 @@
     upper(pieces, [(beside, besides), (lower, lows)], up, rep, high_out)
 
 
-def far_parts(reach_ref, side, low, across, side_a, side_b):
-    half = TILE
-    quarter, rows = 2 * half, 8 * half
-    rep, odd = lax.axis_index("rep"), lax.axis_index("shard") % 2
+def both_keys(reach_ref, low, across):
+    quarter, rows = 2 * TILE, 8 * TILE
+    rep = lax.axis_index("rep")
     lower, beside, up = [(reach_ref[2 * n], reach_ref[2 * n + 1]) for n in range(3)]
     at = rep * quarter
     both = [
         (beside, [key_piece(across, beside[1], rows, at, quarter)]),
         (lower, [key_piece(low, lower[1], rows, at, quarter)]),
     ]
+    return rep, up, both
+
+
+def middle_kernel(reach_ref, prior_ref, low, across, high_1b, high_3a, high_out):
+    rep, up, both = both_keys(reach_ref, low, across)
+    high_out[...] = prior_ref[...]
+    upper([(high_1b, 1, 1), (high_3a, 3, 0)], both, up, rep, high_out)
+
+
+def far_parts(reach_ref, side, low, across, side_a, side_b):
+    half, rows = TILE, 8 * TILE
+    rep, up, both = both_keys(reach_ref, low, across)
+    at = rep * 2 * half
     sides = [
         key_piece(side_a, side[1], rows, at + half, half),
         key_piece(side_b, side[1], rows, at, half),
     ]
-    return rep, odd == 0, up, both, [(side, sides)]
+    return rep, lax.axis_index("shard") % 2 == 0, up, both, [(side, sides)]
 
 
 def far_kernel(reach_ref, prior_ref, low, across, high_0a, high_0b, high_1a, high_1b, high_2a,
@@ -203,10 +215,10 @@
     side_out[0], side_out[1] = side
     rep, even, up, both, sides = far_parts(reach_ref, side, low, across, side_a, side_b)
     high_out[...] = prior_ref[...]
-    late = [(high_1b, 1, 1), (high_2b, 2, 1), (high_3a, 3, 0)]
-    upper(late, both, up, rep, high_out)
-    early = [(high_0a, 0, 0), (high_0b, 0, 1), (high_1a, 1, 0), (high_2a, 2, 0)]
-    upper(early + late, sides, up, rep, high_out, even)
+    upper([(high_2b, 2, 1)], both, up, rep, high_out)
+    pieces = [(high_0a, 0, 0), (high_0b, 0, 1), (high_1a, 1, 0), (high_1b, 1, 1), (high_2a, 2, 0)]
+    pieces += [(high_2b, 2, 1), (high_3a, 3, 0)]
+    upper(pieces, sides, up, rep, high_out, even)
 
 
 def last_kernel(reach_ref, side_ref, prior_ref, low, across, high_3b, side_a, side_b, high_out):
@@ -304,9 +316,11 @@
         [SMEM] + [VMEM] * 10 + [SMEM],
         own_reach, own, best, low, across, high_0a, high_0b, high_1a, high_2a,
     )
-    high_2b, side_a, side_b, high_1b, high_3a, of_high = fence(
-        (high_2b, side_a, side_b, high_1b, high_3a, of_high)
+    (of_high,) = call(
+        middle_kernel, "middle", [line], [SMEM] + [VMEM] * 6,
+        reach, of_high, low, across, high_1b, high_3a,
     )
+    high_2b, side_a, side_b, of_high = fence((high_2b, side_a, side_b, of_high))
     high_3b = other_rep(high_2b, 1)
     of_high, side = call(
         far_kernel, "far", [line, ((2,), jnp.int32)], [SMEM] + [VMEM] * 13 + [SMEM],
@@ -318,9 +332,10 @@
         reach, side, of_high, low, across, high_3b, side_a, side_b,
     )
 
-    above = along_shard(of_high, 2)[0]
-    above = jnp.where(lax.axis_index("shard") >= 2, above, -1.0)
-    return lax.pmax(jnp.maximum(best[0], above), "rep")
+    above = along_shard(of_high, 2)
+    best = jnp.maximum(best, jnp.where(lax.axis_index("shard") >= 2, above, -1.0))
+    others = [other_rep(best, flip) for flip in range(1, reps)]
+    return functools.reduce(jnp.maximum, others, best)[0]
 
 
 def solution(mesh):

time: 73.9 us -> 70.4 us (0.953)
  blocking collectives: 6.61 us -> 0 us
  starting transfers between devices: 24.9 us -> 26.8 us
    pmax x1 -> x0, blocking collectives: 6.61 us -> none  [local(): return lax.pmax(jnp.maximum(best[0], above), 'rep')]
    ppermute x6 -> x9, starting transfers between devices: 3.26 us -> 5.2 us  [other_rep(): return lax.ppermute(block, 'rep', [(i, i ^ flip) for i in range(reps)])]
    ppermute x6 -> x9, waiting for transfers between devices: 0.25 us -> 2.16 us  [other_rep(): return lax.ppermute(block, 'rep', [(i, i ^ flip) for i in range(reps)])]
    ppermute x6, waiting for transfers between devices: 25.3 us -> 23.9 us  [along_shard(): return lax.ppermute(block, 'shard', route)]
    pallas_call x3 -> x4, Pallas kernels: 7.34 us -> 7.9 us  [call(): pl.pallas_call(kernel, out_shape=[jax.ShapeDtypeStruct(shape, dtype) for...]
  transfers between devices with their start and end apart: 13 -> 16, of which waited for: 5 -> 7; matrix products, arithmetic and copies ran while one was open for 0% -> 0% of each run, Pallas kernels for 17% -> 18%
where the time goes in v6:
time: 70.4 us; the launch traced here: 69.8 us
  starting transfers between devices  26.8 us (38%)
  waiting for transfers between devices  26.1 us (37%)
  Pallas kernels  15.4 us (22%)
  local copies, waits for them, and re-layouts  0.77 us (1%)
    ppermute x6, waiting for transfers between devices, along_shard(): return lax.ppermute(block, 'shard', route)  23.9 us
    ppermute x6, starting transfers between devices, along_shard(): return lax.ppermute(block, 'shard', route)  20 us
    pallas_call x4, Pallas kernels, call(): pl.pallas_call(kernel, out_shape=[jax.ShapeDtypeStruct(shape, dtype) for...  7.9 us
    pallas_call x1, Pallas kernels, local(): pl.pallas_call(own_kernel, out_shape=[jax.ShapeDtypeStruct((rows, width),...  6.02 us
    ppermute x9, starting transfers between devices, other_rep(): return lax.ppermute(block, 'rep', [(i, i ^ flip) for i in range(reps)])  5.2 us
    ppermute x9, waiting for transfers between devices, other_rep(): return lax.ppermute(block, 'rep', [(i, i ^ flip) for i in range(reps)])  2.16 us
    ppermute x1, starting transfers between devices, partner(): return lax.ppermute(block, 'shard', [(i, i ^ 1) for i in range(shards)])  1.58 us
    pallas_call x1, Pallas kernels, local(): pl.pallas_call(prepare_kernel, out_shape=[jax.ShapeDtypeStruct((size, wid...  1.47 us
  transfers between devices with their start and end apart: 16, of which 7 were waited for; matrix products, arithmetic and copies ran while one was open for 0% of the time, Pallas kernels for 18%

profile of v6, /device:TPU:8, one launch (start us, length us, event | category | flops | bytes accessed | tf_op | source)
XLA Modules:
  0.0 69.8 jit_solution(3470984349293489517)
XLA Ops:
  0.0 0.7 copy-done
  0.7 1.5 %prepare.1 = (bf16[256,1024]{1,0:T(8,128)(2,1)S(1)}, bf16[272,1024]{1,0:T(8,128)(2,1)S(1)}, bf16[528,1024]{1,0:T(8,128)(2,1)S(1)}) custom-call(bf16[2048,1024]{1,0:T(8,128)(2,1)} %emb_ref.3, s32[16,128]{1,0:T(8,128)S(1)} %bitcast.3), custom_call_target="tpu_custom_call" | custom-call | tf_op jit(solution)/shard_map/prepare/pallas_call | solution.py:262
  2.2 3.5 %collective-permute-start.2 = (bf16[528,1024]{1,0:T(8,128)(2,1)S(1)}, bf16[528,1024]{1,0:T(8,128)(2,1)S(1)}, u32[]{:S(2)}, u32[]{:S(2)}) collective-permute-start(bf16[528,1024]{1,0:T(8,128)(2,1)S(1)} %get-tuple-element.34), channel_id=1, source_target_pairs={{0,8},{4,12},{8,16},{12,20},{16,24},{20,28},{1,9},{5,13},{9,17},{1... | collective-permute-start | bytes 3244040 | tf_op jit(solution)/shard_map/ppermute | solution.py:242
  5.7 1.6 %collective-permute-start.1 = (bf16[528,1024]{1,0:T(8,128)(2,1)S(1)}, bf16[528,1024]{1,0:T(8,128)(2,1)S(1)}, u32[]{:S(2)}, u32[]{:S(2)}) collective-permute-start(bf16[528,1024]{1,0:T(8,128)(2,1)S(1)} %get-tuple-element.34), channel_id=1, source_target_pairs={{0,4},{4,0},{8,12},{12,8},{16,20},{20,16},{24,28},{28,24},{1,5},{5... | collective-permute-start | bytes 3244040 | tf_op jit(solution)/shard_map/ppermute | solution.py:245
  7.3 2.4 %collective-permute-start = (bf16[256,1024]{1,0:T(8,128)(2,1)S(1)}, bf16[256,1024]{1,0:T(8,128)(2,1)S(1)}, u32[]{:S(2)}, u32[]{:S(2)}) collective-permute-start(bf16[256,1024]{1,0:T(8,128)(2,1)S(1)} %get-tuple-element.31), channel_id=1, source_target_pairs={{8,0},{12,4},{16,8},{20,12},{24,16},{28,20},{9,1},{13,5},{17,9},{2... | collective-permute-start | bytes 1572872 | tf_op jit(solution)/shard_map/ppermute | solution.py:242
  9.7 1.9 %collective-permute-start.3 = (bf16[272,1024]{1,0:T(8,128)(2,1)S(1)}, bf16[272,1024]{1,0:T(8,128)(2,1)S(1)}, u32[]{:S(2)}, u32[]{:S(2)}) collective-permute-start(bf16[272,1024]{1,0:T(8,128)(2,1)S(1)} %get-tuple-element.39), channel_id=1, source_target_pairs={{8,0},{12,4},{16,8},{20,12},{24,16},{28,20},{9,1},{13,5},{17,9},{2... | collective-permute-start | bytes 1671176 | tf_op jit(solution)/shard_map/ppermute | solution.py:242
  11.6 12.4 %collective-permute-done.high_0a = bf16[256,1024]{1,0:T(8,128)(2,1)S(1)} collective-permute-done((bf16[256,1024]{1,0:T(8,128)(2,1)S(1)}, bf16[256,1024]{1,0:T(8,128)(2,1)S(1)}, u32[]{:S(2)}, u32[]{:S(2)}) %collective-permute-start) | collective-permute-done | bytes 524320 | tf_op jit(solution)/shard_map/ppermute | solution.py:242
  24.0 1.5 %collective-permute-start.5 = (bf16[256,1024]{1,0:T(8,128)(2,1)S(1)}, bf16[256,1024]{1,0:T(8,128)(2,1)S(1)}, u32[]{:S(2)}, u32[]{:S(2)}) collective-permute-start(bf16[256,1024]{1,0:T(8,128)(2,1)S(1)} %collective-permute-done.high_0a), channel_id=1, source_target_pairs={{0,2},{1,3},{2,0},{3,1},{4,6},{5,7},{6,4},{7,5},{8,10},{9,11},{10,... | collective-permute-start | bytes 1572872 | tf_op jit(solution)/shard_map/ppermute | solution.py:248
  25.5 6.0 %own.1 = (bf16[2048,1024]{1,0:T(8,128)(2,1)S(1)}, f32[1,2048]{1,0:T(1,128)S(1)}, s32[2]{0:T(128)S(1)}) custom-call(bf16[2048,1024]{1,0:T(8,128)(2,1)} %emb_ref.3, s32[1,2048]{1,0:T(1,128)S(1)} %bitcast.4), custom_call_target="tpu_custom_call" | custom-call | flops 1024 | bytes 1024 | tf_op jit(solution)/shard_map/own/pallas_call | solution.py:287
  31.5 2.6 %collective-permute-done.3.high_0b = bf16[272,1024]{1,0:T(8,128)(2,1)S(1)} collective-permute-done((bf16[272,1024]{1,0:T(8,128)(2,1)S(1)}, bf16[272,1024]{1,0:T(8,128)(2,1)S(1)}, u32[]{:S(2)}, u32[]{:S(2)}) %collective-permute-start.3) | collective-permute-done | bytes 557088 | tf_op jit(solution)/shard_map/ppermute | solution.py:242
  34.5 1.3 %collective-permute-start.7 = (bf16[272,1024]{1,0:T(8,128)(2,1)S(1)}, bf16[272,1024]{1,0:T(8,128)(2,1)S(1)}, u32[]{:S(2)}, u32[]{:S(2)}) collective-permute-start(bf16[272,1024]{1,0:T(8,128)(2,1)S(1)} %slice.6), channel_id=1, source_target_pairs={{4,0},{12,8},{20,16},{28,24},{5,1},{13,9},{21,17},{29,25},{6,2},{1... | collective-permute-start | bytes 1671176 | tf_op jit(solution)/shard_map/ppermute | solution.py:242
  35.8 1.6 %collective-permute-start.6 = (bf16[272,1024]{1,0:T(8,128)(2,1)S(1)}, bf16[272,1024]{1,0:T(8,128)(2,1)S(1)}, u32[]{:S(2)}, u32[]{:S(2)}) collective-permute-start(bf16[272,1024]{1,0:T(8,128)(2,1)S(1)} %collective-permute-done.3.high_0b), channel_id=1, source_target_pairs={{0,2},{1,3},{2,0},{3,1},{4,6},{5,7},{6,4},{7,5},{8,10},{9,11},{10,... | collective-permute-start | bytes 1671176 | tf_op jit(solution)/shard_map/ppermute | solution.py:248
  37.6 3.5 %collective-permute-start.8 = (bf16[256,1024]{1,0:T(8,128)(2,1)S(1)}, bf16[256,1024]{1,0:T(8,128)(2,1)S(1)}, u32[]{:S(2)}, u32[]{:S(2)}) collective-permute-start(bf16[256,1024]{1,0:T(8,128)(2,1)S(1)} %slice.7), channel_id=1, source_target_pairs={{0,8},{8,16},{16,24},{1,9},{9,17},{17,25},{2,10},{10,18},{18,26},{... | collective-permute-start | bytes 1572872 | tf_op jit(solution)/shard_map/ppermute | solution.py:242
  41.1 3.3 %near.1 = (f32[1,2048]{1,0:T(1,128)S(1)}, f32[1,2048]{1,0:T(1,128)S(1)}, s32[6]{0:T(128)S(1)}) custom-call(s32[2]{0:T(128)S(1)} %get-tuple-element.33.own_reach, bf16[2048,1024]{1,0:T(8,128)(2,1)S(1)} %get-tuple-element.37.own_ref, f32[1,2048]{1,0:T(1,128)S(1)} %get-tuple-element.38.best_ref, bf16[528,1024]{1,0:T(8,128)(2,1)S(1)} %collective-permute-done.2.low, ...), custom_call_target="tpu_custom_call" | custom-call | flops 1024 | bytes 1024 | tf_op jit(solution)/shard_map/near/pallas_call | solution.py:251
  44.5 1.6 %middle.1.prior_ref = f32[1,2048]{1,0:T(1,128)S(1)} custom-call(s32[6]{0:T(128)S(1)} %get-tuple-element.49.reach_ref, f32[1,2048]{1,0:T(1,128)S(1)} %get-tuple-element.50.prior_ref, bf16[528,1024]{1,0:T(8,128)(2,1)S(1)} %collective-permute-done.2.low, bf16[528,1024]{1,0:T(8,128)(2,1)S(1)} %collective-permute-done.1.across, ...), custom_call_target="tpu_custom_call" | custom-call | flops 1024 | bytes 1024 | tf_op jit(solution)/shard_map/middle/pallas_call | solution.py:251
  46.0 7.6 %collective-permute-done.8.side_b = bf16[256,1024]{1,0:T(8,128)(2,1)S(1)} collective-permute-done((bf16[256,1024]{1,0:T(8,128)(2,1)S(1)}, bf16[256,1024]{1,0:T(8,128)(2,1)S(1)}, u32[]{:S(2)}, u32[]{:S(2)}) %collective-permute-start.8) | collective-permute-done | bytes 524320 | tf_op jit(solution)/shard_map/ppermute | solution.py:242
  53.6 1.9 %far.1 = (f32[1,2048]{1,0:T(1,128)S(1)}, s32[2]{0:T(128)S(1)}) custom-call(s32[6]{0:T(128)S(1)} %get-tuple-element.49.reach_ref, f32[1,2048]{1,0:T(1,128)S(1)} %middle.1.prior_ref, bf16[528,1024]{1,0:T(8,128)(2,1)S(1)} %collective-permute-done.2.low, bf16[528,1024]{1,0:T(8,128)(2,1)S(1)} %collective-permute-done.1.across, ...), custom_call_target="tpu_custom_call" | custom-call | flops 1024 | bytes 1024 | tf_op jit(solution)/shard_map/far/pallas_call | solution.py:251
  55.6 1.1 %last.1 = f32[1,2048]{1,0:T(1,128)S(1)} custom-call(s32[6]{0:T(128)S(1)} %get-tuple-element.49.reach_ref, s32[2]{0:T(128)S(1)} %get-tuple-element.55.side_ref, f32[1,2048]{1,0:T(1,128)S(1)} %get-tuple-element.56.prior_ref, bf16[528,1024]{1,0:T(8,128)(2,1)S(1)} %collective-permute-done.2.low, bf16[528,1024]{1,0:T(8,128)(2,1)S(1)} %collective-permute-done.1.across, ...), custom_call_target="tpu_custom_call" | custom-call | flops 1024 | bytes 1024 | tf_op jit(solution)/shard_map/last/pallas_call | solution.py:251
  56.7 7.4 %collective-permute-start.12 = (f32[1,2048]{1,0:T(1,128)S(1)}, f32[1,2048]{1,0:T(1,128)S(1)}, u32[]{:S(2)}, u32[]{:S(2)}) collective-permute-start(f32[1,2048]{1,0:T(1,128)S(1)} %last.1), channel_id=1, source_target_pairs={{0,8},{4,12},{8,16},{12,20},{16,24},{20,28},{1,9},{5,13},{9,17},{1... | collective-permute-start | bytes 24584 | tf_op jit(solution)/shard_map/ppermute | solution.py:242
  64.1 1.3 %collective-permute-done.12 = f32[1,2048]{1,0:T(1,128)S(1)} collective-permute-done((f32[1,2048]{1,0:T(1,128)S(1)}, f32[1,2048]{1,0:T(1,128)S(1)}, u32[]{:S(2)}, u32[]{:S(2)}) %collective-permute-start.12) | collective-permute-done | bytes 8224 | tf_op jit(solution)/shard_map/ppermute | solution.py:242
  65.5 1.2 %collective-permute-start.14 = (f32[1,2048]{1,0:T(1,128)S(1)}, f32[1,2048]{1,0:T(1,128)S(1)}, u32[]{:S(2)}, u32[]{:S(2)}) collective-permute-start(f32[1,2048]{1,0:T(1,128)S(1)} %fusion), channel_id=1, source_target_pairs={{0,2},{1,3},{2,0},{3,1},{4,6},{5,7},{6,4},{7,5},{8,10},{9,11},{10,... | collective-permute-start | bytes 24584 | tf_op jit(solution)/shard_map/ppermute | solution.py:248
  66.7 0.6 collective-permute-start.13
  67.4 1.2 %collective-permute-done.15 = f32[1,2048]{1,0:T(1,128)S(1)} collective-permute-done((f32[1,2048]{1,0:T(1,128)S(1)}, f32[1,2048]{1,0:T(1,128)S(1)}, u32[]{:S(2)}, u32[]{:S(2)}) %collective-permute-start.15) | collective-permute-done | bytes 8224 | tf_op jit(solution)/shard_map/ppermute | solution.py:248
  68.6 0.7 collective-permute-done.14
  (22 shorter events, 1.3 us)
Async XLA Ops:
  0.0 0.7 copy-start
  0.7 24.8 %copy-start.1 = (s32[2048]{0:T(1024)S(1)}, s32[2048]{0:T(1024)}, u32[]{:S(2)}) copy-start(s32[2048]{0:T(1024)} %param.3) | copy-start | bytes 24580
  2.2 29.4 %collective-permute-start.2 = (bf16[528,1024]{1,0:T(8,128)(2,1)S(1)}, bf16[528,1024]{1,0:T(8,128)(2,1)S(1)}, u32[]{:S(2)}, u32[]{:S(2)}) collective-permute-start(bf16[528,1024]{1,0:T(8,128)(2,1)S(1)} %get-tuple-element.34), channel_id=1, source_target_pairs={{0,8},{4,12},{8,16},{12,20},{16,24},{20,28},{1,9},{5,13},{9,17},{1... | collective-permute-start | bytes 3244040 | tf_op jit(solution)/shard_map/ppermute | solution.py:242
  5.7 25.9 %collective-permute-start.1 = (bf16[528,1024]{1,0:T(8,128)(2,1)S(1)}, bf16[528,1024]{1,0:T(8,128)(2,1)S(1)}, u32[]{:S(2)}, u32[]{:S(2)}) collective-permute-start(bf16[528,1024]{1,0:T(8,128)(2,1)S(1)} %get-tuple-element.34), channel_id=1, source_target_pairs={{0,4},{4,0},{8,12},{12,8},{16,20},{20,16},{24,28},{28,24},{1,5},{5... | collective-permute-start | bytes 3244040 | tf_op jit(solution)/shard_map/ppermute | solution.py:245
  7.3 16.7 %collective-permute-start = (bf16[256,1024]{1,0:T(8,128)(2,1)S(1)}, bf16[256,1024]{1,0:T(8,128)(2,1)S(1)}, u32[]{:S(2)}, u32[]{:S(2)}) collective-permute-start(bf16[256,1024]{1,0:T(8,128)(2,1)S(1)} %get-tuple-element.31), channel_id=1, source_target_pairs={{8,0},{12,4},{16,8},{20,12},{24,16},{28,20},{9,1},{13,5},{17,9},{2... | collective-permute-start | bytes 1572872 | tf_op jit(solution)/shard_map/ppermute | solution.py:242
  9.7 24.5 %collective-permute-start.3 = (bf16[272,1024]{1,0:T(8,128)(2,1)S(1)}, bf16[272,1024]{1,0:T(8,128)(2,1)S(1)}, u32[]{:S(2)}, u32[]{:S(2)}) collective-permute-start(bf16[272,1024]{1,0:T(8,128)(2,1)S(1)} %get-tuple-element.39), channel_id=1, source_target_pairs={{8,0},{12,4},{16,8},{20,12},{24,16},{28,20},{9,1},{13,5},{17,9},{2... | collective-permute-start | bytes 1671176 | tf_op jit(solution)/shard_map/ppermute | solution.py:242
  24.0 10.4 %collective-permute-start.5 = (bf16[256,1024]{1,0:T(8,128)(2,1)S(1)}, bf16[256,1024]{1,0:T(8,128)(2,1)S(1)}, u32[]{:S(2)}, u32[]{:S(2)}) collective-permute-start(bf16[256,1024]{1,0:T(8,128)(2,1)S(1)} %collective-permute-done.high_0a), channel_id=1, source_target_pairs={{0,2},{1,3},{2,0},{3,1},{4,6},{5,7},{6,4},{7,5},{8,10},{9,11},{10,... | collective-permute-start | bytes 1572872 | tf_op jit(solution)/shard_map/ppermute | solution.py:248
  25.5 8.9 %collective-permute-start.4 = (bf16[256,1024]{1,0:T(8,128)(2,1)S(1)}, bf16[256,1024]{1,0:T(8,128)(2,1)S(1)}, u32[]{:S(2)}, u32[]{:S(2)}) collective-permute-start(bf16[256,1024]{1,0:T(8,128)(2,1)S(1)} %collective-permute-done.high_0a), channel_id=1, source_target_pairs={{0,1},{1,0},{2,3},{3,2},{4,5},{5,4},{6,7},{7,6},{8,9},{9,8},{10,11... | collective-permute-start | bytes 1572872 | tf_op jit(solution)/shard_map/ppermute | solution.py:248
  34.4 10.0 %collective-permute-start.9 = (bf16[272,1024]{1,0:T(8,128)(2,1)S(1)}, bf16[272,1024]{1,0:T(8,128)(2,1)S(1)}, u32[]{:S(2)}, u32[]{:S(2)}) collective-permute-start(bf16[272,1024]{1,0:T(8,128)(2,1)S(1)} %collective-permute-done.3.high_0b), channel_id=1, source_target_pairs={{0,1},{1,0},{2,3},{3,2},{4,5},{5,4},{6,7},{7,6},{8,9},{9,8},{10,11... | collective-permute-start | bytes 1671176 | tf_op jit(solution)/shard_map/ppermute | solution.py:248
  34.5 19.1 %collective-permute-start.7 = (bf16[272,1024]{1,0:T(8,128)(2,1)S(1)}, bf16[272,1024]{1,0:T(8,128)(2,1)S(1)}, u32[]{:S(2)}, u32[]{:S(2)}) collective-permute-start(bf16[272,1024]{1,0:T(8,128)(2,1)S(1)} %slice.6), channel_id=1, source_target_pairs={{4,0},{12,8},{20,16},{28,24},{5,1},{13,9},{21,17},{29,25},{6,2},{1... | collective-permute-start | bytes 1671176 | tf_op jit(solution)/shard_map/ppermute | solution.py:242
  35.8 17.8 %collective-permute-start.6 = (bf16[272,1024]{1,0:T(8,128)(2,1)S(1)}, bf16[272,1024]{1,0:T(8,128)(2,1)S(1)}, u32[]{:S(2)}, u32[]{:S(2)}) collective-permute-start(bf16[272,1024]{1,0:T(8,128)(2,1)S(1)} %collective-permute-done.3.high_0b), channel_id=1, source_target_pairs={{0,2},{1,3},{2,0},{3,1},{4,6},{5,7},{6,4},{7,5},{8,10},{9,11},{10,... | collective-permute-start | bytes 1671176 | tf_op jit(solution)/shard_map/ppermute | solution.py:248
  37.3 7.1 %collective-permute-start.10 = (bf16[256,1024]{1,0:T(8,128)(2,1)S(1)}, bf16[256,1024]{1,0:T(8,128)(2,1)S(1)}, u32[]{:S(2)}, u32[]{:S(2)}) collective-permute-start(bf16[256,1024]{1,0:T(8,128)(2,1)S(1)} %collective-permute-done.5.high_2a), channel_id=1, source_target_pairs={{0,1},{1,0},{2,3},{3,2},{4,5},{5,4},{6,7},{7,6},{8,9},{9,8},{10,11... | collective-permute-start | bytes 1572872 | tf_op jit(solution)/shard_map/ppermute | solution.py:248
  37.6 16.0 %collective-permute-start.8 = (bf16[256,1024]{1,0:T(8,128)(2,1)S(1)}, bf16[256,1024]{1,0:T(8,128)(2,1)S(1)}, u32[]{:S(2)}, u32[]{:S(2)}) collective-permute-start(bf16[256,1024]{1,0:T(8,128)(2,1)S(1)} %slice.7), channel_id=1, source_target_pairs={{0,8},{8,16},{16,24},{1,9},{9,17},{17,25},{2,10},{10,18},{18,26},{... | collective-permute-start | bytes 1572872 | tf_op jit(solution)/shard_map/ppermute | solution.py:242
  53.6 2.0 %collective-permute-start.11 = (bf16[272,1024]{1,0:T(8,128)(2,1)S(1)}, bf16[272,1024]{1,0:T(8,128)(2,1)S(1)}, u32[]{:S(2)}, u32[]{:S(2)}) collective-permute-start(bf16[272,1024]{1,0:T(8,128)(2,1)S(1)} %collective-permute-done.6.high_2b), channel_id=1, source_target_pairs={{0,1},{1,0},{2,3},{3,2},{4,5},{5,4},{6,7},{7,6},{8,9},{9,8},{10,11... | collective-permute-start | bytes 1671176 | tf_op jit(solution)/shard_map/ppermute | solution.py:248
  56.7 8.8 %collective-permute-start.12 = (f32[1,2048]{1,0:T(1,128)S(1)}, f32[1,2048]{1,0:T(1,128)S(1)}, u32[]{:S(2)}, u32[]{:S(2)}) collective-permute-start(f32[1,2048]{1,0:T(1,128)S(1)} %last.1), channel_id=1, source_target_pairs={{0,8},{4,12},{8,16},{12,20},{16,24},{20,28},{1,9},{5,13},{9,17},{1... | collective-permute-start | bytes 24584 | tf_op jit(solution)/shard_map/ppermute | solution.py:242
  65.4 3.1 %collective-permute-start.15 = (f32[1,2048]{1,0:T(1,128)S(1)}, f32[1,2048]{1,0:T(1,128)S(1)}, u32[]{:S(2)}, u32[]{:S(2)}) collective-permute-start(f32[1,2048]{1,0:T(1,128)S(1)} %fusion), channel_id=1, source_target_pairs={{0,3},{1,2},{2,1},{3,0},{4,7},{5,6},{6,5},{7,4},{8,11},{9,10},{10,... | collective-permute-start | bytes 24584 | tf_op jit(solution)/shard_map/ppermute | solution.py:248
  65.5 3.7 %collective-permute-start.14 = (f32[1,2048]{1,0:T(1,128)S(1)}, f32[1,2048]{1,0:T(1,128)S(1)}, u32[]{:S(2)}, u32[]{:S(2)}) collective-permute-start(f32[1,2048]{1,0:T(1,128)S(1)} %fusion), channel_id=1, source_target_pairs={{0,2},{1,3},{2,0},{3,1},{4,6},{5,7},{6,4},{7,5},{8,10},{9,11},{10,... | collective-permute-start | bytes 24584 | tf_op jit(solution)/shard_map/ppermute | solution.py:248
  66.7 2.5 %collective-permute-start.13 = (f32[1,2048]{1,0:T(1,128)S(1)}, f32[1,2048]{1,0:T(1,128)S(1)}, u32[]{:S(2)}, u32[]{:S(2)}) collective-permute-start(f32[1,2048]{1,0:T(1,128)S(1)} %fusion), channel_id=1, source_target_pairs={{0,1},{1,0},{2,3},{3,2},{4,5},{5,4},{6,7},{7,6},{8,9},{9,8},{10,11... | collective-permute-start | bytes 24584 | tf_op jit(solution)/shard_map/ppermute | solution.py:248

commit v7 on v6

--- a/solution.py
+++ b/solution.py
@@ -77,15 +77,19 @@
 
 def group(keys, queries_ref, query_rows, out_ref, out_at, count):
     step = min(WIDE, query_rows)
-
-    def over_queries(j, _):
+    clear = functools.reduce(jnp.logical_and, [first <= 0 for *_, first in keys])
+    trips = (count + step - 1) // step
+
+    def over_queries(masked, j, _):
         at = pl.multiple_of(j * step, step)
         queries = queries_ref[pl.ds(at, step), :]
         best = None
         for ref, row, rows, first in keys:
             scores = score(ref[pl.ds(row, rows), :], queries)
-            index = lax.broadcasted_iota(jnp.int32, scores.shape, 0)
-            top = fold(jnp.where(index >= first, scores, -1.0))
+            if masked:
+                index = lax.broadcasted_iota(jnp.int32, scores.shape, 0)
+                scores = jnp.where(index >= first, scores, -1.0)
+            top = fold(scores)
             best = top if best is None else jnp.maximum(best, top)
         best = jnp.max(best, axis=0, keepdims=True)
         col = lax.broadcasted_iota(jnp.int32, best.shape, 1) + at
@@ -93,7 +97,8 @@
         out_ref[:, cols] = jnp.maximum(out_ref[:, cols], jnp.where(col < count, best, -1.0))
         return 0
 
-    lax.fori_loop(0, (count + step - 1) // step, over_queries, 0)
+    lax.fori_loop(0, jnp.where(clear, trips, 0), functools.partial(over_queries, False), 0)
+    lax.fori_loop(0, jnp.where(clear, 0, trips), functools.partial(over_queries, True), 0)
 
 
 def own_kernel(emb_ref, labels_ref, own_out, best_out, reach_out, start, raw, sems):
@@ -198,35 +203,39 @@
     upper([(high_1b, 1, 1), (high_3a, 3, 0)], both, up, rep, high_out)
 
 
-def far_parts(reach_ref, side, low, across, side_a, side_b):
-    half, rows = TILE, 8 * TILE
-    rep, up, both = both_keys(reach_ref, low, across)
-    at = rep * 2 * half
-    sides = [
-        key_piece(side_a, side[1], rows, at + half, half),
-        key_piece(side_b, side[1], rows, at, half),
-    ]
-    return rep, lax.axis_index("shard") % 2 == 0, up, both, [(side, sides)]
+def side_keys(side, sides_ref):
+    quarter, rows = 2 * TILE, 8 * TILE
+    at = lax.axis_index("rep") * quarter
+    return [(side, [key_piece(sides_ref, side[1], rows, at, quarter)])]
 
 
 def far_kernel(reach_ref, prior_ref, low, across, high_0a, high_0b, high_1a, high_1b, high_2a,
-               high_2b, high_3a, side_a, side_b, high_out, side_out):
+               high_2b, high_3a, side_a, side_b, high_out, side_out, sides_out):
+    half = TILE
+    even = lax.axis_index("shard") % 2 == 0
     side = read_reach(side_a, 3)
     side_out[0], side_out[1] = side
-    rep, even, up, both, sides = far_parts(reach_ref, side, low, across, side_a, side_b)
+
+    @pl.when(even)
+    def _():
+        sides_out[pl.ds(0, half), :] = side_b[pl.ds(0, half), :]
+        sides_out[pl.ds(half, half), :] = side_a[pl.ds(0, half), :]
+
+    rep, up, both = both_keys(reach_ref, low, across)
     high_out[...] = prior_ref[...]
     upper([(high_2b, 2, 1)], both, up, rep, high_out)
     pieces = [(high_0a, 0, 0), (high_0b, 0, 1), (high_1a, 1, 0), (high_1b, 1, 1), (high_2a, 2, 0)]
     pieces += [(high_2b, 2, 1), (high_3a, 3, 0)]
-    upper(pieces, sides, up, rep, high_out, even)
-
-
-def last_kernel(reach_ref, side_ref, prior_ref, low, across, high_3b, side_a, side_b, high_out):
+    upper(pieces, side_keys(side, sides_out), up, rep, high_out, even)
+
+
+def last_kernel(reach_ref, side_ref, prior_ref, low, across, high_3b, sides, high_out):
     side = (side_ref[0], side_ref[1])
-    rep, even, up, both, sides = far_parts(reach_ref, side, low, across, side_a, side_b)
+    even = lax.axis_index("shard") % 2 == 0
+    rep, up, both = both_keys(reach_ref, low, across)
     high_out[...] = prior_ref[...]
     upper([(high_3b, 3, 1)], both, up, rep, high_out)
-    upper([(high_3b, 3, 1)], sides, up, rep, high_out, even)
+    upper([(high_3b, 3, 1)], side_keys(side, sides), up, rep, high_out, even)
 
 
 def local(embeddings, labels):
@@ -304,11 +313,11 @@
     )(embeddings, own_labels[None, :])
 
     across, low, own, best = fence((across, low, own, best))
-    side_b = along_shard(across[:half], 2, even_only)
+    side_b = along_shard(across[: half + INFO], 2, even_only)
     side_a = along_shard(low[half:], -1, odd_only)
     high_0b, high_1a, high_2a, across, low = fence((high_0b, high_1a, high_2a, across, low))
     high_2b = other_rep(high_0b, 2)
-    high_1b = other_rep(high_0b, 1)
+    high_1b = other_rep(high_0b[:half], 1)
     high_3a = other_rep(high_2a, 1)
     line = ((1, rows), F32)
     best, of_high, reach = call(
@@ -322,14 +331,15 @@
     )
     high_2b, side_a, side_b, of_high = fence((high_2b, side_a, side_b, of_high))
     high_3b = other_rep(high_2b, 1)
-    of_high, side = call(
-        far_kernel, "far", [line, ((2,), jnp.int32)], [SMEM] + [VMEM] * 13 + [SMEM],
+    of_high, side, sides = call(
+        far_kernel, "far", [line, ((2,), jnp.int32), ((quarter, width), BF16)],
+        [SMEM] + [VMEM] * 13 + [SMEM, VMEM],
         reach, of_high, low, across, high_0a, high_0b, high_1a, high_1b, high_2a, high_2b,
         high_3a, side_a, side_b,
     )
     (of_high,) = call(
-        last_kernel, "last", [line], [SMEM] * 2 + [VMEM] * 7,
-        reach, side, of_high, low, across, high_3b, side_a, side_b,
+        last_kernel, "last", [line], [SMEM] * 2 + [VMEM] * 6,
+        reach, side, of_high, low, across, high_3b, sides,
     )
 
     above = along_shard(of_high, 2)

time: 70.4 us -> 69.8 us (level)
  starting transfers between devices: 26.8 us -> 21.6 us
  Pallas kernels: 15.4 us -> 19.6 us
    ppermute x6, starting transfers between devices: 20 us -> 14.5 us  [along_shard(): return lax.ppermute(block, 'shard', route)]
    pallas_call x4, Pallas kernels: 7.9 us -> 12.1 us  [call(): pl.pallas_call(kernel, out_shape=[jax.ShapeDtypeStruct(shape, dtype) for...]
    ppermute x9, waiting for transfers between devices: 2.16 us -> 3.9 us  [other_rep(): return lax.ppermute(block, 'rep', [(i, i ^ flip) for i in range(reps)])]
    ppermute x6, waiting for transfers between devices: 23.9 us -> 22.2 us  [along_shard(): return lax.ppermute(block, 'shard', route)]
  transfers between devices with their start and end apart: 16 -> 16, of which waited for: 7 -> 9; matrix products, arithmetic and copies ran while one was open for 0% -> 0% of each run, Pallas kernels for 18% -> 24%
where the time goes in v7:
time: 69.8 us; the launch traced here: 69 us
  waiting for transfers between devices  26.1 us (37%)
  starting transfers between devices  21.6 us (31%)
  Pallas kernels  19.6 us (28%)
  local copies, waits for them, and re-layouts  0.81 us (1%)
    ppermute x6, waiting for transfers between devices, along_shard(): return lax.ppermute(block, 'shard', route)  22.2 us
    ppermute x6, starting transfers between devices, along_shard(): return lax.ppermute(block, 'shard', route)  14.5 us
    pallas_call x4, Pallas kernels, call(): pl.pallas_call(kernel, out_shape=[jax.ShapeDtypeStruct(shape, dtype) for...  12.1 us
    pallas_call x1, Pallas kernels, local(): pl.pallas_call(own_kernel, out_shape=[jax.ShapeDtypeStruct((rows, width),...  6.02 us
    ppermute x9, starting transfers between devices, other_rep(): return lax.ppermute(block, 'rep', [(i, i ^ flip) for i in range(reps)])  5.55 us
    ppermute x9, waiting for transfers between devices, other_rep(): return lax.ppermute(block, 'rep', [(i, i ^ flip) for i in range(reps)])  3.9 us
    ppermute x1, starting transfers between devices, partner(): return lax.ppermute(block, 'shard', [(i, i ^ 1) for i in range(shards)])  1.58 us
    pallas_call x1, Pallas kernels, local(): pl.pallas_call(prepare_kernel, out_shape=[jax.ShapeDtypeStruct((size, wid...  1.47 us
  transfers between devices with their start and end apart: 16, of which 9 were waited for; matrix products, arithmetic and copies ran while one was open for 0% of the time, Pallas kernels for 24%

profile of v7, /device:TPU:8, one launch (start us, length us, event | category | flops | bytes accessed | tf_op | source)
XLA Modules:
  0.0 69.0 jit_solution(1898941610898845984)
XLA Ops:
  0.7 1.5 %prepare.1 = (bf16[256,1024]{1,0:T(8,128)(2,1)S(1)}, bf16[272,1024]{1,0:T(8,128)(2,1)S(1)}, bf16[528,1024]{1,0:T(8,128)(2,1)S(1)}) custom-call(bf16[2048,1024]{1,0:T(8,128)(2,1)} %emb_ref.3, s32[16,128]{1,0:T(8,128)S(1)} %bitcast.3), custom_call_target="tpu_custom_call" | custom-call | tf_op jit(solution)/shard_map/prepare/pallas_call | solution.py:271
  2.2 3.5 %collective-permute-start.2 = (bf16[528,1024]{1,0:T(8,128)(2,1)S(1)}, bf16[528,1024]{1,0:T(8,128)(2,1)S(1)}, u32[]{:S(2)}, u32[]{:S(2)}) collective-permute-start(bf16[528,1024]{1,0:T(8,128)(2,1)S(1)} %get-tuple-element.35), channel_id=1, source_target_pairs={{0,8},{4,12},{8,16},{12,20},{16,24},{20,28},{1,9},{5,13},{9,17},{1... | collective-permute-start | bytes 3244040 | tf_op jit(solution)/shard_map/ppermute | solution.py:251
  5.7 1.6 %collective-permute-start.1 = (bf16[528,1024]{1,0:T(8,128)(2,1)S(1)}, bf16[528,1024]{1,0:T(8,128)(2,1)S(1)}, u32[]{:S(2)}, u32[]{:S(2)}) collective-permute-start(bf16[528,1024]{1,0:T(8,128)(2,1)S(1)} %get-tuple-element.35), channel_id=1, source_target_pairs={{0,4},{4,0},{8,12},{12,8},{16,20},{20,16},{24,28},{28,24},{1,5},{5... | collective-permute-start | bytes 3244040 | tf_op jit(solution)/shard_map/ppermute | solution.py:254
  7.3 2.4 %collective-permute-start = (bf16[256,1024]{1,0:T(8,128)(2,1)S(1)}, bf16[256,1024]{1,0:T(8,128)(2,1)S(1)}, u32[]{:S(2)}, u32[]{:S(2)}) collective-permute-start(bf16[256,1024]{1,0:T(8,128)(2,1)S(1)} %get-tuple-element.32), channel_id=1, source_target_pairs={{8,0},{12,4},{16,8},{20,12},{24,16},{28,20},{9,1},{13,5},{17,9},{2... | collective-permute-start | bytes 1572872 | tf_op jit(solution)/shard_map/ppermute | solution.py:251
  9.7 1.9 %collective-permute-start.3 = (bf16[272,1024]{1,0:T(8,128)(2,1)S(1)}, bf16[272,1024]{1,0:T(8,128)(2,1)S(1)}, u32[]{:S(2)}, u32[]{:S(2)}) collective-permute-start(bf16[272,1024]{1,0:T(8,128)(2,1)S(1)} %get-tuple-element.40), channel_id=1, source_target_pairs={{8,0},{12,4},{16,8},{20,12},{24,16},{28,20},{9,1},{13,5},{17,9},{2... | collective-permute-start | bytes 1671176 | tf_op jit(solution)/shard_map/ppermute | solution.py:251
  11.6 12.4 %collective-permute-done.high_0a = bf16[256,1024]{1,0:T(8,128)(2,1)S(1)} collective-permute-done((bf16[256,1024]{1,0:T(8,128)(2,1)S(1)}, bf16[256,1024]{1,0:T(8,128)(2,1)S(1)}, u32[]{:S(2)}, u32[]{:S(2)}) %collective-permute-start) | collective-permute-done | bytes 524320 | tf_op jit(solution)/shard_map/ppermute | solution.py:251
  24.0 1.5 %collective-permute-start.5 = (bf16[256,1024]{1,0:T(8,128)(2,1)S(1)}, bf16[256,1024]{1,0:T(8,128)(2,1)S(1)}, u32[]{:S(2)}, u32[]{:S(2)}) collective-permute-start(bf16[256,1024]{1,0:T(8,128)(2,1)S(1)} %collective-permute-done.high_0a), channel_id=1, source_target_pairs={{0,2},{1,3},{2,0},{3,1},{4,6},{5,7},{6,4},{7,5},{8,10},{9,11},{10,... | collective-permute-start | bytes 1572872 | tf_op jit(solution)/shard_map/ppermute | solution.py:257
  25.5 6.0 %own.1 = (bf16[2048,1024]{1,0:T(8,128)(2,1)S(1)}, f32[1,2048]{1,0:T(1,128)S(1)}, s32[2]{0:T(128)S(1)}) custom-call(bf16[2048,1024]{1,0:T(8,128)(2,1)} %emb_ref.3, s32[1,2048]{1,0:T(1,128)S(1)} %bitcast.4), custom_call_target="tpu_custom_call" | custom-call | flops 1024 | bytes 1024 | tf_op jit(solution)/shard_map/own/pallas_call | solution.py:296
  31.6 2.5 %collective-permute-done.3.high_0b = bf16[272,1024]{1,0:T(8,128)(2,1)S(1)} collective-permute-done((bf16[272,1024]{1,0:T(8,128)(2,1)S(1)}, bf16[272,1024]{1,0:T(8,128)(2,1)S(1)}, u32[]{:S(2)}, u32[]{:S(2)}) %collective-permute-start.3) | collective-permute-done | bytes 557088 | tf_op jit(solution)/shard_map/ppermute | solution.py:251
  34.4 1.3 %collective-permute-start.7 = (bf16[272,1024]{1,0:T(8,128)(2,1)S(1)}, bf16[272,1024]{1,0:T(8,128)(2,1)S(1)}, u32[]{:S(2)}, u32[]{:S(2)}) collective-permute-start(bf16[272,1024]{1,0:T(8,128)(2,1)S(1)} %slice.9), channel_id=1, source_target_pairs={{4,0},{12,8},{20,16},{28,24},{5,1},{13,9},{21,17},{29,25},{6,2},{1... | collective-permute-start | bytes 1671176 | tf_op jit(solution)/shard_map/ppermute | solution.py:251
  35.7 3.5 %collective-permute-start.8 = (bf16[272,1024]{1,0:T(8,128)(2,1)S(1)}, bf16[272,1024]{1,0:T(8,128)(2,1)S(1)}, u32[]{:S(2)}, u32[]{:S(2)}) collective-permute-start(bf16[272,1024]{1,0:T(8,128)(2,1)S(1)} %slice.10), channel_id=1, source_target_pairs={{0,8},{8,16},{16,24},{1,9},{9,17},{17,25},{2,10},{10,18},{18,26},{... | collective-permute-start | bytes 1671176 | tf_op jit(solution)/shard_map/ppermute | solution.py:251
  39.2 1.6 %collective-permute-start.6 = (bf16[272,1024]{1,0:T(8,128)(2,1)S(1)}, bf16[272,1024]{1,0:T(8,128)(2,1)S(1)}, u32[]{:S(2)}, u32[]{:S(2)}) collective-permute-start(bf16[272,1024]{1,0:T(8,128)(2,1)S(1)} %collective-permute-done.3.high_0b), channel_id=1, source_target_pairs={{0,2},{1,3},{2,0},{3,1},{4,6},{5,7},{6,4},{7,5},{8,10},{9,11},{10,... | collective-permute-start | bytes 1671176 | tf_op jit(solution)/shard_map/ppermute | solution.py:257
  41.4 3.4 %near.1 = (f32[1,2048]{1,0:T(1,128)S(1)}, f32[1,2048]{1,0:T(1,128)S(1)}, s32[6]{0:T(128)S(1)}) custom-call(s32[2]{0:T(128)S(1)} %get-tuple-element.34.own_reach, bf16[2048,1024]{1,0:T(8,128)(2,1)S(1)} %get-tuple-element.38.own_ref, f32[1,2048]{1,0:T(1,128)S(1)} %get-tuple-element.39.best_ref, bf16[528,1024]{1,0:T(8,128)(2,1)S(1)} %collective-permute-done.2.low, ...), custom_call_target="tpu_custom_call" | custom-call | flops 1024 | bytes 1024 | tf_op jit(solution)/shard_map/near/pallas_call | solution.py:260
  44.8 1.8 %middle.1.prior_ref = f32[1,2048]{1,0:T(1,128)S(1)} custom-call(s32[6]{0:T(128)S(1)} %get-tuple-element.50.reach_ref, f32[1,2048]{1,0:T(1,128)S(1)} %get-tuple-element.51.prior_ref, bf16[528,1024]{1,0:T(8,128)(2,1)S(1)} %collective-permute-done.2.low, bf16[528,1024]{1,0:T(8,128)(2,1)S(1)} %collective-permute-done.1.across, ...), custom_call_target="tpu_custom_call" | custom-call | flops 1024 | bytes 1024 | tf_op jit(solution)/shard_map/middle/pallas_call | solution.py:260
  46.6 2.4 %collective-permute-done.7.side_a = bf16[272,1024]{1,0:T(8,128)(2,1)S(1)} collective-permute-done((bf16[272,1024]{1,0:T(8,128)(2,1)S(1)}, bf16[272,1024]{1,0:T(8,128)(2,1)S(1)}, u32[]{:S(2)}, u32[]{:S(2)}) %collective-permute-start.7) | collective-permute-done | bytes 557088 | tf_op jit(solution)/shard_map/ppermute | solution.py:251
  48.9 1.3 %collective-permute-done.8.side_b = bf16[272,1024]{1,0:T(8,128)(2,1)S(1)} collective-permute-done((bf16[272,1024]{1,0:T(8,128)(2,1)S(1)}, bf16[272,1024]{1,0:T(8,128)(2,1)S(1)}, u32[]{:S(2)}, u32[]{:S(2)}) %collective-permute-start.8) | collective-permute-done | bytes 557088 | tf_op jit(solution)/shard_map/ppermute | solution.py:251
  50.2 1.4 %collective-permute-done.6.high_2b = bf16[272,1024]{1,0:T(8,128)(2,1)S(1)} collective-permute-done((bf16[272,1024]{1,0:T(8,128)(2,1)S(1)}, bf16[272,1024]{1,0:T(8,128)(2,1)S(1)}, u32[]{:S(2)}, u32[]{:S(2)}) %collective-permute-start.6) | collective-permute-done | bytes 557088 | tf_op jit(solution)/shard_map/ppermute | solution.py:257
  51.6 5.3 %far.1 = (f32[1,2048]{1,0:T(1,128)S(1)}, s32[2]{0:T(128)S(1)}, bf16[512,1024]{1,0:T(8,128)(2,1)S(1)}) custom-call(s32[6]{0:T(128)S(1)} %get-tuple-element.50.reach_ref, f32[1,2048]{1,0:T(1,128)S(1)} %middle.1.prior_ref, bf16[528,1024]{1,0:T(8,128)(2,1)S(1)} %collective-permute-done.2.low, bf16[528,1024]{1,0:T(8,128)(2,1)S(1)} %collective-permute-done.1.across, ...), custom_call_target="tpu_custom_call" | custom-call | flops 1024 | bytes 1024 | tf_op jit(solution)/shard_map/far/pallas_call | solution.py:260
  57.0 1.6 %last.1 = f32[1,2048]{1,0:T(1,128)S(1)} custom-call(s32[6]{0:T(128)S(1)} %get-tuple-element.50.reach_ref, s32[2]{0:T(128)S(1)} %get-tuple-element.56.side_ref, f32[1,2048]{1,0:T(1,128)S(1)} %get-tuple-element.57.prior_ref, bf16[528,1024]{1,0:T(8,128)(2,1)S(1)} %collective-permute-done.2.low, bf16[528,1024]{1,0:T(8,128)(2,1)S(1)} %collective-permute-done.1.across, ...), custom_call_target="tpu_custom_call" | custom-call | flops 1024 | bytes 1024 | tf_op jit(solution)/shard_map/last/pallas_call | solution.py:260
  58.6 1.9 %collective-permute-start.12 = (f32[1,2048]{1,0:T(1,128)S(1)}, f32[1,2048]{1,0:T(1,128)S(1)}, u32[]{:S(2)}, u32[]{:S(2)}) collective-permute-start(f32[1,2048]{1,0:T(1,128)S(1)} %last.1), channel_id=1, source_target_pairs={{0,8},{4,12},{8,16},{12,20},{16,24},{20,28},{1,9},{5,13},{9,17},{1... | collective-permute-start | bytes 24584 | tf_op jit(solution)/shard_map/ppermute | solution.py:251
  60.5 3.6 %collective-permute-done.12 = f32[1,2048]{1,0:T(1,128)S(1)} collective-permute-done((f32[1,2048]{1,0:T(1,128)S(1)}, f32[1,2048]{1,0:T(1,128)S(1)}, u32[]{:S(2)}, u32[]{:S(2)}) %collective-permute-start.12) | collective-permute-done | bytes 8224 | tf_op jit(solution)/shard_map/ppermute | solution.py:251
  64.7 1.1 %collective-permute-start.14 = (f32[1,2048]{1,0:T(1,128)S(1)}, f32[1,2048]{1,0:T(1,128)S(1)}, u32[]{:S(2)}, u32[]{:S(2)}) collective-permute-start(f32[1,2048]{1,0:T(1,128)S(1)} %fusion), channel_id=1, source_target_pairs={{0,2},{1,3},{2,0},{3,1},{4,6},{5,7},{6,4},{7,5},{8,10},{9,11},{10,... | collective-permute-start | bytes 24584 | tf_op jit(solution)/shard_map/ppermute | solution.py:257
  66.1 1.3 %collective-permute-done.15 = f32[1,2048]{1,0:T(1,128)S(1)} collective-permute-done((f32[1,2048]{1,0:T(1,128)S(1)}, f32[1,2048]{1,0:T(1,128)S(1)}, u32[]{:S(2)}, u32[]{:S(2)}) %collective-permute-start.15) | collective-permute-done | bytes 8224 | tf_op jit(solution)/shard_map/ppermute | solution.py:257
  67.3 1.0 %collective-permute-done.14 = f32[1,2048]{1,0:T(1,128)S(1)} collective-permute-done((f32[1,2048]{1,0:T(1,128)S(1)}, f32[1,2048]{1,0:T(1,128)S(1)}, u32[]{:S(2)}, u32[]{:S(2)}) %collective-permute-start.14) | collective-permute-done | bytes 8224 | tf_op jit(solution)/shard_map/ppermute | solution.py:257
  (23 shorter events, 3.1 us)
Async XLA Ops:
  0.0 0.7 %copy-start = (s32[2048]{0:T(1024)S(1)}, s32[2048]{0:T(1024)}, u32[]{:S(2)}) copy-start(s32[2048]{0:T(1024)} %param.3) | copy-start | bytes 24580
  0.7 24.8 %copy-start.1 = (s32[2048]{0:T(1024)S(1)}, s32[2048]{0:T(1024)}, u32[]{:S(2)}) copy-start(s32[2048]{0:T(1024)} %param.3) | copy-start | bytes 24580
  2.2 29.3 %collective-permute-start.2 = (bf16[528,1024]{1,0:T(8,128)(2,1)S(1)}, bf16[528,1024]{1,0:T(8,128)(2,1)S(1)}, u32[]{:S(2)}, u32[]{:S(2)}) collective-permute-start(bf16[528,1024]{1,0:T(8,128)(2,1)S(1)} %get-tuple-element.35), channel_id=1, source_target_pairs={{0,8},{4,12},{8,16},{12,20},{16,24},{20,28},{1,9},{5,13},{9,17},{1... | collective-permute-start | bytes 3244040 | tf_op jit(solution)/shard_map/ppermute | solution.py:251
  5.7 25.9 %collective-permute-start.1 = (bf16[528,1024]{1,0:T(8,128)(2,1)S(1)}, bf16[528,1024]{1,0:T(8,128)(2,1)S(1)}, u32[]{:S(2)}, u32[]{:S(2)}) collective-permute-start(bf16[528,1024]{1,0:T(8,128)(2,1)S(1)} %get-tuple-element.35), channel_id=1, source_target_pairs={{0,4},{4,0},{8,12},{12,8},{16,20},{20,16},{24,28},{28,24},{1,5},{5... | collective-permute-start | bytes 3244040 | tf_op jit(solution)/shard_map/ppermute | solution.py:254
  7.3 16.7 %collective-permute-start = (bf16[256,1024]{1,0:T(8,128)(2,1)S(1)}, bf16[256,1024]{1,0:T(8,128)(2,1)S(1)}, u32[]{:S(2)}, u32[]{:S(2)}) collective-permute-start(bf16[256,1024]{1,0:T(8,128)(2,1)S(1)} %get-tuple-element.32), channel_id=1, source_target_pairs={{8,0},{12,4},{16,8},{20,12},{24,16},{28,20},{9,1},{13,5},{17,9},{2... | collective-permute-start | bytes 1572872 | tf_op jit(solution)/shard_map/ppermute | solution.py:251
  9.7 24.5 %collective-permute-start.3 = (bf16[272,1024]{1,0:T(8,128)(2,1)S(1)}, bf16[272,1024]{1,0:T(8,128)(2,1)S(1)}, u32[]{:S(2)}, u32[]{:S(2)}) collective-permute-start(bf16[272,1024]{1,0:T(8,128)(2,1)S(1)} %get-tuple-element.40), channel_id=1, source_target_pairs={{8,0},{12,4},{16,8},{20,12},{24,16},{28,20},{9,1},{13,5},{17,9},{2... | collective-permute-start | bytes 1671176 | tf_op jit(solution)/shard_map/ppermute | solution.py:251
  24.0 10.4 %collective-permute-start.5 = (bf16[256,1024]{1,0:T(8,128)(2,1)S(1)}, bf16[256,1024]{1,0:T(8,128)(2,1)S(1)}, u32[]{:S(2)}, u32[]{:S(2)}) collective-permute-start(bf16[256,1024]{1,0:T(8,128)(2,1)S(1)} %collective-permute-done.high_0a), channel_id=1, source_target_pairs={{0,2},{1,3},{2,0},{3,1},{4,6},{5,7},{6,4},{7,5},{8,10},{9,11},{10,... | collective-permute-start | bytes 1572872 | tf_op jit(solution)/shard_map/ppermute | solution.py:257
  25.5 8.9 %collective-permute-start.4 = (bf16[256,1024]{1,0:T(8,128)(2,1)S(1)}, bf16[256,1024]{1,0:T(8,128)(2,1)S(1)}, u32[]{:S(2)}, u32[]{:S(2)}) collective-permute-start(bf16[256,1024]{1,0:T(8,128)(2,1)S(1)} %collective-permute-done.high_0a), channel_id=1, source_target_pairs={{0,1},{1,0},{2,3},{3,2},{4,5},{5,4},{6,7},{7,6},{8,9},{9,8},{10,11... | collective-permute-start | bytes 1572872 | tf_op jit(solution)/shard_map/ppermute | solution.py:257
  34.4 14.5 %collective-permute-start.7 = (bf16[272,1024]{1,0:T(8,128)(2,1)S(1)}, bf16[272,1024]{1,0:T(8,128)(2,1)S(1)}, u32[]{:S(2)}, u32[]{:S(2)}) collective-permute-start(bf16[272,1024]{1,0:T(8,128)(2,1)S(1)} %slice.9), channel_id=1, source_target_pairs={{4,0},{12,8},{20,16},{28,24},{5,1},{13,9},{21,17},{29,25},{6,2},{1... | collective-permute-start | bytes 1671176 | tf_op jit(solution)/shard_map/ppermute | solution.py:251
  35.7 14.5 %collective-permute-start.8 = (bf16[272,1024]{1,0:T(8,128)(2,1)S(1)}, bf16[272,1024]{1,0:T(8,128)(2,1)S(1)}, u32[]{:S(2)}, u32[]{:S(2)}) collective-permute-start(bf16[272,1024]{1,0:T(8,128)(2,1)S(1)} %slice.10), channel_id=1, source_target_pairs={{0,8},{8,16},{16,24},{1,9},{9,17},{17,25},{2,10},{10,18},{18,26},{... | collective-permute-start | bytes 1671176 | tf_op jit(solution)/shard_map/ppermute | solution.py:251
  39.2 12.4 %collective-permute-start.6 = (bf16[272,1024]{1,0:T(8,128)(2,1)S(1)}, bf16[272,1024]{1,0:T(8,128)(2,1)S(1)}, u32[]{:S(2)}, u32[]{:S(2)}) collective-permute-start(bf16[272,1024]{1,0:T(8,128)(2,1)S(1)} %collective-permute-done.3.high_0b), channel_id=1, source_target_pairs={{0,2},{1,3},{2,0},{3,1},{4,6},{5,7},{6,4},{7,5},{8,10},{9,11},{10,... | collective-permute-start | bytes 1671176 | tf_op jit(solution)/shard_map/ppermute | solution.py:257
  40.8 4.0 %collective-permute-start.9 = (bf16[256,1024]{1,0:T(8,128)(2,1)S(1)}, bf16[256,1024]{1,0:T(8,128)(2,1)S(1)}, u32[]{:S(2)}, u32[]{:S(2)}) collective-permute-start(bf16[256,1024]{1,0:T(8,128)(2,1)S(1)} %slice.11), channel_id=1, source_target_pairs={{0,1},{1,0},{2,3},{3,2},{4,5},{5,4},{6,7},{7,6},{8,9},{9,8},{10,11... | collective-permute-start | bytes 1572872 | tf_op jit(solution)/shard_map/ppermute | solution.py:257
  40.9 3.9 %collective-permute-start.10 = (bf16[256,1024]{1,0:T(8,128)(2,1)S(1)}, bf16[256,1024]{1,0:T(8,128)(2,1)S(1)}, u32[]{:S(2)}, u32[]{:S(2)}) collective-permute-start(bf16[256,1024]{1,0:T(8,128)(2,1)S(1)} %collective-permute-done.5.high_2a), channel_id=1, source_target_pairs={{0,1},{1,0},{2,3},{3,2},{4,5},{5,4},{6,7},{7,6},{8,9},{9,8},{10,11... | collective-permute-start | bytes 1572872 | tf_op jit(solution)/shard_map/ppermute | solution.py:257
  51.6 5.4 %collective-permute-start.11 = (bf16[272,1024]{1,0:T(8,128)(2,1)S(1)}, bf16[272,1024]{1,0:T(8,128)(2,1)S(1)}, u32[]{:S(2)}, u32[]{:S(2)}) collective-permute-start(bf16[272,1024]{1,0:T(8,128)(2,1)S(1)} %collective-permute-done.6.high_2b), channel_id=1, source_target_pairs={{0,1},{1,0},{2,3},{3,2},{4,5},{5,4},{6,7},{7,6},{8,9},{9,8},{10,11... | collective-permute-start | bytes 1671176 | tf_op jit(solution)/shard_map/ppermute | solution.py:257
  58.6 5.5 %collective-permute-start.12 = (f32[1,2048]{1,0:T(1,128)S(1)}, f32[1,2048]{1,0:T(1,128)S(1)}, u32[]{:S(2)}, u32[]{:S(2)}) collective-permute-start(f32[1,2048]{1,0:T(1,128)S(1)} %last.1), channel_id=1, source_target_pairs={{0,8},{4,12},{8,16},{12,20},{16,24},{20,28},{1,9},{5,13},{9,17},{1... | collective-permute-start | bytes 24584 | tf_op jit(solution)/shard_map/ppermute | solution.py:251
  64.2 3.2 %collective-permute-start.15 = (f32[1,2048]{1,0:T(1,128)S(1)}, f32[1,2048]{1,0:T(1,128)S(1)}, u32[]{:S(2)}, u32[]{:S(2)}) collective-permute-start(f32[1,2048]{1,0:T(1,128)S(1)} %fusion), channel_id=1, source_target_pairs={{0,3},{1,2},{2,1},{3,0},{4,7},{5,6},{6,5},{7,4},{8,11},{9,10},{10,... | collective-permute-start | bytes 24584 | tf_op jit(solution)/shard_map/ppermute | solution.py:257
  64.7 3.7 %collective-permute-start.14 = (f32[1,2048]{1,0:T(1,128)S(1)}, f32[1,2048]{1,0:T(1,128)S(1)}, u32[]{:S(2)}, u32[]{:S(2)}) collective-permute-start(f32[1,2048]{1,0:T(1,128)S(1)} %fusion), channel_id=1, source_target_pairs={{0,2},{1,3},{2,0},{3,1},{4,6},{5,7},{6,4},{7,5},{8,10},{9,11},{10,... | collective-permute-start | bytes 24584 | tf_op jit(solution)/shard_map/ppermute | solution.py:257
  65.8 2.6 %collective-permute-start.13 = (f32[1,2048]{1,0:T(1,128)S(1)}, f32[1,2048]{1,0:T(1,128)S(1)}, u32[]{:S(2)}, u32[]{:S(2)}) collective-permute-start(f32[1,2048]{1,0:T(1,128)S(1)} %fusion), channel_id=1, source_target_pairs={{0,1},{1,0},{2,3},{3,2},{4,5},{5,4},{6,7},{7,6},{8,9},{9,8},{10,11... | collective-permute-start | bytes 24584 | tf_op jit(solution)/shard_map/ppermute | solution.py:257

commit v8 on v7

--- a/solution.py
+++ b/solution.py
@@ -165,20 +165,31 @@
             group(several, ref, half, out_ref, at, count)
 
 
-def near_kernel(own_reach, own_ref, best_ref, low, across, high_0a, high_0b, high_1a, high_2a,
-                best_out, high_out, reach_out):
+def lower_kernel(own_reach, own_ref, best_ref, low, best_out, lower_out):
+    rows = own_ref.shape[0]
+    quarter = low.shape[0] - INFO
+    lower = read_reach(low, 3)
+    lower_out[0], lower_out[1] = lower
+    best_out[...] = best_ref[...]
+    lows = [key_piece(low, lower[1], rows, lax.axis_index("rep") * quarter, quarter)]
+    mine = (own_reach[0], own_reach[1])
+    group(lows, own_ref, rows, best_out, 0, reached(mine, lower, 0, rows))
+
+
+def near_kernel(own_reach, lower_reach, own_ref, best_ref, low, across, high_0a, high_0b, high_1a,
+                high_2a, best_out, high_out, reach_out):
     rows = own_ref.shape[0]
     quarter = across.shape[0] - INFO
     rep, odd = lax.axis_index("rep"), lax.axis_index("shard") % 2
     mine = (own_reach[0], own_reach[1])
-    lower, beside, up = read_reach(low, 3), read_reach(across, 3), read_reach(high_0b, 0)
+    lower = (lower_reach[0], lower_reach[1])
+    beside, up = read_reach(across, 3), read_reach(high_0b, 0)
     for n, value in enumerate(lower + beside + up):
         reach_out[n] = value
     best_out[...] = best_ref[...]
     high_out[...] = jnp.full(high_out.shape, -1.0, F32)
     lows = [key_piece(low, lower[1], rows, rep * quarter, quarter)]
     besides = [key_piece(across, beside[1], rows, rep * quarter, quarter)]
-    group(lows, own_ref, rows, best_out, 0, reached(mine, lower, 0, rows))
     count = jnp.where(odd == 1, reached(mine, beside, 0, rows), 0)
     group(besides, own_ref, rows, best_out, 0, count)
     pieces = [(high_0a, 0, 0), (high_0b, 0, 1), (high_1a, 1, 0), (high_2a, 2, 0)]
@@ -290,9 +301,6 @@
     across = partner(mine)
     high_0b = along_shard(hi, -2)
 
-    high_0a, own_labels = fence((high_0a, labels))
-    high_2a = other_rep(high_0a, 2)
-    high_1a = other_rep(high_0a, 1)
     own, best, own_reach = pl.pallas_call(
         own_kernel,
         out_shape=[
@@ -310,26 +318,35 @@
         compiler_params=pltpu.CompilerParams(vmem_limit_bytes=OWN_LIMIT),
         cost_estimate=pl.CostEstimate(flops=1024, bytes_accessed=1024, transcendentals=0),
         name="own",
-    )(embeddings, own_labels[None, :])
-
-    across, low, own, best = fence((across, low, own, best))
+    )(embeddings, labels[None, :])
+
+    high_0a, own, best = fence((high_0a, own, best))
+    high_2a = other_rep(high_0a, 2)
+    high_1a = other_rep(high_0a, 1)
+    line = ((1, rows), F32)
+    best, lower_reach = call(
+        lower_kernel, "lower", [line, ((2,), jnp.int32)], [SMEM] + [VMEM] * 4 + [SMEM],
+        own_reach, own, best, low,
+    )
+
+    across, low, best = fence((across, low, best))
     side_b = along_shard(across[: half + INFO], 2, even_only)
     side_a = along_shard(low[half:], -1, odd_only)
     high_0b, high_1a, high_2a, across, low = fence((high_0b, high_1a, high_2a, across, low))
     high_2b = other_rep(high_0b, 2)
     high_1b = other_rep(high_0b[:half], 1)
     high_3a = other_rep(high_2a, 1)
-    line = ((1, rows), F32)
     best, of_high, reach = call(
         near_kernel, "near", [line, line, ((6,), jnp.int32)],
-        [SMEM] + [VMEM] * 10 + [SMEM],
-        own_reach, own, best, low, across, high_0a, high_0b, high_1a, high_2a,
-    )
+        [SMEM] * 2 + [VMEM] * 10 + [SMEM],
+        own_reach, lower_reach, own, best, low, across, high_0a, high_0b, high_1a, high_2a,
+    )
+    best_1 = other_rep(best, 1)
     (of_high,) = call(
         middle_kernel, "middle", [line], [SMEM] + [VMEM] * 6,
         reach, of_high, low, across, high_1b, high_3a,
     )
-    high_2b, side_a, side_b, of_high = fence((high_2b, side_a, side_b, of_high))
+    high_2b, side_a, side_b, of_high, best_1 = fence((high_2b, side_a, side_b, of_high, best_1))
     high_3b = other_rep(high_2b, 1)
     of_high, side, sides = call(
         far_kernel, "far", [line, ((2,), jnp.int32), ((quarter, width), BF16)],
@@ -343,9 +360,13 @@
     )
 
     above = along_shard(of_high, 2)
-    best = jnp.maximum(best, jnp.where(lax.axis_index("shard") >= 2, above, -1.0))
-    others = [other_rep(best, flip) for flip in range(1, reps)]
-    return functools.reduce(jnp.maximum, others, best)[0]
+    route = [
+        (i * reps + j, (i + 2) * reps + (j ^ 1)) for i in range(shards - 2) for j in range(reps)
+    ]
+    above = jnp.maximum(above, lax.ppermute(of_high, ("shard", "rep"), route))
+    above = jnp.where(lax.axis_index("shard") >= 2, above, -1.0)
+    best = jnp.maximum(jnp.maximum(best, best_1), above)
+    return jnp.maximum(best, other_rep(best, 2))[0]
 
 
 def solution(mesh):

time: 69.8 us -> 71 us (1.017)
  the two profiles are of different devices: /device:TPU:8 before, /device:TPU:0 now
where the time goes in v8:
time: 71 us; the launch traced here: 69.7 us
  starting transfers between devices  26.9 us (38%)
  waiting for transfers between devices  23.4 us (33%)
  Pallas kernels  17.7 us (25%)
  local copies, waits for them, and re-layouts  0.81 us (1%)
    ppermute x6, waiting for transfers between devices, along_shard(): return lax.ppermute(block, 'shard', route)  18.9 us
    ppermute x6, starting transfers between devices, along_shard(): return lax.ppermute(block, 'shard', route)  14.1 us
    pallas_call x5, Pallas kernels, call(): pl.pallas_call(kernel, out_shape=[jax.ShapeDtypeStruct(shape, dtype) for...  10.2 us
    ppermute x8, starting transfers between devices, other_rep(): return lax.ppermute(block, 'rep', [(i, i ^ flip) for i in range(reps)])  7.26 us
    pallas_call x1, Pallas kernels, local(): pl.pallas_call(own_kernel, out_shape=[jax.ShapeDtypeStruct((rows, width),...  6.02 us
    ppermute x8, waiting for transfers between devices, other_rep(): return lax.ppermute(block, 'rep', [(i, i ^ flip) for i in range(reps)])  4.2 us
    ppermute x1, starting transfers between devices, local(): above = jnp.maximum(above, lax.ppermute(of_high, ('shard', 'rep'), route))  3.96 us
    ppermute x1, starting transfers between devices, partner(): return lax.ppermute(block, 'shard', [(i, i ^ 1) for i in range(shards)])  1.58 us
  transfers between devices with their start and end apart: 16, of which 10 were waited for; matrix products, arithmetic and copies ran while one was open for 0% of the time, Pallas kernels for 22%

profile of v8, /device:TPU:0, one launch (start us, length us, event | category | flops | bytes accessed | tf_op | source)
XLA Modules:
  0.0 69.7 jit_solution(11934893496839954150)
XLA Ops:
  0.7 1.5 %prepare.1 = (bf16[256,1024]{1,0:T(8,128)(2,1)S(1)}, bf16[272,1024]{1,0:T(8,128)(2,1)S(1)}, bf16[528,1024]{1,0:T(8,128)(2,1)S(1)}) custom-call(bf16[2048,1024]{1,0:T(8,128)(2,1)} %emb_ref.3, s32[16,128]{1,0:T(8,128)S(1)} %bitcast.3), custom_call_target="tpu_custom_call" | custom-call | tf_op jit(solution)/shard_map/prepare/pallas_call | solution.py:282
  2.2 5.0 %collective-permute-start.1 = (bf16[528,1024]{1,0:T(8,128)(2,1)S(1)}, bf16[528,1024]{1,0:T(8,128)(2,1)S(1)}, u32[]{:S(2)}, u32[]{:S(2)}) collective-permute-start(bf16[528,1024]{1,0:T(8,128)(2,1)S(1)} %get-tuple-element.41), channel_id=1, source_target_pairs={{0,8},{4,12},{8,16},{12,20},{16,24},{20,28},{1,9},{5,13},{9,17},{1... | collective-permute-start | bytes 3244040 | tf_op jit(solution)/shard_map/ppermute | solution.py:262
  7.2 1.6 %collective-permute-start.2 = (bf16[528,1024]{1,0:T(8,128)(2,1)S(1)}, bf16[528,1024]{1,0:T(8,128)(2,1)S(1)}, u32[]{:S(2)}, u32[]{:S(2)}) collective-permute-start(bf16[528,1024]{1,0:T(8,128)(2,1)S(1)} %get-tuple-element.41), channel_id=1, source_target_pairs={{0,4},{4,0},{8,12},{12,8},{16,20},{20,16},{24,28},{28,24},{1,5},{5... | collective-permute-start | bytes 3244040 | tf_op jit(solution)/shard_map/ppermute | solution.py:265
  8.8 1.3 %collective-permute-start = (bf16[256,1024]{1,0:T(8,128)(2,1)S(1)}, bf16[256,1024]{1,0:T(8,128)(2,1)S(1)}, u32[]{:S(2)}, u32[]{:S(2)}) collective-permute-start(bf16[256,1024]{1,0:T(8,128)(2,1)S(1)} %get-tuple-element.36), channel_id=1, source_target_pairs={{8,0},{12,4},{16,8},{20,12},{24,16},{28,20},{9,1},{13,5},{17,9},{2... | collective-permute-start | bytes 1572872 | tf_op jit(solution)/shard_map/ppermute | solution.py:262
  10.1 1.3 %collective-permute-start.3 = (bf16[272,1024]{1,0:T(8,128)(2,1)S(1)}, bf16[272,1024]{1,0:T(8,128)(2,1)S(1)}, u32[]{:S(2)}, u32[]{:S(2)}) collective-permute-start(bf16[272,1024]{1,0:T(8,128)(2,1)S(1)} %get-tuple-element.45), channel_id=1, source_target_pairs={{8,0},{12,4},{16,8},{20,12},{24,16},{28,20},{9,1},{13,5},{17,9},{2... | collective-permute-start | bytes 1671176 | tf_op jit(solution)/shard_map/ppermute | solution.py:262
  11.4 6.0 %own.1 = (bf16[2048,1024]{1,0:T(8,128)(2,1)S(1)}, f32[1,2048]{1,0:T(1,128)S(1)}, s32[2]{0:T(128)S(1)}) custom-call(bf16[2048,1024]{1,0:T(8,128)(2,1)} %emb_ref.3, s32[1,2048]{1,0:T(1,128)S(1)} %bitcast.4), custom_call_target="tpu_custom_call" | custom-call | flops 1024 | bytes 1024 | tf_op jit(solution)/shard_map/own/pallas_call | solution.py:304
  17.4 8.1 %collective-permute-done.high_0a = bf16[256,1024]{1,0:T(8,128)(2,1)S(1)} collective-permute-done((bf16[256,1024]{1,0:T(8,128)(2,1)S(1)}, bf16[256,1024]{1,0:T(8,128)(2,1)S(1)}, u32[]{:S(2)}, u32[]{:S(2)}) %collective-permute-start) | collective-permute-done | bytes 524320 | tf_op jit(solution)/shard_map/ppermute | solution.py:262
  25.5 1.5 %collective-permute-start.5 = (bf16[256,1024]{1,0:T(8,128)(2,1)S(1)}, bf16[256,1024]{1,0:T(8,128)(2,1)S(1)}, u32[]{:S(2)}, u32[]{:S(2)}) collective-permute-start(bf16[256,1024]{1,0:T(8,128)(2,1)S(1)} %collective-permute-done.high_0a), channel_id=1, source_target_pairs={{0,2},{1,3},{2,0},{3,1},{4,6},{5,7},{6,4},{7,5},{8,10},{9,11},{10,... | collective-permute-start | bytes 1572872 | tf_op jit(solution)/shard_map/ppermute | solution.py:268
  27.0 3.2 %collective-permute-done.1.low = bf16[528,1024]{1,0:T(8,128)(2,1)S(1)} collective-permute-done((bf16[528,1024]{1,0:T(8,128)(2,1)S(1)}, bf16[528,1024]{1,0:T(8,128)(2,1)S(1)}, u32[]{:S(2)}, u32[]{:S(2)}) %collective-permute-start.1) | collective-permute-done | bytes 1081376 | tf_op jit(solution)/shard_map/ppermute | solution.py:262
  30.2 2.0 %lower.1 = (f32[1,2048]{1,0:T(1,128)S(1)}, s32[2]{0:T(128)S(1)}) custom-call(s32[2]{0:T(128)S(1)} %get-tuple-element.35.own_reach, bf16[2048,1024]{1,0:T(8,128)(2,1)S(1)} %get-tuple-element.39.own_ref, f32[1,2048]{1,0:T(1,128)S(1)} %get-tuple-element.40.best_ref, bf16[528,1024]{1,0:T(8,128)(2,1)S(1)} %collective-permute-done.1.low), custom_call_target="tpu_custom_call" | custom-call | flops 1024 | bytes 1024 | tf_op jit(solution)/shard_map/lower/pallas_call | solution.py:271
  32.7 3.0 %collective-permute-done.3.high_0b = bf16[272,1024]{1,0:T(8,128)(2,1)S(1)} collective-permute-done((bf16[272,1024]{1,0:T(8,128)(2,1)S(1)}, bf16[272,1024]{1,0:T(8,128)(2,1)S(1)}, u32[]{:S(2)}, u32[]{:S(2)}) %collective-permute-start.3) | collective-permute-done | bytes 557088 | tf_op jit(solution)/shard_map/ppermute | solution.py:262
  35.9 1.3 %collective-permute-start.7 = (bf16[272,1024]{1,0:T(8,128)(2,1)S(1)}, bf16[272,1024]{1,0:T(8,128)(2,1)S(1)}, u32[]{:S(2)}, u32[]{:S(2)}) collective-permute-start(bf16[272,1024]{1,0:T(8,128)(2,1)S(1)} %slice.9), channel_id=1, source_target_pairs={{4,0},{12,8},{20,16},{28,24},{5,1},{13,9},{21,17},{29,25},{6,2},{1... | collective-permute-start | bytes 1671176 | tf_op jit(solution)/shard_map/ppermute | solution.py:262
  37.2 3.5 %collective-permute-start.8 = (bf16[272,1024]{1,0:T(8,128)(2,1)S(1)}, bf16[272,1024]{1,0:T(8,128)(2,1)S(1)}, u32[]{:S(2)}, u32[]{:S(2)}) collective-permute-start(bf16[272,1024]{1,0:T(8,128)(2,1)S(1)} %slice.10), channel_id=1, source_target_pairs={{0,8},{8,16},{16,24},{1,9},{9,17},{17,25},{2,10},{10,18},{18,26},{... | collective-permute-start | bytes 1671176 | tf_op jit(solution)/shard_map/ppermute | solution.py:262
  40.7 1.6 %collective-permute-start.6 = (bf16[272,1024]{1,0:T(8,128)(2,1)S(1)}, bf16[272,1024]{1,0:T(8,128)(2,1)S(1)}, u32[]{:S(2)}, u32[]{:S(2)}) collective-permute-start(bf16[272,1024]{1,0:T(8,128)(2,1)S(1)} %collective-permute-done.3.high_0b), channel_id=1, source_target_pairs={{0,2},{1,3},{2,0},{3,1},{4,6},{5,7},{6,4},{7,5},{8,10},{9,11},{10,... | collective-permute-start | bytes 1671176 | tf_op jit(solution)/shard_map/ppermute | solution.py:268
  42.9 3.4 %near.1 = (f32[1,2048]{1,0:T(1,128)S(1)}, f32[1,2048]{1,0:T(1,128)S(1)}, s32[6]{0:T(128)S(1)}) custom-call(s32[2]{0:T(128)S(1)} %get-tuple-element.35.own_reach, s32[2]{0:T(128)S(1)} %get-tuple-element.42.lower_reach, bf16[2048,1024]{1,0:T(8,128)(2,1)S(1)} %get-tuple-element.39.own_ref, f32[1,2048]{1,0:T(1,128)S(1)} %get-tuple-element.44.best_ref, ...), custom_call_target="tpu_custom_call" | custom-call | flops 1024 | bytes 1024 | tf_op jit(solution)/shard_map/near/pallas_call | solution.py:271
  46.4 1.8 %middle.1.prior_ref = f32[1,2048]{1,0:T(1,128)S(1)} custom-call(s32[6]{0:T(128)S(1)} %get-tuple-element.55.reach_ref, f32[1,2048]{1,0:T(1,128)S(1)} %get-tuple-element.56.prior_ref, bf16[528,1024]{1,0:T(8,128)(2,1)S(1)} %collective-permute-done.1.low, bf16[528,1024]{1,0:T(8,128)(2,1)S(1)} %collective-permute-done.2.across, ...), custom_call_target="tpu_custom_call" | custom-call | flops 1024 | bytes 1024 | tf_op jit(solution)/shard_map/middle/pallas_call | solution.py:271
  48.2 2.3 %collective-permute-done.7.side_a = bf16[272,1024]{1,0:T(8,128)(2,1)S(1)} collective-permute-done((bf16[272,1024]{1,0:T(8,128)(2,1)S(1)}, bf16[272,1024]{1,0:T(8,128)(2,1)S(1)}, u32[]{:S(2)}, u32[]{:S(2)}) %collective-permute-start.7) | collective-permute-done | bytes 557088 | tf_op jit(solution)/shard_map/ppermute | solution.py:262
  51.4 2.3 %collective-permute-done.6.high_2b = bf16[272,1024]{1,0:T(8,128)(2,1)S(1)} collective-permute-done((bf16[272,1024]{1,0:T(8,128)(2,1)S(1)}, bf16[272,1024]{1,0:T(8,128)(2,1)S(1)}, u32[]{:S(2)}, u32[]{:S(2)}) %collective-permute-start.6) | collective-permute-done | bytes 557088 | tf_op jit(solution)/shard_map/ppermute | solution.py:268
  53.7 2.0 %far.1 = (f32[1,2048]{1,0:T(1,128)S(1)}, s32[2]{0:T(128)S(1)}, bf16[512,1024]{1,0:T(8,128)(2,1)S(1)}) custom-call(s32[6]{0:T(128)S(1)} %get-tuple-element.55.reach_ref, f32[1,2048]{1,0:T(1,128)S(1)} %middle.1.prior_ref, bf16[528,1024]{1,0:T(8,128)(2,1)S(1)} %collective-permute-done.1.low, bf16[528,1024]{1,0:T(8,128)(2,1)S(1)} %collective-permute-done.2.across, ...), custom_call_target="tpu_custom_call" | custom-call | flops 1024 | bytes 1024 | tf_op jit(solution)/shard_map/far/pallas_call | solution.py:271
  56.8 4.0 %collective-permute-start.14 = (f32[1,2048]{1,0:T(1,128)S(1)}, f32[1,2048]{1,0:T(1,128)S(1)}, u32[]{:S(2)}, u32[]{:S(2)}) collective-permute-start(f32[1,2048]{1,0:T(1,128)S(1)} %last.1), channel_id=1, source_target_pairs={{0,9},{1,8},{2,11},{3,10},{4,13},{5,12},{6,15},{7,14},{8,17},{9,16... | collective-permute-start | bytes 24584 | tf_op jit(solution)/shard_map/ppermute | solution.py:366
  60.7 1.8 %collective-permute-start.13 = (f32[1,2048]{1,0:T(1,128)S(1)}, f32[1,2048]{1,0:T(1,128)S(1)}, u32[]{:S(2)}, u32[]{:S(2)}) collective-permute-start(f32[1,2048]{1,0:T(1,128)S(1)} %last.1), channel_id=1, source_target_pairs={{0,8},{4,12},{8,16},{12,20},{16,24},{20,28},{1,9},{5,13},{9,17},{1... | collective-permute-start | bytes 24584 | tf_op jit(solution)/shard_map/ppermute | solution.py:262
  62.6 1.3 %collective-permute-done.13 = f32[1,2048]{1,0:T(1,128)S(1)} collective-permute-done((f32[1,2048]{1,0:T(1,128)S(1)}, f32[1,2048]{1,0:T(1,128)S(1)}, u32[]{:S(2)}, u32[]{:S(2)}) %collective-permute-start.13) | collective-permute-done | bytes 8224 | tf_op jit(solution)/shard_map/ppermute | solution.py:262
  63.9 3.5 %collective-permute-start.15 = (f32[1,2048]{1,0:T(1,128)S(1)}, f32[1,2048]{1,0:T(1,128)S(1)}, u32[]{:S(2)}, u32[]{:S(2)}) collective-permute-start(f32[1,2048]{1,0:T(1,128)S(1)} %fusion), channel_id=1, source_target_pairs={{0,2},{1,3},{2,0},{3,1},{4,6},{5,7},{6,4},{7,5},{8,10},{9,11},{10,... | collective-permute-start | bytes 24584 | tf_op jit(solution)/shard_map/ppermute | solution.py:268
  67.4 1.6 %collective-permute-done.15 = f32[1,2048]{1,0:T(1,128)S(1)} collective-permute-done((f32[1,2048]{1,0:T(1,128)S(1)}, f32[1,2048]{1,0:T(1,128)S(1)}, u32[]{:S(2)}, u32[]{:S(2)}) %collective-permute-start.15) | collective-permute-done | bytes 8224 | tf_op jit(solution)/shard_map/ppermute | solution.py:268
  (24 shorter events, 4.7 us)
Async XLA Ops:
  0.0 0.7 %copy-start = (s32[2048]{0:T(1024)S(1)}, s32[2048]{0:T(1024)}, u32[]{:S(2)}) copy-start(s32[2048]{0:T(1024)} %param.3) | copy-start | bytes 24580
  0.7 10.7 %copy-start.1 = (s32[2048]{0:T(1024)S(1)}, s32[2048]{0:T(1024)}, u32[]{:S(2)}) copy-start(s32[2048]{0:T(1024)} %param.3) | copy-start | bytes 24580
  2.2 28.0 %collective-permute-start.1 = (bf16[528,1024]{1,0:T(8,128)(2,1)S(1)}, bf16[528,1024]{1,0:T(8,128)(2,1)S(1)}, u32[]{:S(2)}, u32[]{:S(2)}) collective-permute-start(bf16[528,1024]{1,0:T(8,128)(2,1)S(1)} %get-tuple-element.41), channel_id=1, source_target_pairs={{0,8},{4,12},{8,16},{12,20},{16,24},{20,28},{1,9},{5,13},{9,17},{1... | collective-permute-start | bytes 3244040 | tf_op jit(solution)/shard_map/ppermute | solution.py:262
  7.2 25.4 %collective-permute-start.2 = (bf16[528,1024]{1,0:T(8,128)(2,1)S(1)}, bf16[528,1024]{1,0:T(8,128)(2,1)S(1)}, u32[]{:S(2)}, u32[]{:S(2)}) collective-permute-start(bf16[528,1024]{1,0:T(8,128)(2,1)S(1)} %get-tuple-element.41), channel_id=1, source_target_pairs={{0,4},{4,0},{8,12},{12,8},{16,20},{20,16},{24,28},{28,24},{1,5},{5... | collective-permute-start | bytes 3244040 | tf_op jit(solution)/shard_map/ppermute | solution.py:265
  8.8 16.7 %collective-permute-start = (bf16[256,1024]{1,0:T(8,128)(2,1)S(1)}, bf16[256,1024]{1,0:T(8,128)(2,1)S(1)}, u32[]{:S(2)}, u32[]{:S(2)}) collective-permute-start(bf16[256,1024]{1,0:T(8,128)(2,1)S(1)} %get-tuple-element.36), channel_id=1, source_target_pairs={{8,0},{12,4},{16,8},{20,12},{24,16},{28,20},{9,1},{13,5},{17,9},{2... | collective-permute-start | bytes 1572872 | tf_op jit(solution)/shard_map/ppermute | solution.py:262
  10.1 25.6 %collective-permute-start.3 = (bf16[272,1024]{1,0:T(8,128)(2,1)S(1)}, bf16[272,1024]{1,0:T(8,128)(2,1)S(1)}, u32[]{:S(2)}, u32[]{:S(2)}) collective-permute-start(bf16[272,1024]{1,0:T(8,128)(2,1)S(1)} %get-tuple-element.45), channel_id=1, source_target_pairs={{8,0},{12,4},{16,8},{20,12},{24,16},{28,20},{9,1},{13,5},{17,9},{2... | collective-permute-start | bytes 1671176 | tf_op jit(solution)/shard_map/ppermute | solution.py:262
  25.5 10.4 %collective-permute-start.5 = (bf16[256,1024]{1,0:T(8,128)(2,1)S(1)}, bf16[256,1024]{1,0:T(8,128)(2,1)S(1)}, u32[]{:S(2)}, u32[]{:S(2)}) collective-permute-start(bf16[256,1024]{1,0:T(8,128)(2,1)S(1)} %collective-permute-done.high_0a), channel_id=1, source_target_pairs={{0,2},{1,3},{2,0},{3,1},{4,6},{5,7},{6,4},{7,5},{8,10},{9,11},{10,... | collective-permute-start | bytes 1572872 | tf_op jit(solution)/shard_map/ppermute | solution.py:268
  27.0 8.9 %collective-permute-start.4 = (bf16[256,1024]{1,0:T(8,128)(2,1)S(1)}, bf16[256,1024]{1,0:T(8,128)(2,1)S(1)}, u32[]{:S(2)}, u32[]{:S(2)}) collective-permute-start(bf16[256,1024]{1,0:T(8,128)(2,1)S(1)} %collective-permute-done.high_0a), channel_id=1, source_target_pairs={{0,1},{1,0},{2,3},{3,2},{4,5},{5,4},{6,7},{7,6},{8,9},{9,8},{10,11... | collective-permute-start | bytes 1572872 | tf_op jit(solution)/shard_map/ppermute | solution.py:268
  35.9 14.5 %collective-permute-start.7 = (bf16[272,1024]{1,0:T(8,128)(2,1)S(1)}, bf16[272,1024]{1,0:T(8,128)(2,1)S(1)}, u32[]{:S(2)}, u32[]{:S(2)}) collective-permute-start(bf16[272,1024]{1,0:T(8,128)(2,1)S(1)} %slice.9), channel_id=1, source_target_pairs={{4,0},{12,8},{20,16},{28,24},{5,1},{13,9},{21,17},{29,25},{6,2},{1... | collective-permute-start | bytes 1671176 | tf_op jit(solution)/shard_map/ppermute | solution.py:262
  37.2 14.1 %collective-permute-start.8 = (bf16[272,1024]{1,0:T(8,128)(2,1)S(1)}, bf16[272,1024]{1,0:T(8,128)(2,1)S(1)}, u32[]{:S(2)}, u32[]{:S(2)}) collective-permute-start(bf16[272,1024]{1,0:T(8,128)(2,1)S(1)} %slice.10), channel_id=1, source_target_pairs={{0,8},{8,16},{16,24},{1,9},{9,17},{17,25},{2,10},{10,18},{18,26},{... | collective-permute-start | bytes 1671176 | tf_op jit(solution)/shard_map/ppermute | solution.py:262
  40.7 13.0 %collective-permute-start.6 = (bf16[272,1024]{1,0:T(8,128)(2,1)S(1)}, bf16[272,1024]{1,0:T(8,128)(2,1)S(1)}, u32[]{:S(2)}, u32[]{:S(2)}) collective-permute-start(bf16[272,1024]{1,0:T(8,128)(2,1)S(1)} %collective-permute-done.3.high_0b), channel_id=1, source_target_pairs={{0,2},{1,3},{2,0},{3,1},{4,6},{5,7},{6,4},{7,5},{8,10},{9,11},{10,... | collective-permute-start | bytes 1671176 | tf_op jit(solution)/shard_map/ppermute | solution.py:268
  42.3 4.0 %collective-permute-start.9 = (bf16[256,1024]{1,0:T(8,128)(2,1)S(1)}, bf16[256,1024]{1,0:T(8,128)(2,1)S(1)}, u32[]{:S(2)}, u32[]{:S(2)}) collective-permute-start(bf16[256,1024]{1,0:T(8,128)(2,1)S(1)} %slice.11), channel_id=1, source_target_pairs={{0,1},{1,0},{2,3},{3,2},{4,5},{5,4},{6,7},{7,6},{8,9},{9,8},{10,11... | collective-permute-start | bytes 1572872 | tf_op jit(solution)/shard_map/ppermute | solution.py:268
  42.4 4.0 %collective-permute-start.10 = (bf16[256,1024]{1,0:T(8,128)(2,1)S(1)}, bf16[256,1024]{1,0:T(8,128)(2,1)S(1)}, u32[]{:S(2)}, u32[]{:S(2)}) collective-permute-start(bf16[256,1024]{1,0:T(8,128)(2,1)S(1)} %collective-permute-done.5.high_2a), channel_id=1, source_target_pairs={{0,1},{1,0},{2,3},{3,2},{4,5},{5,4},{6,7},{7,6},{8,9},{9,8},{10,11... | collective-permute-start | bytes 1572872 | tf_op jit(solution)/shard_map/ppermute | solution.py:268
  46.2 1.9 %collective-permute-start.11 = (f32[1,2048]{1,0:T(1,128)S(1)}, f32[1,2048]{1,0:T(1,128)S(1)}, u32[]{:S(2)}, u32[]{:S(2)}) collective-permute-start(f32[1,2048]{1,0:T(1,128)S(1)} %get-tuple-element.54), channel_id=1, source_target_pairs={{0,1},{1,0},{2,3},{3,2},{4,5},{5,4},{6,7},{7,6},{8,9},{9,8},{10,11... | collective-permute-start | bytes 24584 | tf_op jit(solution)/shard_map/ppermute | solution.py:268
  53.7 2.0 %collective-permute-start.12 = (bf16[272,1024]{1,0:T(8,128)(2,1)S(1)}, bf16[272,1024]{1,0:T(8,128)(2,1)S(1)}, u32[]{:S(2)}, u32[]{:S(2)}) collective-permute-start(bf16[272,1024]{1,0:T(8,128)(2,1)S(1)} %collective-permute-done.6.high_2b), channel_id=1, source_target_pairs={{0,1},{1,0},{2,3},{3,2},{4,5},{5,4},{6,7},{7,6},{8,9},{9,8},{10,11... | collective-permute-start | bytes 1671176 | tf_op jit(solution)/shard_map/ppermute | solution.py:268
  56.8 5.8 %collective-permute-start.14 = (f32[1,2048]{1,0:T(1,128)S(1)}, f32[1,2048]{1,0:T(1,128)S(1)}, u32[]{:S(2)}, u32[]{:S(2)}) collective-permute-start(f32[1,2048]{1,0:T(1,128)S(1)} %last.1), channel_id=1, source_target_pairs={{0,9},{1,8},{2,11},{3,10},{4,13},{5,12},{6,15},{7,14},{8,17},{9,16... | collective-permute-start | bytes 24584 | tf_op jit(solution)/shard_map/ppermute | solution.py:366
  60.7 3.2 %collective-permute-start.13 = (f32[1,2048]{1,0:T(1,128)S(1)}, f32[1,2048]{1,0:T(1,128)S(1)}, u32[]{:S(2)}, u32[]{:S(2)}) collective-permute-start(f32[1,2048]{1,0:T(1,128)S(1)} %last.1), channel_id=1, source_target_pairs={{0,8},{4,12},{8,16},{12,20},{16,24},{20,28},{1,9},{5,13},{9,17},{1... | collective-permute-start | bytes 24584 | tf_op jit(solution)/shard_map/ppermute | solution.py:262
  63.9 5.1 %collective-permute-start.15 = (f32[1,2048]{1,0:T(1,128)S(1)}, f32[1,2048]{1,0:T(1,128)S(1)}, u32[]{:S(2)}, u32[]{:S(2)}) collective-permute-start(f32[1,2048]{1,0:T(1,128)S(1)} %fusion), channel_id=1, source_target_pairs={{0,2},{1,3},{2,0},{3,1},{4,6},{5,7},{6,4},{7,5},{8,10},{9,11},{10,... | collective-permute-start | bytes 24584 | tf_op jit(solution)/shard_map/ppermute | solution.py:268

commit v9 on v8

--- a/solution.py
+++ b/solution.py
@@ -341,12 +341,11 @@
         [SMEM] * 2 + [VMEM] * 10 + [SMEM],
         own_reach, lower_reach, own, best, low, across, high_0a, high_0b, high_1a, high_2a,
     )
-    best_1 = other_rep(best, 1)
     (of_high,) = call(
         middle_kernel, "middle", [line], [SMEM] + [VMEM] * 6,
         reach, of_high, low, across, high_1b, high_3a,
     )
-    high_2b, side_a, side_b, of_high, best_1 = fence((high_2b, side_a, side_b, of_high, best_1))
+    high_2b, side_a, side_b, of_high = fence((high_2b, side_a, side_b, of_high))
     high_3b = other_rep(high_2b, 1)
     of_high, side, sides = call(
         far_kernel, "far", [line, ((2,), jnp.int32), ((quarter, width), BF16)],
@@ -360,13 +359,9 @@
     )
 
     above = along_shard(of_high, 2)
-    route = [
-        (i * reps + j, (i + 2) * reps + (j ^ 1)) for i in range(shards - 2) for j in range(reps)
-    ]
-    above = jnp.maximum(above, lax.ppermute(of_high, ("shard", "rep"), route))
-    above = jnp.where(lax.axis_index("shard") >= 2, above, -1.0)
-    best = jnp.maximum(jnp.maximum(best, best_1), above)
-    return jnp.maximum(best, other_rep(best, 2))[0]
+    best = jnp.maximum(best, jnp.where(lax.axis_index("shard") >= 2, above, -1.0))
+    others = [other_rep(best, flip) for flip in range(1, reps)]
+    return functools.reduce(jnp.maximum, others, best)[0]
 
 
 def solution(mesh):

time: 71 us -> 70.1 us (0.987)
  the two profiles are of different devices: /device:TPU:0 before, /device:TPU:8 now
where the time goes in v9:
time: 70.1 us; the launch traced here: 69.1 us
  starting transfers between devices  27.7 us (40%)
  waiting for transfers between devices  22.8 us (33%)
  Pallas kernels  17 us (24%)
  local copies, waits for them, and re-layouts  0.81 us (1%)
    ppermute x6, starting transfers between devices, along_shard(): return lax.ppermute(block, 'shard', route)  20.5 us
    ppermute x6, waiting for transfers between devices, along_shard(): return lax.ppermute(block, 'shard', route)  18.6 us
    pallas_call x5, Pallas kernels, call(): pl.pallas_call(kernel, out_shape=[jax.ShapeDtypeStruct(shape, dtype) for...  9.5 us
    pallas_call x1, Pallas kernels, local(): pl.pallas_call(own_kernel, out_shape=[jax.ShapeDtypeStruct((rows, width),...  6.02 us
    ppermute x9, starting transfers between devices, other_rep(): return lax.ppermute(block, 'rep', [(i, i ^ flip) for i in range(reps)])  5.55 us
    ppermute x9, waiting for transfers between devices, other_rep(): return lax.ppermute(block, 'rep', [(i, i ^ flip) for i in range(reps)])  4.16 us
    ppermute x1, starting transfers between devices, partner(): return lax.ppermute(block, 'shard', [(i, i ^ 1) for i in range(shards)])  1.58 us
    pallas_call x1, Pallas kernels, local(): pl.pallas_call(prepare_kernel, out_shape=[jax.ShapeDtypeStruct((size, wid...  1.47 us
  transfers between devices with their start and end apart: 16, of which 11 were waited for; matrix products, arithmetic and copies ran while one was open for 0% of the time, Pallas kernels for 21%

profile of v9, /device:TPU:8, one launch (start us, length us, event | category | flops | bytes accessed | tf_op | source)
XLA Modules:
  0.0 69.1 jit_solution(4084520136185359749)
XLA Ops:
  0.7 1.5 %prepare.1 = (bf16[256,1024]{1,0:T(8,128)(2,1)S(1)}, bf16[272,1024]{1,0:T(8,128)(2,1)S(1)}, bf16[528,1024]{1,0:T(8,128)(2,1)S(1)}) custom-call(bf16[2048,1024]{1,0:T(8,128)(2,1)} %emb_ref.3, s32[16,128]{1,0:T(8,128)S(1)} %bitcast.3), custom_call_target="tpu_custom_call" | custom-call | tf_op jit(solution)/shard_map/prepare/pallas_call | solution.py:282
  2.2 3.5 %collective-permute-start.1 = (bf16[528,1024]{1,0:T(8,128)(2,1)S(1)}, bf16[528,1024]{1,0:T(8,128)(2,1)S(1)}, u32[]{:S(2)}, u32[]{:S(2)}) collective-permute-start(bf16[528,1024]{1,0:T(8,128)(2,1)S(1)} %get-tuple-element.40), channel_id=1, source_target_pairs={{0,8},{4,12},{8,16},{12,20},{16,24},{20,28},{1,9},{5,13},{9,17},{1... | collective-permute-start | bytes 3244040 | tf_op jit(solution)/shard_map/ppermute | solution.py:262
  5.7 1.6 %collective-permute-start.2 = (bf16[528,1024]{1,0:T(8,128)(2,1)S(1)}, bf16[528,1024]{1,0:T(8,128)(2,1)S(1)}, u32[]{:S(2)}, u32[]{:S(2)}) collective-permute-start(bf16[528,1024]{1,0:T(8,128)(2,1)S(1)} %get-tuple-element.40), channel_id=1, source_target_pairs={{0,4},{4,0},{8,12},{12,8},{16,20},{20,16},{24,28},{28,24},{1,5},{5... | collective-permute-start | bytes 3244040 | tf_op jit(solution)/shard_map/ppermute | solution.py:265
  7.3 2.4 %collective-permute-start = (bf16[256,1024]{1,0:T(8,128)(2,1)S(1)}, bf16[256,1024]{1,0:T(8,128)(2,1)S(1)}, u32[]{:S(2)}, u32[]{:S(2)}) collective-permute-start(bf16[256,1024]{1,0:T(8,128)(2,1)S(1)} %get-tuple-element.35), channel_id=1, source_target_pairs={{8,0},{12,4},{16,8},{20,12},{24,16},{28,20},{9,1},{13,5},{17,9},{2... | collective-permute-start | bytes 1572872 | tf_op jit(solution)/shard_map/ppermute | solution.py:262
  9.7 1.9 %collective-permute-start.3 = (bf16[272,1024]{1,0:T(8,128)(2,1)S(1)}, bf16[272,1024]{1,0:T(8,128)(2,1)S(1)}, u32[]{:S(2)}, u32[]{:S(2)}) collective-permute-start(bf16[272,1024]{1,0:T(8,128)(2,1)S(1)} %get-tuple-element.44), channel_id=1, source_target_pairs={{8,0},{12,4},{16,8},{20,12},{24,16},{28,20},{9,1},{13,5},{17,9},{2... | collective-permute-start | bytes 1671176 | tf_op jit(solution)/shard_map/ppermute | solution.py:262
  11.6 6.0 %own.1 = (bf16[2048,1024]{1,0:T(8,128)(2,1)S(1)}, f32[1,2048]{1,0:T(1,128)S(1)}, s32[2]{0:T(128)S(1)}) custom-call(bf16[2048,1024]{1,0:T(8,128)(2,1)} %emb_ref.3, s32[1,2048]{1,0:T(1,128)S(1)} %bitcast.4), custom_call_target="tpu_custom_call" | custom-call | flops 1024 | bytes 1024 | tf_op jit(solution)/shard_map/own/pallas_call | solution.py:304
  17.6 6.4 %collective-permute-done.high_0a = bf16[256,1024]{1,0:T(8,128)(2,1)S(1)} collective-permute-done((bf16[256,1024]{1,0:T(8,128)(2,1)S(1)}, bf16[256,1024]{1,0:T(8,128)(2,1)S(1)}, u32[]{:S(2)}, u32[]{:S(2)}) %collective-permute-start) | collective-permute-done | bytes 524320 | tf_op jit(solution)/shard_map/ppermute | solution.py:262
  24.0 1.5 %collective-permute-start.5 = (bf16[256,1024]{1,0:T(8,128)(2,1)S(1)}, bf16[256,1024]{1,0:T(8,128)(2,1)S(1)}, u32[]{:S(2)}, u32[]{:S(2)}) collective-permute-start(bf16[256,1024]{1,0:T(8,128)(2,1)S(1)} %collective-permute-done.high_0a), channel_id=1, source_target_pairs={{0,2},{1,3},{2,0},{3,1},{4,6},{5,7},{6,4},{7,5},{8,10},{9,11},{10,... | collective-permute-start | bytes 1572872 | tf_op jit(solution)/shard_map/ppermute | solution.py:268
  25.5 4.2 %collective-permute-done.1.low = bf16[528,1024]{1,0:T(8,128)(2,1)S(1)} collective-permute-done((bf16[528,1024]{1,0:T(8,128)(2,1)S(1)}, bf16[528,1024]{1,0:T(8,128)(2,1)S(1)}, u32[]{:S(2)}, u32[]{:S(2)}) %collective-permute-start.1) | collective-permute-done | bytes 1081376 | tf_op jit(solution)/shard_map/ppermute | solution.py:262
  29.7 1.3 %lower.1 = (f32[1,2048]{1,0:T(1,128)S(1)}, s32[2]{0:T(128)S(1)}) custom-call(s32[2]{0:T(128)S(1)} %get-tuple-element.34.own_reach, bf16[2048,1024]{1,0:T(8,128)(2,1)S(1)} %get-tuple-element.38.own_ref, f32[1,2048]{1,0:T(1,128)S(1)} %get-tuple-element.39.best_ref, bf16[528,1024]{1,0:T(8,128)(2,1)S(1)} %collective-permute-done.1.low), custom_call_target="tpu_custom_call" | custom-call | flops 1024 | bytes 1024 | tf_op jit(solution)/shard_map/lower/pallas_call | solution.py:271
  31.1 3.0 %collective-permute-done.3.high_0b = bf16[272,1024]{1,0:T(8,128)(2,1)S(1)} collective-permute-done((bf16[272,1024]{1,0:T(8,128)(2,1)S(1)}, bf16[272,1024]{1,0:T(8,128)(2,1)S(1)}, u32[]{:S(2)}, u32[]{:S(2)}) %collective-permute-start.3) | collective-permute-done | bytes 557088 | tf_op jit(solution)/shard_map/ppermute | solution.py:262
  34.4 1.3 %collective-permute-start.7 = (bf16[272,1024]{1,0:T(8,128)(2,1)S(1)}, bf16[272,1024]{1,0:T(8,128)(2,1)S(1)}, u32[]{:S(2)}, u32[]{:S(2)}) collective-permute-start(bf16[272,1024]{1,0:T(8,128)(2,1)S(1)} %slice.9), channel_id=1, source_target_pairs={{4,0},{12,8},{20,16},{28,24},{5,1},{13,9},{21,17},{29,25},{6,2},{1... | collective-permute-start | bytes 1671176 | tf_op jit(solution)/shard_map/ppermute | solution.py:262
  35.7 3.5 %collective-permute-start.8 = (bf16[272,1024]{1,0:T(8,128)(2,1)S(1)}, bf16[272,1024]{1,0:T(8,128)(2,1)S(1)}, u32[]{:S(2)}, u32[]{:S(2)}) collective-permute-start(bf16[272,1024]{1,0:T(8,128)(2,1)S(1)} %slice.10), channel_id=1, source_target_pairs={{0,8},{8,16},{16,24},{1,9},{9,17},{17,25},{2,10},{10,18},{18,26},{... | collective-permute-start | bytes 1671176 | tf_op jit(solution)/shard_map/ppermute | solution.py:262
  39.2 1.6 %collective-permute-start.6 = (bf16[272,1024]{1,0:T(8,128)(2,1)S(1)}, bf16[272,1024]{1,0:T(8,128)(2,1)S(1)}, u32[]{:S(2)}, u32[]{:S(2)}) collective-permute-start(bf16[272,1024]{1,0:T(8,128)(2,1)S(1)} %collective-permute-done.3.high_0b), channel_id=1, source_target_pairs={{0,2},{1,3},{2,0},{3,1},{4,6},{5,7},{6,4},{7,5},{8,10},{9,11},{10,... | collective-permute-start | bytes 1671176 | tf_op jit(solution)/shard_map/ppermute | solution.py:268
  41.4 3.4 %near.1 = (f32[1,2048]{1,0:T(1,128)S(1)}, f32[1,2048]{1,0:T(1,128)S(1)}, s32[6]{0:T(128)S(1)}) custom-call(s32[2]{0:T(128)S(1)} %get-tuple-element.34.own_reach, s32[2]{0:T(128)S(1)} %get-tuple-element.41.lower_reach, bf16[2048,1024]{1,0:T(8,128)(2,1)S(1)} %get-tuple-element.38.own_ref, f32[1,2048]{1,0:T(1,128)S(1)} %get-tuple-element.43.best_ref, ...), custom_call_target="tpu_custom_call" | custom-call | flops 1024 | bytes 1024 | tf_op jit(solution)/shard_map/near/pallas_call | solution.py:271
  44.8 1.8 %middle.1.prior_ref = f32[1,2048]{1,0:T(1,128)S(1)} custom-call(s32[6]{0:T(128)S(1)} %get-tuple-element.54.reach_ref, f32[1,2048]{1,0:T(1,128)S(1)} %get-tuple-element.55.prior_ref, bf16[528,1024]{1,0:T(8,128)(2,1)S(1)} %collective-permute-done.1.low, bf16[528,1024]{1,0:T(8,128)(2,1)S(1)} %collective-permute-done.2.across, ...), custom_call_target="tpu_custom_call" | custom-call | flops 1024 | bytes 1024 | tf_op jit(solution)/shard_map/middle/pallas_call | solution.py:271
  46.6 2.4 %collective-permute-done.7.side_a = bf16[272,1024]{1,0:T(8,128)(2,1)S(1)} collective-permute-done((bf16[272,1024]{1,0:T(8,128)(2,1)S(1)}, bf16[272,1024]{1,0:T(8,128)(2,1)S(1)}, u32[]{:S(2)}, u32[]{:S(2)}) %collective-permute-start.7) | collective-permute-done | bytes 557088 | tf_op jit(solution)/shard_map/ppermute | solution.py:262
  48.9 1.3 %collective-permute-done.8.side_b = bf16[272,1024]{1,0:T(8,128)(2,1)S(1)} collective-permute-done((bf16[272,1024]{1,0:T(8,128)(2,1)S(1)}, bf16[272,1024]{1,0:T(8,128)(2,1)S(1)}, u32[]{:S(2)}, u32[]{:S(2)}) %collective-permute-start.8) | collective-permute-done | bytes 557088 | tf_op jit(solution)/shard_map/ppermute | solution.py:262
  50.2 1.4 %collective-permute-done.6.high_2b = bf16[272,1024]{1,0:T(8,128)(2,1)S(1)} collective-permute-done((bf16[272,1024]{1,0:T(8,128)(2,1)S(1)}, bf16[272,1024]{1,0:T(8,128)(2,1)S(1)}, u32[]{:S(2)}, u32[]{:S(2)}) %collective-permute-start.6) | collective-permute-done | bytes 557088 | tf_op jit(solution)/shard_map/ppermute | solution.py:268
  51.6 2.0 %far.1 = (f32[1,2048]{1,0:T(1,128)S(1)}, s32[2]{0:T(128)S(1)}, bf16[512,1024]{1,0:T(8,128)(2,1)S(1)}) custom-call(s32[6]{0:T(128)S(1)} %get-tuple-element.54.reach_ref, f32[1,2048]{1,0:T(1,128)S(1)} %middle.1.prior_ref, bf16[528,1024]{1,0:T(8,128)(2,1)S(1)} %collective-permute-done.1.low, bf16[528,1024]{1,0:T(8,128)(2,1)S(1)} %collective-permute-done.2.across, ...), custom_call_target="tpu_custom_call" | custom-call | flops 1024 | bytes 1024 | tf_op jit(solution)/shard_map/far/pallas_call | solution.py:271
  54.7 7.9 %collective-permute-start.12 = (f32[1,2048]{1,0:T(1,128)S(1)}, f32[1,2048]{1,0:T(1,128)S(1)}, u32[]{:S(2)}, u32[]{:S(2)}) collective-permute-start(f32[1,2048]{1,0:T(1,128)S(1)} %last.1), channel_id=1, source_target_pairs={{0,8},{4,12},{8,16},{12,20},{16,24},{20,28},{1,9},{5,13},{9,17},{1... | collective-permute-start | bytes 24584 | tf_op jit(solution)/shard_map/ppermute | solution.py:262
  62.7 1.3 %collective-permute-done.12 = f32[1,2048]{1,0:T(1,128)S(1)} collective-permute-done((f32[1,2048]{1,0:T(1,128)S(1)}, f32[1,2048]{1,0:T(1,128)S(1)}, u32[]{:S(2)}, u32[]{:S(2)}) %collective-permute-start.12) | collective-permute-done | bytes 8224 | tf_op jit(solution)/shard_map/ppermute | solution.py:262
  66.0 1.3 %collective-permute-done.15 = f32[1,2048]{1,0:T(1,128)S(1)} collective-permute-done((f32[1,2048]{1,0:T(1,128)S(1)}, f32[1,2048]{1,0:T(1,128)S(1)}, u32[]{:S(2)}, u32[]{:S(2)}) %collective-permute-start.15) | collective-permute-done | bytes 8224 | tf_op jit(solution)/shard_map/ppermute | solution.py:268
  67.2 1.3 %collective-permute-done.14 = f32[1,2048]{1,0:T(1,128)S(1)} collective-permute-done((f32[1,2048]{1,0:T(1,128)S(1)}, f32[1,2048]{1,0:T(1,128)S(1)}, u32[]{:S(2)}, u32[]{:S(2)}) %collective-permute-start.14) | collective-permute-done | bytes 8224 | tf_op jit(solution)/shard_map/ppermute | solution.py:268
  (24 shorter events, 5.4 us)
Async XLA Ops:
  0.0 0.7 %copy-start = (s32[2048]{0:T(1024)S(1)}, s32[2048]{0:T(1024)}, u32[]{:S(2)}) copy-start(s32[2048]{0:T(1024)} %param.3) | copy-start | bytes 24580
  0.7 10.9 %copy-start.1 = (s32[2048]{0:T(1024)S(1)}, s32[2048]{0:T(1024)}, u32[]{:S(2)}) copy-start(s32[2048]{0:T(1024)} %param.3) | copy-start | bytes 24580
  2.2 27.5 %collective-permute-start.1 = (bf16[528,1024]{1,0:T(8,128)(2,1)S(1)}, bf16[528,1024]{1,0:T(8,128)(2,1)S(1)}, u32[]{:S(2)}, u32[]{:S(2)}) collective-permute-start(bf16[528,1024]{1,0:T(8,128)(2,1)S(1)} %get-tuple-element.40), channel_id=1, source_target_pairs={{0,8},{4,12},{8,16},{12,20},{16,24},{20,28},{1,9},{5,13},{9,17},{1... | collective-permute-start | bytes 3244040 | tf_op jit(solution)/shard_map/ppermute | solution.py:262
  5.7 25.4 %collective-permute-start.2 = (bf16[528,1024]{1,0:T(8,128)(2,1)S(1)}, bf16[528,1024]{1,0:T(8,128)(2,1)S(1)}, u32[]{:S(2)}, u32[]{:S(2)}) collective-permute-start(bf16[528,1024]{1,0:T(8,128)(2,1)S(1)} %get-tuple-element.40), channel_id=1, source_target_pairs={{0,4},{4,0},{8,12},{12,8},{16,20},{20,16},{24,28},{28,24},{1,5},{5... | collective-permute-start | bytes 3244040 | tf_op jit(solution)/shard_map/ppermute | solution.py:265
  7.3 16.7 %collective-permute-start = (bf16[256,1024]{1,0:T(8,128)(2,1)S(1)}, bf16[256,1024]{1,0:T(8,128)(2,1)S(1)}, u32[]{:S(2)}, u32[]{:S(2)}) collective-permute-start(bf16[256,1024]{1,0:T(8,128)(2,1)S(1)} %get-tuple-element.35), channel_id=1, source_target_pairs={{8,0},{12,4},{16,8},{20,12},{24,16},{28,20},{9,1},{13,5},{17,9},{2... | collective-permute-start | bytes 1572872 | tf_op jit(solution)/shard_map/ppermute | solution.py:262
  9.7 24.5 %collective-permute-start.3 = (bf16[272,1024]{1,0:T(8,128)(2,1)S(1)}, bf16[272,1024]{1,0:T(8,128)(2,1)S(1)}, u32[]{:S(2)}, u32[]{:S(2)}) collective-permute-start(bf16[272,1024]{1,0:T(8,128)(2,1)S(1)} %get-tuple-element.44), channel_id=1, source_target_pairs={{8,0},{12,4},{16,8},{20,12},{24,16},{28,20},{9,1},{13,5},{17,9},{2... | collective-permute-start | bytes 1671176 | tf_op jit(solution)/shard_map/ppermute | solution.py:262
  24.0 10.4 %collective-permute-start.5 = (bf16[256,1024]{1,0:T(8,128)(2,1)S(1)}, bf16[256,1024]{1,0:T(8,128)(2,1)S(1)}, u32[]{:S(2)}, u32[]{:S(2)}) collective-permute-start(bf16[256,1024]{1,0:T(8,128)(2,1)S(1)} %collective-permute-done.high_0a), channel_id=1, source_target_pairs={{0,2},{1,3},{2,0},{3,1},{4,6},{5,7},{6,4},{7,5},{8,10},{9,11},{10,... | collective-permute-start | bytes 1572872 | tf_op jit(solution)/shard_map/ppermute | solution.py:268
  25.5 8.9 %collective-permute-start.4 = (bf16[256,1024]{1,0:T(8,128)(2,1)S(1)}, bf16[256,1024]{1,0:T(8,128)(2,1)S(1)}, u32[]{:S(2)}, u32[]{:S(2)}) collective-permute-start(bf16[256,1024]{1,0:T(8,128)(2,1)S(1)} %collective-permute-done.high_0a), channel_id=1, source_target_pairs={{0,1},{1,0},{2,3},{3,2},{4,5},{5,4},{6,7},{7,6},{8,9},{9,8},{10,11... | collective-permute-start | bytes 1572872 | tf_op jit(solution)/shard_map/ppermute | solution.py:268
  34.4 14.5 %collective-permute-start.7 = (bf16[272,1024]{1,0:T(8,128)(2,1)S(1)}, bf16[272,1024]{1,0:T(8,128)(2,1)S(1)}, u32[]{:S(2)}, u32[]{:S(2)}) collective-permute-start(bf16[272,1024]{1,0:T(8,128)(2,1)S(1)} %slice.9), channel_id=1, source_target_pairs={{4,0},{12,8},{20,16},{28,24},{5,1},{13,9},{21,17},{29,25},{6,2},{1... | collective-permute-start | bytes 1671176 | tf_op jit(solution)/shard_map/ppermute | solution.py:262
  35.7 14.5 %collective-permute-start.8 = (bf16[272,1024]{1,0:T(8,128)(2,1)S(1)}, bf16[272,1024]{1,0:T(8,128)(2,1)S(1)}, u32[]{:S(2)}, u32[]{:S(2)}) collective-permute-start(bf16[272,1024]{1,0:T(8,128)(2,1)S(1)} %slice.10), channel_id=1, source_target_pairs={{0,8},{8,16},{16,24},{1,9},{9,17},{17,25},{2,10},{10,18},{18,26},{... | collective-permute-start | bytes 1671176 | tf_op jit(solution)/shard_map/ppermute | solution.py:262
  39.2 12.4 %collective-permute-start.6 = (bf16[272,1024]{1,0:T(8,128)(2,1)S(1)}, bf16[272,1024]{1,0:T(8,128)(2,1)S(1)}, u32[]{:S(2)}, u32[]{:S(2)}) collective-permute-start(bf16[272,1024]{1,0:T(8,128)(2,1)S(1)} %collective-permute-done.3.high_0b), channel_id=1, source_target_pairs={{0,2},{1,3},{2,0},{3,1},{4,6},{5,7},{6,4},{7,5},{8,10},{9,11},{10,... | collective-permute-start | bytes 1671176 | tf_op jit(solution)/shard_map/ppermute | solution.py:268
  40.8 4.0 %collective-permute-start.9 = (bf16[256,1024]{1,0:T(8,128)(2,1)S(1)}, bf16[256,1024]{1,0:T(8,128)(2,1)S(1)}, u32[]{:S(2)}, u32[]{:S(2)}) collective-permute-start(bf16[256,1024]{1,0:T(8,128)(2,1)S(1)} %slice.11), channel_id=1, source_target_pairs={{0,1},{1,0},{2,3},{3,2},{4,5},{5,4},{6,7},{7,6},{8,9},{9,8},{10,11... | collective-permute-start | bytes 1572872 | tf_op jit(solution)/shard_map/ppermute | solution.py:268
  40.9 3.9 %collective-permute-start.10 = (bf16[256,1024]{1,0:T(8,128)(2,1)S(1)}, bf16[256,1024]{1,0:T(8,128)(2,1)S(1)}, u32[]{:S(2)}, u32[]{:S(2)}) collective-permute-start(bf16[256,1024]{1,0:T(8,128)(2,1)S(1)} %collective-permute-done.5.high_2a), channel_id=1, source_target_pairs={{0,1},{1,0},{2,3},{3,2},{4,5},{5,4},{6,7},{7,6},{8,9},{9,8},{10,11... | collective-permute-start | bytes 1572872 | tf_op jit(solution)/shard_map/ppermute | solution.py:268
  51.6 2.0 %collective-permute-start.11 = (bf16[272,1024]{1,0:T(8,128)(2,1)S(1)}, bf16[272,1024]{1,0:T(8,128)(2,1)S(1)}, u32[]{:S(2)}, u32[]{:S(2)}) collective-permute-start(bf16[272,1024]{1,0:T(8,128)(2,1)S(1)} %collective-permute-done.6.high_2b), channel_id=1, source_target_pairs={{0,1},{1,0},{2,3},{3,2},{4,5},{5,4},{6,7},{7,6},{8,9},{9,8},{10,11... | collective-permute-start | bytes 1671176 | tf_op jit(solution)/shard_map/ppermute | solution.py:268
  54.7 9.3 %collective-permute-start.12 = (f32[1,2048]{1,0:T(1,128)S(1)}, f32[1,2048]{1,0:T(1,128)S(1)}, u32[]{:S(2)}, u32[]{:S(2)}) collective-permute-start(f32[1,2048]{1,0:T(1,128)S(1)} %last.1), channel_id=1, source_target_pairs={{0,8},{4,12},{8,16},{12,20},{16,24},{20,28},{1,9},{5,13},{9,17},{1... | collective-permute-start | bytes 24584 | tf_op jit(solution)/shard_map/ppermute | solution.py:262
  64.0 3.2 %collective-permute-start.15 = (f32[1,2048]{1,0:T(1,128)S(1)}, f32[1,2048]{1,0:T(1,128)S(1)}, u32[]{:S(2)}, u32[]{:S(2)}) collective-permute-start(f32[1,2048]{1,0:T(1,128)S(1)} %fusion), channel_id=1, source_target_pairs={{0,3},{1,2},{2,1},{3,0},{4,7},{5,6},{6,5},{7,4},{8,11},{9,10},{10,... | collective-permute-start | bytes 24584 | tf_op jit(solution)/shard_map/ppermute | solution.py:268
  64.8 3.7 %collective-permute-start.14 = (f32[1,2048]{1,0:T(1,128)S(1)}, f32[1,2048]{1,0:T(1,128)S(1)}, u32[]{:S(2)}, u32[]{:S(2)}) collective-permute-start(f32[1,2048]{1,0:T(1,128)S(1)} %fusion), channel_id=1, source_target_pairs={{0,2},{1,3},{2,0},{3,1},{4,6},{5,7},{6,4},{7,5},{8,10},{9,11},{10,... | collective-permute-start | bytes 24584 | tf_op jit(solution)/shard_map/ppermute | solution.py:268
  65.7 2.8 %collective-permute-start.13 = (f32[1,2048]{1,0:T(1,128)S(1)}, f32[1,2048]{1,0:T(1,128)S(1)}, u32[]{:S(2)}, u32[]{:S(2)}) collective-permute-start(f32[1,2048]{1,0:T(1,128)S(1)} %fusion), channel_id=1, source_target_pairs={{0,1},{1,0},{2,3},{3,2},{4,5},{5,4},{6,7},{7,6},{8,9},{9,8},{10,11... | collective-permute-start | bytes 24584 | tf_op jit(solution)/shard_map/ppermute | solution.py:268

commit v10 on v7

--- a/solution.py
+++ b/solution.py
@@ -77,19 +77,15 @@
 
 def group(keys, queries_ref, query_rows, out_ref, out_at, count):
     step = min(WIDE, query_rows)
-    clear = functools.reduce(jnp.logical_and, [first <= 0 for *_, first in keys])
-    trips = (count + step - 1) // step
-
-    def over_queries(masked, j, _):
+
+    def over_queries(j, _):
         at = pl.multiple_of(j * step, step)
         queries = queries_ref[pl.ds(at, step), :]
         best = None
         for ref, row, rows, first in keys:
             scores = score(ref[pl.ds(row, rows), :], queries)
-            if masked:
-                index = lax.broadcasted_iota(jnp.int32, scores.shape, 0)
-                scores = jnp.where(index >= first, scores, -1.0)
-            top = fold(scores)
+            index = lax.broadcasted_iota(jnp.int32, scores.shape, 0)
+            top = fold(jnp.where(index >= first, scores, -1.0))
             best = top if best is None else jnp.maximum(best, top)
         best = jnp.max(best, axis=0, keepdims=True)
         col = lax.broadcasted_iota(jnp.int32, best.shape, 1) + at
@@ -97,8 +93,7 @@
         out_ref[:, cols] = jnp.maximum(out_ref[:, cols], jnp.where(col < count, best, -1.0))
         return 0
 
-    lax.fori_loop(0, jnp.where(clear, trips, 0), functools.partial(over_queries, False), 0)
-    lax.fori_loop(0, jnp.where(clear, 0, trips), functools.partial(over_queries, True), 0)
+    lax.fori_loop(0, (count + step - 1) // step, over_queries, 0)
 
 
 def own_kernel(emb_ref, labels_ref, own_out, best_out, reach_out, start, raw, sems):
@@ -156,13 +151,31 @@
     return (ref, 0, size, jnp.clip(rows - tail - at, 0, size))
 
 
-def upper(pieces, keys, up, rep, out_ref, enabled=True):
+def bundle(pieces, keys, up, rep, out_ref):
     half = TILE
-    for ref, flip, part in pieces:
-        at = (rep ^ flip) * 2 * half + part * half
-        for last, several in keys:
-            count = jnp.where(enabled, reached(up, last, at, half), 0)
-            group(several, ref, half, out_ref, at, count)
+    firsts, wanted = [], []
+    for last, enabled, (_, _, rows, first) in keys:
+        some = enabled & (up[0] == last[0]) & (first < rows)
+        firsts.append(jnp.where(some, first, rows))
+        wanted.append(some)
+    starts = [(rep ^ flip) * 2 * half + part * half for _, flip, part in pieces]
+    wanted = functools.reduce(jnp.logical_or, wanted)
+    reached_one = functools.reduce(jnp.logical_or, [up[1] > at for at in starts])
+
+    @pl.when(wanted & reached_one)
+    def _():
+        for (ref, _, _), at in zip(pieces, starts):
+            queries = ref[pl.ds(0, half), :]
+            best = None
+            for (_, _, (key_ref, row, rows, _)), first in zip(keys, firsts):
+                scores = score(key_ref[pl.ds(row, rows), :], queries)
+                index = lax.broadcasted_iota(jnp.int32, scores.shape, 0)
+                top = fold(jnp.where(index >= first, scores, -1.0))
+                best = top if best is None else jnp.maximum(best, top)
+            best = jnp.max(best, axis=0, keepdims=True)
+            col = lax.broadcasted_iota(jnp.int32, best.shape, 1) + at
+            cols = pl.ds(pl.multiple_of(at, half), half)
+            out_ref[:, cols] = jnp.maximum(out_ref[:, cols], jnp.where(col < up[1], best, -1.0))
 
 
 def near_kernel(own_reach, own_ref, best_ref, low, across, high_0a, high_0b, high_1a, high_2a,
@@ -181,8 +194,10 @@
     group(lows, own_ref, rows, best_out, 0, reached(mine, lower, 0, rows))
     count = jnp.where(odd == 1, reached(mine, beside, 0, rows), 0)
     group(besides, own_ref, rows, best_out, 0, count)
-    pieces = [(high_0a, 0, 0), (high_0b, 0, 1), (high_1a, 1, 0), (high_2a, 2, 0)]
-    upper(pieces, [(beside, besides), (lower, lows)], up, rep, high_out)
+    both = [(beside, True, besides[0]), (lower, True, lows[0])]
+    bundle([(high_0a, 0, 0), (high_0b, 0, 1)], both, up, rep, high_out)
+    bundle([(high_1a, 1, 0)], both, up, rep, high_out)
+    bundle([(high_2a, 2, 0)], both, up, rep, high_out)
 
 
 def both_keys(reach_ref, low, across):
@@ -191,8 +206,8 @@
     lower, beside, up = [(reach_ref[2 * n], reach_ref[2 * n + 1]) for n in range(3)]
     at = rep * quarter
     both = [
-        (beside, [key_piece(across, beside[1], rows, at, quarter)]),
-        (lower, [key_piece(low, lower[1], rows, at, quarter)]),
+        (beside, True, key_piece(across, beside[1], rows, at, quarter)),
+        (lower, True, key_piece(low, lower[1], rows, at, quarter)),
     ]
     return rep, up, both
 
@@ -200,42 +215,39 @@
 def middle_kernel(reach_ref, prior_ref, low, across, high_1b, high_3a, high_out):
     rep, up, both = both_keys(reach_ref, low, across)
     high_out[...] = prior_ref[...]
-    upper([(high_1b, 1, 1), (high_3a, 3, 0)], both, up, rep, high_out)
+    bundle([(high_1b, 1, 1)], both, up, rep, high_out)
+    bundle([(high_3a, 3, 0)], both, up, rep, high_out)
 
 
 def side_keys(side, sides_ref):
     quarter, rows = 2 * TILE, 8 * TILE
+    even = lax.axis_index("shard") % 2 == 0
     at = lax.axis_index("rep") * quarter
-    return [(side, [key_piece(sides_ref, side[1], rows, at, quarter)])]
+    return [(side, even, key_piece(sides_ref, side[1], rows, at, quarter))]
 
 
 def far_kernel(reach_ref, prior_ref, low, across, high_0a, high_0b, high_1a, high_1b, high_2a,
                high_2b, high_3a, side_a, side_b, high_out, side_out, sides_out):
     half = TILE
-    even = lax.axis_index("shard") % 2 == 0
     side = read_reach(side_a, 3)
     side_out[0], side_out[1] = side
-
-    @pl.when(even)
-    def _():
-        sides_out[pl.ds(0, half), :] = side_b[pl.ds(0, half), :]
-        sides_out[pl.ds(half, half), :] = side_a[pl.ds(0, half), :]
-
+    sides_out[pl.ds(0, half), :] = side_b[pl.ds(0, half), :]
+    sides_out[pl.ds(half, half), :] = side_a[pl.ds(0, half), :]
     rep, up, both = both_keys(reach_ref, low, across)
     high_out[...] = prior_ref[...]
-    upper([(high_2b, 2, 1)], both, up, rep, high_out)
-    pieces = [(high_0a, 0, 0), (high_0b, 0, 1), (high_1a, 1, 0), (high_1b, 1, 1), (high_2a, 2, 0)]
-    pieces += [(high_2b, 2, 1), (high_3a, 3, 0)]
-    upper(pieces, side_keys(side, sides_out), up, rep, high_out, even)
+    sides = side_keys(side, sides_out)
+    bundle([(high_2b, 2, 1)], both, up, rep, high_out)
+    bundle([(high_0a, 0, 0), (high_0b, 0, 1)], sides, up, rep, high_out)
+    bundle([(high_1a, 1, 0), (high_1b, 1, 1)], sides, up, rep, high_out)
+    bundle([(high_2a, 2, 0), (high_2b, 2, 1)], sides, up, rep, high_out)
+    bundle([(high_3a, 3, 0)], sides, up, rep, high_out)
 
 
 def last_kernel(reach_ref, side_ref, prior_ref, low, across, high_3b, sides, high_out):
     side = (side_ref[0], side_ref[1])
-    even = lax.axis_index("shard") % 2 == 0
     rep, up, both = both_keys(reach_ref, low, across)
     high_out[...] = prior_ref[...]
-    upper([(high_3b, 3, 1)], both, up, rep, high_out)
-    upper([(high_3b, 3, 1)], side_keys(side, sides), up, rep, high_out, even)
+    bundle([(high_3b, 3, 1)], both + side_keys(side, sides), up, rep, high_out)
 
 
 def local(embeddings, labels):

time: 69.8 us -> 67.2 us (0.963)
  Pallas kernels: 19.6 us -> 11.3 us
  waiting for transfers between devices: 26.1 us -> 29.2 us
  starting transfers between devices: 21.6 us -> 24.6 us
    pallas_call x4, Pallas kernels: 12.1 us -> 3.76 us  [call(): pl.pallas_call(kernel, out_shape=[jax.ShapeDtypeStruct(shape, dtype) for...]
    ppermute x9, waiting for transfers between devices: 3.9 us -> 5.88 us  [other_rep(): return lax.ppermute(block, 'rep', [(i, i ^ flip) for i in range(reps)])]
    ppermute x9, starting transfers between devices: 5.55 us -> 7.15 us  [other_rep(): return lax.ppermute(block, 'rep', [(i, i ^ flip) for i in range(reps)])]
    ppermute x6, starting transfers between devices: 14.5 us -> 15.9 us  [along_shard(): return lax.ppermute(block, 'shard', route)]
    ppermute x6, waiting for transfers between devices: 22.2 us -> 23.3 us  [along_shard(): return lax.ppermute(block, 'shard', route)]
  transfers between devices with their start and end apart: 16 -> 16, of which waited for: 9 -> 12; matrix products, arithmetic and copies ran while one was open for 0% -> 0% of each run, Pallas kernels for 24% -> 14%
where the time goes in v10:
time: 67.2 us; the launch traced here: 66.7 us
  waiting for transfers between devices  29.2 us (43%)
  starting transfers between devices  24.6 us (37%)
  Pallas kernels  11.3 us (17%)
  local copies, waits for them, and re-layouts  0.81 us (1%)
    ppermute x6, waiting for transfers between devices, along_shard(): return lax.ppermute(block, 'shard', route)  23.3 us
    ppermute x6, starting transfers between devices, along_shard(): return lax.ppermute(block, 'shard', route)  15.9 us
    ppermute x9, starting transfers between devices, other_rep(): return lax.ppermute(block, 'rep', [(i, i ^ flip) for i in range(reps)])  7.15 us
    pallas_call x1, Pallas kernels, local(): pl.pallas_call(own_kernel, out_shape=[jax.ShapeDtypeStruct((rows, width),...  6.02 us
    ppermute x9, waiting for transfers between devices, other_rep(): return lax.ppermute(block, 'rep', [(i, i ^ flip) for i in range(reps)])  5.88 us
    pallas_call x4, Pallas kernels, call(): pl.pallas_call(kernel, out_shape=[jax.ShapeDtypeStruct(shape, dtype) for...  3.76 us
    ppermute x1, starting transfers between devices, partner(): return lax.ppermute(block, 'shard', [(i, i ^ 1) for i in range(shards)])  1.58 us
    pallas_call x1, Pallas kernels, local(): pl.pallas_call(prepare_kernel, out_shape=[jax.ShapeDtypeStruct((size, wid...  1.47 us
  transfers between devices with their start and end apart: 16, of which 12 were waited for; matrix products, arithmetic and copies ran while one was open for 0% of the time, Pallas kernels for 14%

profile of v10, /device:TPU:8, one launch (start us, length us, event | category | flops | bytes accessed | tf_op | source)
XLA Modules:
  0.0 66.7 jit_solution(5763150305293478885)
XLA Ops:
  0.0 0.7 %copy-done = s32[2048]{0:T(1024)S(1)} copy-done((s32[2048]{0:T(1024)S(1)}, s32[2048]{0:T(1024)}, u32[]{:S(2)}) %copy-start) | copy-done | bytes 8216
  0.7 1.5 %prepare.1 = (bf16[256,1024]{1,0:T(8,128)(2,1)S(1)}, bf16[272,1024]{1,0:T(8,128)(2,1)S(1)}, bf16[528,1024]{1,0:T(8,128)(2,1)S(1)}) custom-call(bf16[2048,1024]{1,0:T(8,128)(2,1)} %emb_ref.3, s32[16,128]{1,0:T(8,128)S(1)} %bitcast.3), custom_call_target="tpu_custom_call" | custom-call | tf_op jit(solution)/shard_map/prepare/pallas_call | solution.py:283
  2.2 3.5 %collective-permute-start.2 = (bf16[528,1024]{1,0:T(8,128)(2,1)S(1)}, bf16[528,1024]{1,0:T(8,128)(2,1)S(1)}, u32[]{:S(2)}, u32[]{:S(2)}) collective-permute-start(bf16[528,1024]{1,0:T(8,128)(2,1)S(1)} %get-tuple-element.35), channel_id=1, source_target_pairs={{0,8},{4,12},{8,16},{12,20},{16,24},{20,28},{1,9},{5,13},{9,17},{1... | collective-permute-start | bytes 3244040 | tf_op jit(solution)/shard_map/ppermute | solution.py:263
  5.7 1.6 %collective-permute-start.1 = (bf16[528,1024]{1,0:T(8,128)(2,1)S(1)}, bf16[528,1024]{1,0:T(8,128)(2,1)S(1)}, u32[]{:S(2)}, u32[]{:S(2)}) collective-permute-start(bf16[528,1024]{1,0:T(8,128)(2,1)S(1)} %get-tuple-element.35), channel_id=1, source_target_pairs={{0,4},{4,0},{8,12},{12,8},{16,20},{20,16},{24,28},{28,24},{1,5},{5... | collective-permute-start | bytes 3244040 | tf_op jit(solution)/shard_map/ppermute | solution.py:266
  7.3 2.4 %collective-permute-start = (bf16[256,1024]{1,0:T(8,128)(2,1)S(1)}, bf16[256,1024]{1,0:T(8,128)(2,1)S(1)}, u32[]{:S(2)}, u32[]{:S(2)}) collective-permute-start(bf16[256,1024]{1,0:T(8,128)(2,1)S(1)} %get-tuple-element.32), channel_id=1, source_target_pairs={{8,0},{12,4},{16,8},{20,12},{24,16},{28,20},{9,1},{13,5},{17,9},{2... | collective-permute-start | bytes 1572872 | tf_op jit(solution)/shard_map/ppermute | solution.py:263
  9.7 1.9 %collective-permute-start.3 = (bf16[272,1024]{1,0:T(8,128)(2,1)S(1)}, bf16[272,1024]{1,0:T(8,128)(2,1)S(1)}, u32[]{:S(2)}, u32[]{:S(2)}) collective-permute-start(bf16[272,1024]{1,0:T(8,128)(2,1)S(1)} %get-tuple-element.40), channel_id=1, source_target_pairs={{8,0},{12,4},{16,8},{20,12},{24,16},{28,20},{9,1},{13,5},{17,9},{2... | collective-permute-start | bytes 1671176 | tf_op jit(solution)/shard_map/ppermute | solution.py:263
  11.6 12.4 %collective-permute-done.high_0a = bf16[256,1024]{1,0:T(8,128)(2,1)S(1)} collective-permute-done((bf16[256,1024]{1,0:T(8,128)(2,1)S(1)}, bf16[256,1024]{1,0:T(8,128)(2,1)S(1)}, u32[]{:S(2)}, u32[]{:S(2)}) %collective-permute-start) | collective-permute-done | bytes 524320 | tf_op jit(solution)/shard_map/ppermute | solution.py:263
  24.0 1.5 %collective-permute-start.5 = (bf16[256,1024]{1,0:T(8,128)(2,1)S(1)}, bf16[256,1024]{1,0:T(8,128)(2,1)S(1)}, u32[]{:S(2)}, u32[]{:S(2)}) collective-permute-start(bf16[256,1024]{1,0:T(8,128)(2,1)S(1)} %collective-permute-done.high_0a), channel_id=1, source_target_pairs={{0,2},{1,3},{2,0},{3,1},{4,6},{5,7},{6,4},{7,5},{8,10},{9,11},{10,... | collective-permute-start | bytes 1572872 | tf_op jit(solution)/shard_map/ppermute | solution.py:269
  25.5 6.0 %own.1 = (bf16[2048,1024]{1,0:T(8,128)(2,1)S(1)}, f32[1,2048]{1,0:T(1,128)S(1)}, s32[2]{0:T(128)S(1)}) custom-call(bf16[2048,1024]{1,0:T(8,128)(2,1)} %emb_ref.3, s32[1,2048]{1,0:T(1,128)S(1)} %bitcast.4), custom_call_target="tpu_custom_call" | custom-call | flops 1024 | bytes 1024 | tf_op jit(solution)/shard_map/own/pallas_call | solution.py:308
  31.6 2.5 %collective-permute-done.3.high_0b = bf16[272,1024]{1,0:T(8,128)(2,1)S(1)} collective-permute-done((bf16[272,1024]{1,0:T(8,128)(2,1)S(1)}, bf16[272,1024]{1,0:T(8,128)(2,1)S(1)}, u32[]{:S(2)}, u32[]{:S(2)}) %collective-permute-start.3) | collective-permute-done | bytes 557088 | tf_op jit(solution)/shard_map/ppermute | solution.py:263
  34.4 1.3 %collective-permute-start.7 = (bf16[272,1024]{1,0:T(8,128)(2,1)S(1)}, bf16[272,1024]{1,0:T(8,128)(2,1)S(1)}, u32[]{:S(2)}, u32[]{:S(2)}) collective-permute-start(bf16[272,1024]{1,0:T(8,128)(2,1)S(1)} %slice.9), channel_id=1, source_target_pairs={{4,0},{12,8},{20,16},{28,24},{5,1},{13,9},{21,17},{29,25},{6,2},{1... | collective-permute-start | bytes 1671176 | tf_op jit(solution)/shard_map/ppermute | solution.py:263
  35.7 3.5 %collective-permute-start.8 = (bf16[272,1024]{1,0:T(8,128)(2,1)S(1)}, bf16[272,1024]{1,0:T(8,128)(2,1)S(1)}, u32[]{:S(2)}, u32[]{:S(2)}) collective-permute-start(bf16[272,1024]{1,0:T(8,128)(2,1)S(1)} %slice.10), channel_id=1, source_target_pairs={{0,8},{8,16},{16,24},{1,9},{9,17},{17,25},{2,10},{10,18},{18,26},{... | collective-permute-start | bytes 1671176 | tf_op jit(solution)/shard_map/ppermute | solution.py:263
  39.2 1.6 %collective-permute-start.6 = (bf16[272,1024]{1,0:T(8,128)(2,1)S(1)}, bf16[272,1024]{1,0:T(8,128)(2,1)S(1)}, u32[]{:S(2)}, u32[]{:S(2)}) collective-permute-start(bf16[272,1024]{1,0:T(8,128)(2,1)S(1)} %collective-permute-done.3.high_0b), channel_id=1, source_target_pairs={{0,2},{1,3},{2,0},{3,1},{4,6},{5,7},{6,4},{7,5},{8,10},{9,11},{10,... | collective-permute-start | bytes 1671176 | tf_op jit(solution)/shard_map/ppermute | solution.py:269
  41.4 1.3 %near.1 = (f32[1,2048]{1,0:T(1,128)S(1)}, f32[1,2048]{1,0:T(1,128)S(1)}, s32[6]{0:T(128)S(1)}) custom-call(s32[2]{0:T(128)S(1)} %get-tuple-element.34.own_reach, bf16[2048,1024]{1,0:T(8,128)(2,1)S(1)} %get-tuple-element.38.own_ref, f32[1,2048]{1,0:T(1,128)S(1)} %get-tuple-element.39.best_ref, bf16[528,1024]{1,0:T(8,128)(2,1)S(1)} %collective-permute-done.2.low, ...), custom_call_target="tpu_custom_call" | custom-call | flops 1024 | bytes 1024 | tf_op jit(solution)/shard_map/near/pallas_call | solution.py:272
  42.8 0.7 %collective-permute-done.10.high_3a = bf16[256,1024]{1,0:T(8,128)(2,1)S(1)} collective-permute-done((bf16[256,1024]{1,0:T(8,128)(2,1)S(1)}, bf16[256,1024]{1,0:T(8,128)(2,1)S(1)}, u32[]{:S(2)}, u32[]{:S(2)}) %collective-permute-start.10) | collective-permute-done | bytes 524320 | tf_op jit(solution)/shard_map/ppermute | solution.py:269
  44.1 4.9 %collective-permute-done.7.side_a = bf16[272,1024]{1,0:T(8,128)(2,1)S(1)} collective-permute-done((bf16[272,1024]{1,0:T(8,128)(2,1)S(1)}, bf16[272,1024]{1,0:T(8,128)(2,1)S(1)}, u32[]{:S(2)}, u32[]{:S(2)}) %collective-permute-start.7) | collective-permute-done | bytes 557088 | tf_op jit(solution)/shard_map/ppermute | solution.py:263
  48.9 1.3 %collective-permute-done.8.side_b = bf16[272,1024]{1,0:T(8,128)(2,1)S(1)} collective-permute-done((bf16[272,1024]{1,0:T(8,128)(2,1)S(1)}, bf16[272,1024]{1,0:T(8,128)(2,1)S(1)}, u32[]{:S(2)}, u32[]{:S(2)}) %collective-permute-start.8) | collective-permute-done | bytes 557088 | tf_op jit(solution)/shard_map/ppermute | solution.py:263
  50.2 1.4 %collective-permute-done.6.high_2b = bf16[272,1024]{1,0:T(8,128)(2,1)S(1)} collective-permute-done((bf16[272,1024]{1,0:T(8,128)(2,1)S(1)}, bf16[272,1024]{1,0:T(8,128)(2,1)S(1)}, u32[]{:S(2)}, u32[]{:S(2)}) %collective-permute-start.6) | collective-permute-done | bytes 557088 | tf_op jit(solution)/shard_map/ppermute | solution.py:269
  51.6 1.3 %far.1 = (f32[1,2048]{1,0:T(1,128)S(1)}, s32[2]{0:T(128)S(1)}, bf16[512,1024]{1,0:T(8,128)(2,1)S(1)}) custom-call(s32[6]{0:T(128)S(1)} %get-tuple-element.50.reach_ref, f32[1,2048]{1,0:T(1,128)S(1)} %middle.1.prior_ref, bf16[528,1024]{1,0:T(8,128)(2,1)S(1)} %collective-permute-done.2.low, bf16[528,1024]{1,0:T(8,128)(2,1)S(1)} %collective-permute-done.1.across, ...), custom_call_target="tpu_custom_call" | custom-call | flops 1024 | bytes 1024 | tf_op jit(solution)/shard_map/far/pallas_call | solution.py:272
  54.2 3.3 %collective-permute-start.12 = (f32[1,2048]{1,0:T(1,128)S(1)}, f32[1,2048]{1,0:T(1,128)S(1)}, u32[]{:S(2)}, u32[]{:S(2)}) collective-permute-start(f32[1,2048]{1,0:T(1,128)S(1)} %last.1), channel_id=1, source_target_pairs={{0,8},{4,12},{8,16},{12,20},{16,24},{20,28},{1,9},{5,13},{9,17},{1... | collective-permute-start | bytes 24584 | tf_op jit(solution)/shard_map/ppermute | solution.py:263
  57.5 2.2 %collective-permute-done.12 = f32[1,2048]{1,0:T(1,128)S(1)} collective-permute-done((f32[1,2048]{1,0:T(1,128)S(1)}, f32[1,2048]{1,0:T(1,128)S(1)}, u32[]{:S(2)}, u32[]{:S(2)}) %collective-permute-start.12) | collective-permute-done | bytes 8224 | tf_op jit(solution)/shard_map/ppermute | solution.py:263
  59.7 2.7 %collective-permute-start.15 = (f32[1,2048]{1,0:T(1,128)S(1)}, f32[1,2048]{1,0:T(1,128)S(1)}, u32[]{:S(2)}, u32[]{:S(2)}) collective-permute-start(f32[1,2048]{1,0:T(1,128)S(1)} %fusion), channel_id=1, source_target_pairs={{0,3},{1,2},{2,1},{3,0},{4,7},{5,6},{6,5},{7,4},{8,11},{9,10},{10,... | collective-permute-start | bytes 24584 | tf_op jit(solution)/shard_map/ppermute | solution.py:269
  62.4 0.8 %collective-permute-start.14 = (f32[1,2048]{1,0:T(1,128)S(1)}, f32[1,2048]{1,0:T(1,128)S(1)}, u32[]{:S(2)}, u32[]{:S(2)}) collective-permute-start(f32[1,2048]{1,0:T(1,128)S(1)} %fusion), channel_id=1, source_target_pairs={{0,2},{1,3},{2,0},{3,1},{4,6},{5,7},{6,4},{7,5},{8,10},{9,11},{10,... | collective-permute-start | bytes 24584 | tf_op jit(solution)/shard_map/ppermute | solution.py:269
  63.8 2.3 %collective-permute-done.14 = f32[1,2048]{1,0:T(1,128)S(1)} collective-permute-done((f32[1,2048]{1,0:T(1,128)S(1)}, f32[1,2048]{1,0:T(1,128)S(1)}, u32[]{:S(2)}, u32[]{:S(2)}) %collective-permute-start.14) | collective-permute-done | bytes 8224 | tf_op jit(solution)/shard_map/ppermute | solution.py:269
  (23 shorter events, 4.0 us)
Async XLA Ops:
  0.0 0.7 %copy-start = (s32[2048]{0:T(1024)S(1)}, s32[2048]{0:T(1024)}, u32[]{:S(2)}) copy-start(s32[2048]{0:T(1024)} %param.3) | copy-start | bytes 24580
  0.7 24.8 %copy-start.1 = (s32[2048]{0:T(1024)S(1)}, s32[2048]{0:T(1024)}, u32[]{:S(2)}) copy-start(s32[2048]{0:T(1024)} %param.3) | copy-start | bytes 24580
  2.2 29.4 %collective-permute-start.2 = (bf16[528,1024]{1,0:T(8,128)(2,1)S(1)}, bf16[528,1024]{1,0:T(8,128)(2,1)S(1)}, u32[]{:S(2)}, u32[]{:S(2)}) collective-permute-start(bf16[528,1024]{1,0:T(8,128)(2,1)S(1)} %get-tuple-element.35), channel_id=1, source_target_pairs={{0,8},{4,12},{8,16},{12,20},{16,24},{20,28},{1,9},{5,13},{9,17},{1... | collective-permute-start | bytes 3244040 | tf_op jit(solution)/shard_map/ppermute | solution.py:263
  5.7 25.9 %collective-permute-start.1 = (bf16[528,1024]{1,0:T(8,128)(2,1)S(1)}, bf16[528,1024]{1,0:T(8,128)(2,1)S(1)}, u32[]{:S(2)}, u32[]{:S(2)}) collective-permute-start(bf16[528,1024]{1,0:T(8,128)(2,1)S(1)} %get-tuple-element.35), channel_id=1, source_target_pairs={{0,4},{4,0},{8,12},{12,8},{16,20},{20,16},{24,28},{28,24},{1,5},{5... | collective-permute-start | bytes 3244040 | tf_op jit(solution)/shard_map/ppermute | solution.py:266
  7.3 16.7 %collective-permute-start = (bf16[256,1024]{1,0:T(8,128)(2,1)S(1)}, bf16[256,1024]{1,0:T(8,128)(2,1)S(1)}, u32[]{:S(2)}, u32[]{:S(2)}) collective-permute-start(bf16[256,1024]{1,0:T(8,128)(2,1)S(1)} %get-tuple-element.32), channel_id=1, source_target_pairs={{8,0},{12,4},{16,8},{20,12},{24,16},{28,20},{9,1},{13,5},{17,9},{2... | collective-permute-start | bytes 1572872 | tf_op jit(solution)/shard_map/ppermute | solution.py:263
  9.7 24.5 %collective-permute-start.3 = (bf16[272,1024]{1,0:T(8,128)(2,1)S(1)}, bf16[272,1024]{1,0:T(8,128)(2,1)S(1)}, u32[]{:S(2)}, u32[]{:S(2)}) collective-permute-start(bf16[272,1024]{1,0:T(8,128)(2,1)S(1)} %get-tuple-element.40), channel_id=1, source_target_pairs={{8,0},{12,4},{16,8},{20,12},{24,16},{28,20},{9,1},{13,5},{17,9},{2... | collective-permute-start | bytes 1671176 | tf_op jit(solution)/shard_map/ppermute | solution.py:263
  24.0 10.4 %collective-permute-start.5 = (bf16[256,1024]{1,0:T(8,128)(2,1)S(1)}, bf16[256,1024]{1,0:T(8,128)(2,1)S(1)}, u32[]{:S(2)}, u32[]{:S(2)}) collective-permute-start(bf16[256,1024]{1,0:T(8,128)(2,1)S(1)} %collective-permute-done.high_0a), channel_id=1, source_target_pairs={{0,2},{1,3},{2,0},{3,1},{4,6},{5,7},{6,4},{7,5},{8,10},{9,11},{10,... | collective-permute-start | bytes 1572872 | tf_op jit(solution)/shard_map/ppermute | solution.py:269
  25.5 8.9 %collective-permute-start.4 = (bf16[256,1024]{1,0:T(8,128)(2,1)S(1)}, bf16[256,1024]{1,0:T(8,128)(2,1)S(1)}, u32[]{:S(2)}, u32[]{:S(2)}) collective-permute-start(bf16[256,1024]{1,0:T(8,128)(2,1)S(1)} %collective-permute-done.high_0a), channel_id=1, source_target_pairs={{0,1},{1,0},{2,3},{3,2},{4,5},{5,4},{6,7},{7,6},{8,9},{9,8},{10,11... | collective-permute-start | bytes 1572872 | tf_op jit(solution)/shard_map/ppermute | solution.py:269
  34.4 14.5 %collective-permute-start.7 = (bf16[272,1024]{1,0:T(8,128)(2,1)S(1)}, bf16[272,1024]{1,0:T(8,128)(2,1)S(1)}, u32[]{:S(2)}, u32[]{:S(2)}) collective-permute-start(bf16[272,1024]{1,0:T(8,128)(2,1)S(1)} %slice.9), channel_id=1, source_target_pairs={{4,0},{12,8},{20,16},{28,24},{5,1},{13,9},{21,17},{29,25},{6,2},{1... | collective-permute-start | bytes 1671176 | tf_op jit(solution)/shard_map/ppermute | solution.py:263
  35.7 14.5 %collective-permute-start.8 = (bf16[272,1024]{1,0:T(8,128)(2,1)S(1)}, bf16[272,1024]{1,0:T(8,128)(2,1)S(1)}, u32[]{:S(2)}, u32[]{:S(2)}) collective-permute-start(bf16[272,1024]{1,0:T(8,128)(2,1)S(1)} %slice.10), channel_id=1, source_target_pairs={{0,8},{8,16},{16,24},{1,9},{9,17},{17,25},{2,10},{10,18},{18,26},{... | collective-permute-start | bytes 1671176 | tf_op jit(solution)/shard_map/ppermute | solution.py:263
  39.2 12.4 %collective-permute-start.6 = (bf16[272,1024]{1,0:T(8,128)(2,1)S(1)}, bf16[272,1024]{1,0:T(8,128)(2,1)S(1)}, u32[]{:S(2)}, u32[]{:S(2)}) collective-permute-start(bf16[272,1024]{1,0:T(8,128)(2,1)S(1)} %collective-permute-done.3.high_0b), channel_id=1, source_target_pairs={{0,2},{1,3},{2,0},{3,1},{4,6},{5,7},{6,4},{7,5},{8,10},{9,11},{10,... | collective-permute-start | bytes 1671176 | tf_op jit(solution)/shard_map/ppermute | solution.py:269
  40.8 2.0 %collective-permute-start.9 = (bf16[256,1024]{1,0:T(8,128)(2,1)S(1)}, bf16[256,1024]{1,0:T(8,128)(2,1)S(1)}, u32[]{:S(2)}, u32[]{:S(2)}) collective-permute-start(bf16[256,1024]{1,0:T(8,128)(2,1)S(1)} %slice.11), channel_id=1, source_target_pairs={{0,1},{1,0},{2,3},{3,2},{4,5},{5,4},{6,7},{7,6},{8,9},{9,8},{10,11... | collective-permute-start | bytes 1572872 | tf_op jit(solution)/shard_map/ppermute | solution.py:269
  40.9 2.6 %collective-permute-start.10 = (bf16[256,1024]{1,0:T(8,128)(2,1)S(1)}, bf16[256,1024]{1,0:T(8,128)(2,1)S(1)}, u32[]{:S(2)}, u32[]{:S(2)}) collective-permute-start(bf16[256,1024]{1,0:T(8,128)(2,1)S(1)} %collective-permute-done.5.high_2a), channel_id=1, source_target_pairs={{0,1},{1,0},{2,3},{3,2},{4,5},{5,4},{6,7},{7,6},{8,9},{9,8},{10,11... | collective-permute-start | bytes 1572872 | tf_op jit(solution)/shard_map/ppermute | solution.py:269
  51.6 2.0 %collective-permute-start.11 = (bf16[272,1024]{1,0:T(8,128)(2,1)S(1)}, bf16[272,1024]{1,0:T(8,128)(2,1)S(1)}, u32[]{:S(2)}, u32[]{:S(2)}) collective-permute-start(bf16[272,1024]{1,0:T(8,128)(2,1)S(1)} %collective-permute-done.6.high_2b), channel_id=1, source_target_pairs={{0,1},{1,0},{2,3},{3,2},{4,5},{5,4},{6,7},{7,6},{8,9},{9,8},{10,11... | collective-permute-start | bytes 1671176 | tf_op jit(solution)/shard_map/ppermute | solution.py:269
  54.2 5.5 %collective-permute-start.12 = (f32[1,2048]{1,0:T(1,128)S(1)}, f32[1,2048]{1,0:T(1,128)S(1)}, u32[]{:S(2)}, u32[]{:S(2)}) collective-permute-start(f32[1,2048]{1,0:T(1,128)S(1)} %last.1), channel_id=1, source_target_pairs={{0,8},{4,12},{8,16},{12,20},{16,24},{20,28},{1,9},{5,13},{9,17},{1... | collective-permute-start | bytes 24584 | tf_op jit(solution)/shard_map/ppermute | solution.py:263
  59.7 4.0 %collective-permute-start.15 = (f32[1,2048]{1,0:T(1,128)S(1)}, f32[1,2048]{1,0:T(1,128)S(1)}, u32[]{:S(2)}, u32[]{:S(2)}) collective-permute-start(f32[1,2048]{1,0:T(1,128)S(1)} %fusion), channel_id=1, source_target_pairs={{0,3},{1,2},{2,1},{3,0},{4,7},{5,6},{6,5},{7,4},{8,11},{9,10},{10,... | collective-permute-start | bytes 24584 | tf_op jit(solution)/shard_map/ppermute | solution.py:269
  62.4 3.7 %collective-permute-start.14 = (f32[1,2048]{1,0:T(1,128)S(1)}, f32[1,2048]{1,0:T(1,128)S(1)}, u32[]{:S(2)}, u32[]{:S(2)}) collective-permute-start(f32[1,2048]{1,0:T(1,128)S(1)} %fusion), channel_id=1, source_target_pairs={{0,2},{1,3},{2,0},{3,1},{4,6},{5,7},{6,4},{7,5},{8,10},{9,11},{10,... | collective-permute-start | bytes 24584 | tf_op jit(solution)/shard_map/ppermute | solution.py:269
  63.2 2.8 %collective-permute-start.13 = (f32[1,2048]{1,0:T(1,128)S(1)}, f32[1,2048]{1,0:T(1,128)S(1)}, u32[]{:S(2)}, u32[]{:S(2)}) collective-permute-start(f32[1,2048]{1,0:T(1,128)S(1)} %fusion), channel_id=1, source_target_pairs={{0,1},{1,0},{2,3},{3,2},{4,5},{5,4},{6,7},{7,6},{8,9},{9,8},{10,11... | collective-permute-start | bytes 24584 | tf_op jit(solution)/shard_map/ppermute | solution.py:269

commit v11 on v10

--- a/solution.py
+++ b/solution.py
@@ -328,8 +328,9 @@
     side_b = along_shard(across[: half + INFO], 2, even_only)
     side_a = along_shard(low[half:], -1, odd_only)
     high_0b, high_1a, high_2a, across, low = fence((high_0b, high_1a, high_2a, across, low))
-    high_2b = other_rep(high_0b, 2)
-    high_1b = other_rep(high_0b[:half], 1)
+    rest = high_0b[:half]
+    high_2b = other_rep(rest, 2)
+    high_1b = other_rep(rest, 1)
     high_3a = other_rep(high_2a, 1)
     line = ((1, rows), F32)
     best, of_high, reach = call(

time: 67.2 us -> 65.9 us (0.981)
  the two profiles are of different devices: /device:TPU:8 before, /device:TPU:0 now
where the time goes in v11:
time: 65.9 us; the launch traced here: 65.3 us
  waiting for transfers between devices  24.2 us (37%)
  starting transfers between devices  21.4 us (32%)
  Pallas kernels  18.1 us (27%)
  local copies, waits for them, and re-layouts  0.81 us (1%)
    ppermute x6, waiting for transfers between devices, along_shard(): return lax.ppermute(block, 'shard', route)  15.5 us
    ppermute x6, starting transfers between devices, along_shard(): return lax.ppermute(block, 'shard', route)  14.8 us
    pallas_call x4, Pallas kernels, call(): pl.pallas_call(kernel, out_shape=[jax.ShapeDtypeStruct(shape, dtype) for...  10.6 us
    ppermute x9, waiting for transfers between devices, other_rep(): return lax.ppermute(block, 'rep', [(i, i ^ flip) for i in range(reps)])  8.68 us
    pallas_call x1, Pallas kernels, local(): pl.pallas_call(own_kernel, out_shape=[jax.ShapeDtypeStruct((rows, width),...  6.02 us
    ppermute x9, starting transfers between devices, other_rep(): return lax.ppermute(block, 'rep', [(i, i ^ flip) for i in range(reps)])  4.99 us
    ppermute x1, starting transfers between devices, partner(): return lax.ppermute(block, 'shard', [(i, i ^ 1) for i in range(shards)])  1.58 us
    pallas_call x1, Pallas kernels, local(): pl.pallas_call(prepare_kernel, out_shape=[jax.ShapeDtypeStruct((size, wid...  1.47 us
  transfers between devices with their start and end apart: 16, of which 5 were waited for; matrix products, arithmetic and copies ran while one was open for 0% of the time, Pallas kernels for 23%

profile of v11, /device:TPU:0, one launch (start us, length us, event | category | flops | bytes accessed | tf_op | source)
XLA Modules:
  0.0 65.3 jit_solution(16903266886737231504)
XLA Ops:
  0.0 0.7 %copy-done = s32[2048]{0:T(1024)S(1)} copy-done((s32[2048]{0:T(1024)S(1)}, s32[2048]{0:T(1024)}, u32[]{:S(2)}) %copy-start) | copy-done | bytes 8216
  0.7 1.5 %prepare.1 = (bf16[256,1024]{1,0:T(8,128)(2,1)S(1)}, bf16[272,1024]{1,0:T(8,128)(2,1)S(1)}, bf16[528,1024]{1,0:T(8,128)(2,1)S(1)}) custom-call(bf16[2048,1024]{1,0:T(8,128)(2,1)} %emb_ref.3, s32[16,128]{1,0:T(8,128)S(1)} %bitcast.3), custom_call_target="tpu_custom_call" | custom-call | tf_op jit(solution)/shard_map/prepare/pallas_call | solution.py:283
  2.2 5.0 %collective-permute-start.2 = (bf16[528,1024]{1,0:T(8,128)(2,1)S(1)}, bf16[528,1024]{1,0:T(8,128)(2,1)S(1)}, u32[]{:S(2)}, u32[]{:S(2)}) collective-permute-start(bf16[528,1024]{1,0:T(8,128)(2,1)S(1)} %get-tuple-element.35), channel_id=1, source_target_pairs={{0,8},{4,12},{8,16},{12,20},{16,24},{20,28},{1,9},{5,13},{9,17},{1... | collective-permute-start | bytes 3244040 | tf_op jit(solution)/shard_map/ppermute | solution.py:263
  7.2 1.6 %collective-permute-start.1 = (bf16[528,1024]{1,0:T(8,128)(2,1)S(1)}, bf16[528,1024]{1,0:T(8,128)(2,1)S(1)}, u32[]{:S(2)}, u32[]{:S(2)}) collective-permute-start(bf16[528,1024]{1,0:T(8,128)(2,1)S(1)} %get-tuple-element.35), channel_id=1, source_target_pairs={{0,4},{4,0},{8,12},{12,8},{16,20},{20,16},{24,28},{28,24},{1,5},{5... | collective-permute-start | bytes 3244040 | tf_op jit(solution)/shard_map/ppermute | solution.py:266
  8.8 1.3 %collective-permute-start = (bf16[256,1024]{1,0:T(8,128)(2,1)S(1)}, bf16[256,1024]{1,0:T(8,128)(2,1)S(1)}, u32[]{:S(2)}, u32[]{:S(2)}) collective-permute-start(bf16[256,1024]{1,0:T(8,128)(2,1)S(1)} %get-tuple-element.32), channel_id=1, source_target_pairs={{8,0},{12,4},{16,8},{20,12},{24,16},{28,20},{9,1},{13,5},{17,9},{2... | collective-permute-start | bytes 1572872 | tf_op jit(solution)/shard_map/ppermute | solution.py:263
  10.1 1.3 %collective-permute-start.3 = (bf16[272,1024]{1,0:T(8,128)(2,1)S(1)}, bf16[272,1024]{1,0:T(8,128)(2,1)S(1)}, u32[]{:S(2)}, u32[]{:S(2)}) collective-permute-start(bf16[272,1024]{1,0:T(8,128)(2,1)S(1)} %get-tuple-element.40), channel_id=1, source_target_pairs={{8,0},{12,4},{16,8},{20,12},{24,16},{28,20},{9,1},{13,5},{17,9},{2... | collective-permute-start | bytes 1671176 | tf_op jit(solution)/shard_map/ppermute | solution.py:263
  11.4 14.2 %collective-permute-done.high_0a = bf16[256,1024]{1,0:T(8,128)(2,1)S(1)} collective-permute-done((bf16[256,1024]{1,0:T(8,128)(2,1)S(1)}, bf16[256,1024]{1,0:T(8,128)(2,1)S(1)}, u32[]{:S(2)}, u32[]{:S(2)}) %collective-permute-start) | collective-permute-done | bytes 524320 | tf_op jit(solution)/shard_map/ppermute | solution.py:263
  25.5 1.5 %collective-permute-start.5 = (bf16[256,1024]{1,0:T(8,128)(2,1)S(1)}, bf16[256,1024]{1,0:T(8,128)(2,1)S(1)}, u32[]{:S(2)}, u32[]{:S(2)}) collective-permute-start(bf16[256,1024]{1,0:T(8,128)(2,1)S(1)} %collective-permute-done.high_0a), channel_id=1, source_target_pairs={{0,2},{1,3},{2,0},{3,1},{4,6},{5,7},{6,4},{7,5},{8,10},{9,11},{10,... | collective-permute-start | bytes 1572872 | tf_op jit(solution)/shard_map/ppermute | solution.py:269
  27.0 6.0 %own.1 = (bf16[2048,1024]{1,0:T(8,128)(2,1)S(1)}, f32[1,2048]{1,0:T(1,128)S(1)}, s32[2]{0:T(128)S(1)}) custom-call(bf16[2048,1024]{1,0:T(8,128)(2,1)} %emb_ref.3, s32[1,2048]{1,0:T(1,128)S(1)} %bitcast.4), custom_call_target="tpu_custom_call" | custom-call | flops 1024 | bytes 1024 | tf_op jit(solution)/shard_map/own/pallas_call | solution.py:308
  33.1 1.3 %collective-permute-start.7 = (bf16[272,1024]{1,0:T(8,128)(2,1)S(1)}, bf16[272,1024]{1,0:T(8,128)(2,1)S(1)}, u32[]{:S(2)}, u32[]{:S(2)}) collective-permute-start(bf16[272,1024]{1,0:T(8,128)(2,1)S(1)} %slice.10), channel_id=1, source_target_pairs={{4,0},{12,8},{20,16},{28,24},{5,1},{13,9},{21,17},{29,25},{6,2},{1... | collective-permute-start | bytes 1671176 | tf_op jit(solution)/shard_map/ppermute | solution.py:263
  34.4 3.5 %collective-permute-start.8 = (bf16[272,1024]{1,0:T(8,128)(2,1)S(1)}, bf16[272,1024]{1,0:T(8,128)(2,1)S(1)}, u32[]{:S(2)}, u32[]{:S(2)}) collective-permute-start(bf16[272,1024]{1,0:T(8,128)(2,1)S(1)} %slice.11), channel_id=1, source_target_pairs={{0,8},{8,16},{16,24},{1,9},{9,17},{17,25},{2,10},{10,18},{18,26},{... | collective-permute-start | bytes 1671176 | tf_op jit(solution)/shard_map/ppermute | solution.py:263
  38.6 1.0 %collective-permute-start.6 = (bf16[256,1024]{1,0:T(8,128)(2,1)S(1)}, bf16[256,1024]{1,0:T(8,128)(2,1)S(1)}, u32[]{:S(2)}, u32[]{:S(2)}) collective-permute-start(bf16[256,1024]{1,0:T(8,128)(2,1)S(1)} %slice.9), channel_id=1, source_target_pairs={{0,2},{1,3},{2,0},{3,1},{4,6},{5,7},{6,4},{7,5},{8,10},{9,11},{10,... | collective-permute-start | bytes 1572872 | tf_op jit(solution)/shard_map/ppermute | solution.py:269
  39.6 4.9 %near.1 = (f32[1,2048]{1,0:T(1,128)S(1)}, f32[1,2048]{1,0:T(1,128)S(1)}, s32[6]{0:T(128)S(1)}) custom-call(s32[2]{0:T(128)S(1)} %get-tuple-element.34.own_reach, bf16[2048,1024]{1,0:T(8,128)(2,1)S(1)} %get-tuple-element.38.own_ref, f32[1,2048]{1,0:T(1,128)S(1)} %get-tuple-element.39.best_ref, bf16[528,1024]{1,0:T(8,128)(2,1)S(1)} %collective-permute-done.2.low, ...), custom_call_target="tpu_custom_call" | custom-call | flops 1024 | bytes 1024 | tf_op jit(solution)/shard_map/near/pallas_call | solution.py:272
  44.5 2.1 %middle.1.prior_ref = f32[1,2048]{1,0:T(1,128)S(1)} custom-call(s32[6]{0:T(128)S(1)} %get-tuple-element.50.reach_ref, f32[1,2048]{1,0:T(1,128)S(1)} %get-tuple-element.51.prior_ref, bf16[528,1024]{1,0:T(8,128)(2,1)S(1)} %collective-permute-done.2.low, bf16[528,1024]{1,0:T(8,128)(2,1)S(1)} %collective-permute-done.1.across, ...), custom_call_target="tpu_custom_call" | custom-call | flops 1024 | bytes 1024 | tf_op jit(solution)/shard_map/middle/pallas_call | solution.py:272
  46.6 6.0 %collective-permute-done.6.high_2b = bf16[256,1024]{1,0:T(8,128)(2,1)S(1)} collective-permute-done((bf16[256,1024]{1,0:T(8,128)(2,1)S(1)}, bf16[256,1024]{1,0:T(8,128)(2,1)S(1)}, u32[]{:S(2)}, u32[]{:S(2)}) %collective-permute-start.6) | collective-permute-done | bytes 524320 | tf_op jit(solution)/shard_map/ppermute | solution.py:269
  52.6 2.0 %far.1 = (f32[1,2048]{1,0:T(1,128)S(1)}, s32[2]{0:T(128)S(1)}, bf16[512,1024]{1,0:T(8,128)(2,1)S(1)}) custom-call(s32[6]{0:T(128)S(1)} %get-tuple-element.50.reach_ref, f32[1,2048]{1,0:T(1,128)S(1)} %middle.1.prior_ref, bf16[528,1024]{1,0:T(8,128)(2,1)S(1)} %collective-permute-done.2.low, bf16[528,1024]{1,0:T(8,128)(2,1)S(1)} %collective-permute-done.1.across, ...), custom_call_target="tpu_custom_call" | custom-call | flops 1024 | bytes 1024 | tf_op jit(solution)/shard_map/far/pallas_call | solution.py:272
  54.7 1.6 %last.1 = f32[1,2048]{1,0:T(1,128)S(1)} custom-call(s32[6]{0:T(128)S(1)} %get-tuple-element.50.reach_ref, s32[2]{0:T(128)S(1)} %get-tuple-element.56.side_ref, f32[1,2048]{1,0:T(1,128)S(1)} %get-tuple-element.57.prior_ref, bf16[528,1024]{1,0:T(8,128)(2,1)S(1)} %collective-permute-done.2.low, bf16[528,1024]{1,0:T(8,128)(2,1)S(1)} %collective-permute-done.1.across, ...), custom_call_target="tpu_custom_call" | custom-call | flops 1024 | bytes 1024 | tf_op jit(solution)/shard_map/last/pallas_call | solution.py:272
  56.3 2.5 %collective-permute-start.12 = (f32[1,2048]{1,0:T(1,128)S(1)}, f32[1,2048]{1,0:T(1,128)S(1)}, u32[]{:S(2)}, u32[]{:S(2)}) collective-permute-start(f32[1,2048]{1,0:T(1,128)S(1)} %last.1), channel_id=1, source_target_pairs={{0,8},{4,12},{8,16},{12,20},{16,24},{20,28},{1,9},{5,13},{9,17},{1... | collective-permute-start | bytes 24584 | tf_op jit(solution)/shard_map/ppermute | solution.py:263
  58.8 1.3 %collective-permute-done.12 = f32[1,2048]{1,0:T(1,128)S(1)} collective-permute-done((f32[1,2048]{1,0:T(1,128)S(1)}, f32[1,2048]{1,0:T(1,128)S(1)}, u32[]{:S(2)}, u32[]{:S(2)}) %collective-permute-start.12) | collective-permute-done | bytes 8224 | tf_op jit(solution)/shard_map/ppermute | solution.py:263
  60.1 0.9 %collective-permute-start.15 = (f32[1,2048]{1,0:T(1,128)S(1)}, f32[1,2048]{1,0:T(1,128)S(1)}, u32[]{:S(2)}, u32[]{:S(2)}) collective-permute-start(f32[1,2048]{1,0:T(1,128)S(1)} %fusion), channel_id=1, source_target_pairs={{0,3},{1,2},{2,1},{3,0},{4,7},{5,6},{6,5},{7,4},{8,11},{9,10},{10,... | collective-permute-start | bytes 24584 | tf_op jit(solution)/shard_map/ppermute | solution.py:269
  61.0 0.8 %collective-permute-start.14 = (f32[1,2048]{1,0:T(1,128)S(1)}, f32[1,2048]{1,0:T(1,128)S(1)}, u32[]{:S(2)}, u32[]{:S(2)}) collective-permute-start(f32[1,2048]{1,0:T(1,128)S(1)} %fusion), channel_id=1, source_target_pairs={{0,2},{1,3},{2,0},{3,1},{4,6},{5,7},{6,4},{7,5},{8,10},{9,11},{10,... | collective-permute-start | bytes 24584 | tf_op jit(solution)/shard_map/ppermute | solution.py:269
  62.0 1.2 %collective-permute-done.15 = f32[1,2048]{1,0:T(1,128)S(1)} collective-permute-done((f32[1,2048]{1,0:T(1,128)S(1)}, f32[1,2048]{1,0:T(1,128)S(1)}, u32[]{:S(2)}, u32[]{:S(2)}) %collective-permute-start.15) | collective-permute-done | bytes 8224 | tf_op jit(solution)/shard_map/ppermute | solution.py:269
  63.3 1.4 %collective-permute-done.14 = f32[1,2048]{1,0:T(1,128)S(1)} collective-permute-done((f32[1,2048]{1,0:T(1,128)S(1)}, f32[1,2048]{1,0:T(1,128)S(1)}, u32[]{:S(2)}, u32[]{:S(2)}) %collective-permute-start.14) | collective-permute-done | bytes 8224 | tf_op jit(solution)/shard_map/ppermute | solution.py:269
  64.7 0.6 maximum_maximum_fusion
  (23 shorter events, 1.0 us)
Async XLA Ops:
  0.0 0.7 %copy-start = (s32[2048]{0:T(1024)S(1)}, s32[2048]{0:T(1024)}, u32[]{:S(2)}) copy-start(s32[2048]{0:T(1024)} %param.3) | copy-start | bytes 24580
  0.7 26.3 %copy-start.1 = (s32[2048]{0:T(1024)S(1)}, s32[2048]{0:T(1024)}, u32[]{:S(2)}) copy-start(s32[2048]{0:T(1024)} %param.3) | copy-start | bytes 24580
  2.2 30.9 %collective-permute-start.2 = (bf16[528,1024]{1,0:T(8,128)(2,1)S(1)}, bf16[528,1024]{1,0:T(8,128)(2,1)S(1)}, u32[]{:S(2)}, u32[]{:S(2)}) collective-permute-start(bf16[528,1024]{1,0:T(8,128)(2,1)S(1)} %get-tuple-element.35), channel_id=1, source_target_pairs={{0,8},{4,12},{8,16},{12,20},{16,24},{20,28},{1,9},{5,13},{9,17},{1... | collective-permute-start | bytes 3244040 | tf_op jit(solution)/shard_map/ppermute | solution.py:263
  7.2 25.9 %collective-permute-start.1 = (bf16[528,1024]{1,0:T(8,128)(2,1)S(1)}, bf16[528,1024]{1,0:T(8,128)(2,1)S(1)}, u32[]{:S(2)}, u32[]{:S(2)}) collective-permute-start(bf16[528,1024]{1,0:T(8,128)(2,1)S(1)} %get-tuple-element.35), channel_id=1, source_target_pairs={{0,4},{4,0},{8,12},{12,8},{16,20},{20,16},{24,28},{28,24},{1,5},{5... | collective-permute-start | bytes 3244040 | tf_op jit(solution)/shard_map/ppermute | solution.py:266
  8.8 16.7 %collective-permute-start = (bf16[256,1024]{1,0:T(8,128)(2,1)S(1)}, bf16[256,1024]{1,0:T(8,128)(2,1)S(1)}, u32[]{:S(2)}, u32[]{:S(2)}) collective-permute-start(bf16[256,1024]{1,0:T(8,128)(2,1)S(1)} %get-tuple-element.32), channel_id=1, source_target_pairs={{8,0},{12,4},{16,8},{20,12},{24,16},{28,20},{9,1},{13,5},{17,9},{2... | collective-permute-start | bytes 1572872 | tf_op jit(solution)/shard_map/ppermute | solution.py:263
  10.1 27.9 %collective-permute-start.3 = (bf16[272,1024]{1,0:T(8,128)(2,1)S(1)}, bf16[272,1024]{1,0:T(8,128)(2,1)S(1)}, u32[]{:S(2)}, u32[]{:S(2)}) collective-permute-start(bf16[272,1024]{1,0:T(8,128)(2,1)S(1)} %get-tuple-element.40), channel_id=1, source_target_pairs={{8,0},{12,4},{16,8},{20,12},{24,16},{28,20},{9,1},{13,5},{17,9},{2... | collective-permute-start | bytes 1671176 | tf_op jit(solution)/shard_map/ppermute | solution.py:263
  25.5 12.4 %collective-permute-start.5 = (bf16[256,1024]{1,0:T(8,128)(2,1)S(1)}, bf16[256,1024]{1,0:T(8,128)(2,1)S(1)}, u32[]{:S(2)}, u32[]{:S(2)}) collective-permute-start(bf16[256,1024]{1,0:T(8,128)(2,1)S(1)} %collective-permute-done.high_0a), channel_id=1, source_target_pairs={{0,2},{1,3},{2,0},{3,1},{4,6},{5,7},{6,4},{7,5},{8,10},{9,11},{10,... | collective-permute-start | bytes 1572872 | tf_op jit(solution)/shard_map/ppermute | solution.py:269
  27.0 10.9 %collective-permute-start.4 = (bf16[256,1024]{1,0:T(8,128)(2,1)S(1)}, bf16[256,1024]{1,0:T(8,128)(2,1)S(1)}, u32[]{:S(2)}, u32[]{:S(2)}) collective-permute-start(bf16[256,1024]{1,0:T(8,128)(2,1)S(1)} %collective-permute-done.high_0a), channel_id=1, source_target_pairs={{0,1},{1,0},{2,3},{3,2},{4,5},{5,4},{6,7},{7,6},{8,9},{9,8},{10,11... | collective-permute-start | bytes 1572872 | tf_op jit(solution)/shard_map/ppermute | solution.py:269
  33.1 19.5 %collective-permute-start.7 = (bf16[272,1024]{1,0:T(8,128)(2,1)S(1)}, bf16[272,1024]{1,0:T(8,128)(2,1)S(1)}, u32[]{:S(2)}, u32[]{:S(2)}) collective-permute-start(bf16[272,1024]{1,0:T(8,128)(2,1)S(1)} %slice.10), channel_id=1, source_target_pairs={{4,0},{12,8},{20,16},{28,24},{5,1},{13,9},{21,17},{29,25},{6,2},{1... | collective-permute-start | bytes 1671176 | tf_op jit(solution)/shard_map/ppermute | solution.py:263
  34.4 18.2 %collective-permute-start.8 = (bf16[272,1024]{1,0:T(8,128)(2,1)S(1)}, bf16[272,1024]{1,0:T(8,128)(2,1)S(1)}, u32[]{:S(2)}, u32[]{:S(2)}) collective-permute-start(bf16[272,1024]{1,0:T(8,128)(2,1)S(1)} %slice.11), channel_id=1, source_target_pairs={{0,8},{8,16},{16,24},{1,9},{9,17},{17,25},{2,10},{10,18},{18,26},{... | collective-permute-start | bytes 1671176 | tf_op jit(solution)/shard_map/ppermute | solution.py:263
  38.0 6.5 %collective-permute-start.9 = (bf16[256,1024]{1,0:T(8,128)(2,1)S(1)}, bf16[256,1024]{1,0:T(8,128)(2,1)S(1)}, u32[]{:S(2)}, u32[]{:S(2)}) collective-permute-start(bf16[256,1024]{1,0:T(8,128)(2,1)S(1)} %slice.9), channel_id=1, source_target_pairs={{0,1},{1,0},{2,3},{3,2},{4,5},{5,4},{6,7},{7,6},{8,9},{9,8},{10,11... | collective-permute-start | bytes 1572872 | tf_op jit(solution)/shard_map/ppermute | solution.py:269
  38.3 6.2 %collective-permute-start.10 = (bf16[256,1024]{1,0:T(8,128)(2,1)S(1)}, bf16[256,1024]{1,0:T(8,128)(2,1)S(1)}, u32[]{:S(2)}, u32[]{:S(2)}) collective-permute-start(bf16[256,1024]{1,0:T(8,128)(2,1)S(1)} %collective-permute-done.5.high_2a), channel_id=1, source_target_pairs={{0,1},{1,0},{2,3},{3,2},{4,5},{5,4},{6,7},{7,6},{8,9},{9,8},{10,11... | collective-permute-start | bytes 1572872 | tf_op jit(solution)/shard_map/ppermute | solution.py:269
  38.6 14.1 %collective-permute-start.6 = (bf16[256,1024]{1,0:T(8,128)(2,1)S(1)}, bf16[256,1024]{1,0:T(8,128)(2,1)S(1)}, u32[]{:S(2)}, u32[]{:S(2)}) collective-permute-start(bf16[256,1024]{1,0:T(8,128)(2,1)S(1)} %slice.9), channel_id=1, source_target_pairs={{0,2},{1,3},{2,0},{3,1},{4,6},{5,7},{6,4},{7,5},{8,10},{9,11},{10,... | collective-permute-start | bytes 1572872 | tf_op jit(solution)/shard_map/ppermute | solution.py:269
  52.6 2.0 %collective-permute-start.11 = (bf16[256,1024]{1,0:T(8,128)(2,1)S(1)}, bf16[256,1024]{1,0:T(8,128)(2,1)S(1)}, u32[]{:S(2)}, u32[]{:S(2)}) collective-permute-start(bf16[256,1024]{1,0:T(8,128)(2,1)S(1)} %collective-permute-done.6.high_2b), channel_id=1, source_target_pairs={{0,1},{1,0},{2,3},{3,2},{4,5},{5,4},{6,7},{7,6},{8,9},{9,8},{10,11... | collective-permute-start | bytes 1572872 | tf_op jit(solution)/shard_map/ppermute | solution.py:269
  56.3 3.8 %collective-permute-start.12 = (f32[1,2048]{1,0:T(1,128)S(1)}, f32[1,2048]{1,0:T(1,128)S(1)}, u32[]{:S(2)}, u32[]{:S(2)}) collective-permute-start(f32[1,2048]{1,0:T(1,128)S(1)} %last.1), channel_id=1, source_target_pairs={{0,8},{4,12},{8,16},{12,20},{16,24},{20,28},{1,9},{5,13},{9,17},{1... | collective-permute-start | bytes 24584 | tf_op jit(solution)/shard_map/ppermute | solution.py:263
  60.1 3.1 %collective-permute-start.15 = (f32[1,2048]{1,0:T(1,128)S(1)}, f32[1,2048]{1,0:T(1,128)S(1)}, u32[]{:S(2)}, u32[]{:S(2)}) collective-permute-start(f32[1,2048]{1,0:T(1,128)S(1)} %fusion), channel_id=1, source_target_pairs={{0,3},{1,2},{2,1},{3,0},{4,7},{5,6},{6,5},{7,4},{8,11},{9,10},{10,... | collective-permute-start | bytes 24584 | tf_op jit(solution)/shard_map/ppermute | solution.py:269
  61.0 3.7 %collective-permute-start.14 = (f32[1,2048]{1,0:T(1,128)S(1)}, f32[1,2048]{1,0:T(1,128)S(1)}, u32[]{:S(2)}, u32[]{:S(2)}) collective-permute-start(f32[1,2048]{1,0:T(1,128)S(1)} %fusion), channel_id=1, source_target_pairs={{0,2},{1,3},{2,0},{3,1},{4,6},{5,7},{6,4},{7,5},{8,10},{9,11},{10,... | collective-permute-start | bytes 24584 | tf_op jit(solution)/shard_map/ppermute | solution.py:269
  61.8 2.9 %collective-permute-start.13 = (f32[1,2048]{1,0:T(1,128)S(1)}, f32[1,2048]{1,0:T(1,128)S(1)}, u32[]{:S(2)}, u32[]{:S(2)}) collective-permute-start(f32[1,2048]{1,0:T(1,128)S(1)} %fusion), channel_id=1, source_target_pairs={{0,1},{1,0},{2,3},{3,2},{4,5},{5,4},{6,7},{7,6},{8,9},{9,8},{10,11... | collective-permute-start | bytes 24584 | tf_op jit(solution)/shard_map/ppermute | solution.py:269
